TPU v7x, 32 devices: a whole 2x2x4 slice. The times are simulated.
32 devices in a mesh: grp: 2 (over x), gx: 8 (over z, y), gy: 2 (over core).
Axes of the slice: x: 2, y: 2, z: 4, core: 2. Of those that a mesh axis runs over, the one named last changes fastest.
Arguments:
- fields: float32 [4, 4, 48, 512, 512], P('grp', None, None, 'gx', 'gy'), parts along dimension 0, may hold values from -2.5 to 2.5
- member_index: int32 [4], P('grp'), parts along dimension 0, may hold values from 0 to 7
- member_table: float32 [8, 4, 4], replicated, may hold values from 0.5 to 2
- seed_x: int32 [4, 16], P('grp'), parts along dimension 0, may hold values from 0 to 511
- seed_y: int32 [4, 16], P('grp'), parts along dimension 0, may hold values from 0 to 511
- seed_z: int32 [4, 16], P('grp'), parts along dimension 0, may hold values from 0 to 47
- start_basis: float32 [4, 512, 64], P('grp'), parts along dimension 0, may hold values from -6 to 6
Outputs:
- fields_next: float32 [4, 4, 48, 512, 512], P('grp', None, None, 'gx', 'gy'), parts along dimension 0
- basis: float32 [4, 512, 64], P('grp'), parts along dimension 0
- core: float32 [4, 64, 4, 4, 512], P('grp', 'gx', None, None, 'gy'), parts along dimension 0
There are 2 independent parts, one for each index of `grp`. A program takes and returns all parts, laid end to end along the dimension named above; an argument that names none is the same for every part. Nothing has to cross between parts.
All inputs are finite; a program needn't handle non-finite values.
Results may differ from a plain program's by a relative error of at most 0.0003.
Values sent between devices are 32-bit elements; how exact they have to be, the bound alone decides.
No kernel may reach another device: no remote copies, remote signals or barrier semaphores. Data moves between devices by JAX's collectives and lax.ppermute only.
A program may use at most 448 MiB of HBM per device.

v0:
```python
import jax
import jax.numpy as jnp
from jax import lax
from jax.sharding import PartitionSpec as P

ZS = 4
ITERS = 3


highest = lax.Precision.HIGHEST
time_step = 0.05
bump_width = 18.0
source_gain = 0.5


def with_halo(value, sides, width):
    for axis, dim in sides:
        size, length = (lax.axis_size(axis), value.shape[dim])
        up = [(i, (i + 1) % size) for i in range(size - 1)]
        down = [(j, i) for i, j in up]
        last = lax.slice_in_dim(value, length - width, length, axis=dim)
        initial = lax.slice_in_dim(value, 0, width, axis=dim)
        before = lax.ppermute(last, axis, up)
        after = lax.ppermute(initial, axis, down)
        value = jnp.concatenate([before, value, after], axis=dim)
    return value


def member_params(member_index, member_table):
    table_rows = member_table.shape[0]
    onehot = (member_index[:, None] == jnp.arange(table_rows, dtype=jnp.int32)[None, :]).astype(
        jnp.float32
    )
    return jnp.einsum("mp,pfk->mfk", onehot, member_table, precision=highest)


def seed_bumps(seed_x, seed_y, seed_z, x_start, y_start, rows_x, rows_y, planes):
    along_x = (x_start + jnp.arange(rows_x, dtype=jnp.int32)).astype(jnp.float32)
    along_y = (y_start + jnp.arange(rows_y, dtype=jnp.int32)).astype(jnp.float32)
    along_z = jnp.arange(planes, dtype=jnp.int32).astype(jnp.float32)
    bump_x = jnp.exp(
        -jnp.square(along_x[None, None, :] - seed_x[:, :, None].astype(jnp.float32)) / bump_width
    )
    bump_y = jnp.exp(
        -jnp.square(along_y[None, None, :] - seed_y[:, :, None].astype(jnp.float32)) / bump_width
    )
    bump_z = jnp.exp(
        -jnp.square(along_z[None, None, :] - seed_z[:, :, None].astype(jnp.float32)) / bump_width
    )
    plane_x = bump_z[:, :, :, None] * bump_x[:, :, None, :]
    return jnp.einsum("mszx,msy->mzxy", plane_x, bump_y, precision=highest)


def advance(fields, padded, params, source):
    lap_plane = (
        padded[..., 2:, 1:-1]
        + padded[..., :-2, 1:-1]
        + padded[..., 1:-1, 2:]
        + padded[..., 1:-1, :-2]
    )
    above = jnp.concatenate([fields[:, :, 1:], fields[:, :, -1:]], axis=2)
    below = jnp.concatenate([fields[:, :, :1], fields[:, :, :-1]], axis=2)
    laplace = lap_plane + above + below - 6.0 * fields
    kappa = params[:, :, 0][:, :, None, None, None]
    mobility = params[:, :, 1][:, :, None, None, None]
    gamma = params[:, :, 2][:, :, None, None, None]
    strength = params[:, :, 3][:, :, None, None, None]
    squares = jnp.sum(fields * fields, axis=1, keepdims=True)
    drive = fields * fields * fields - fields + gamma * fields * (squares - fields * fields)
    return (
        fields
        + time_step * mobility * (kappa * laplace - drive)
        + source_gain * strength * source[:, None]
    )


def orthonormal(image):
    cov = jnp.einsum("mxk,mxl->mkl", image, image, precision=highest)
    lower = jnp.linalg.cholesky(cov)
    return lax.linalg.triangular_solve(lower, image, left_side=False, lower=True, transpose_a=True)


def fibre_gram(fibre):
    gram = jnp.einsum("mfzxy,mfzwy->mxw", fibre, fibre, precision=highest)
    return (gram, fibre)


def per_device(fields, member_index, member_table, seed_x, seed_y, seed_z, start_basis):
    rows_x = fields.shape[3]
    rows_y = fields.shape[4]
    planes = fields.shape[2]
    x_start = lax.axis_index("gx") * rows_x
    y_start = lax.axis_index("gy") * rows_y
    padded = with_halo(fields, (("gx", 3), ("gy", 4)), 1)
    params = member_params(member_index, member_table)
    source = seed_bumps(seed_x, seed_y, seed_z, x_start, y_start, rows_x, rows_y, planes)
    fields_next = advance(fields, padded, params, source)
    slab = fields_next[:, :, :ZS]
    gram_part, fibre = fibre_gram(
        lax.all_to_all(slab, "gx", split_axis=4, concat_axis=3, tiled=True)
    )
    basis = start_basis
    gram = lax.psum(gram_part, ("gx", "gy"))
    for turn in range(ITERS):
        basis = orthonormal(jnp.einsum("mxw,mwk->mxk", gram, basis, precision=highest))
    core_fibre = jnp.einsum("mxr,mfzxy->mrfzy", basis, fibre, precision=highest)
    core = lax.all_to_all(core_fibre, "gx", split_axis=1, concat_axis=4, tiled=True)
    return (fields_next, basis, core)


def solution(mesh):
    placed = (
        P("grp", None, None, "gx", "gy"),
        P("grp"),
        P(),
        P("grp", None),
        P("grp", None),
        P("grp", None),
        P("grp", None, None),
    )
    return jax.shard_map(
        per_device,
        mesh=mesh,
        in_specs=placed,
        out_specs=(
            P("grp", None, None, "gx", "gy"),
            P("grp", None, None),
            P("grp", "gx", None, None, "gy"),
        ),
        check_vma=False,
    )
```

profile of v0, /device:TPU:0, one launch (start us, length us, event | category | flops | bytes accessed | tf_op | source)
XLA Modules:
  0.0 813.2 jit_solution(3383106381043264656)
XLA Ops:
  7.2 3.5 fusion.44
  10.8 1.3 collective-permute-start
  12.1 5.5 collective-permute-start.1
  17.6 45.2 %copy.181 = f32[2,4,48,64,256]{3,2,1,0,4:T(8,128)} copy(f32[2,4,48,64,256]{4,3,2,1,0:T(8,128)} %param.10) | data formatting | bytes 50331648 | tf_op args[0]
  62.8 65.1 %fusion.42 = (f32[2,4,47,64,256]{3,2,1,0,4:T(8,128)}, f32[2,4,47,64,256]{3,2,1,0,4:T(8,128)}) fusion(f32[2,4,48,64,256]{3,2,1,0,4:T(8,128)} %copy.181), kind=kLoop, calls=%fused_computation.81 | loop fusion | bytes 98566144 | tf_op jit(solution)/shard_map/slice | solution.py:62
  128.0 21.8 %multiply_reduce_fusion = f32[2,48,64,256]{2,1,0,3:T(8,128)} fusion(f32[2,4,48,64,256]{3,2,1,0,4:T(8,128)} %copy.181), kind=kLoop, calls=%fused_computation.2 | loop fusion | flops 11010048 | bytes 31457280 | tf_op jit(solution)/shard_map/reduce_sum | solution.py:68
  149.7 1.3 fusion.43
  151.1 0.2 fusion.36
  151.3 0.1 fusion.45
  151.6 0.1 copy.207
  151.7 0.1 copy.210
  151.9 7.7 fusion.15
  159.7 38.4 %copy.163 = f32[2,4,48,1,256]{3,2,1,0,4:T(8,128)} copy(f32[2,4,48,1,256]{4,2,3,1,0:T(8,128)S(1)} %collective-permute-done) | data formatting | bytes 786432 | tf_op jit(solution)/shard_map/ppermute | solution.py:24
  198.0 38.3 %copy.165 = f32[2,4,48,1,256]{3,2,1,0,4:T(8,128)} copy(f32[2,4,48,1,256]{4,2,3,1,0:T(8,128)S(1)} %collective-permute-done.1) | data formatting | bytes 786432 | tf_op jit(solution)/shard_map/ppermute | solution.py:23
  236.3 2.3 pad_maximum_fusion.10
  238.6 1.3 collective-permute-start.2
  239.9 3.3 collective-permute-start.3
  243.2 0.1 copy.160
  243.3 0.1 copy.179
  243.4 12.8 %copy.184 = f32[2,48,64,256]{2,1,0,3:T(8,128)} copy(f32[2,48,64,256]{3,2,1,0:T(8,128)} %fusion.15) | data formatting | bytes 12582912 | tf_op jit(solution)/shard_map/mszx,msy->mzxy/dot_general | solution.py:51
  256.1 0.8 copy.171
  256.9 0.8 copy.173
  257.7 220.6 %fusion.5 = f32[2,4,48,64,256]{3,2,1,0,4:T(8,128)} fusion(f32[2,4,48,64,256]{3,2,1,0,4:T(8,128)} %copy.181, f32[2,4,48,66,1]{3,2,1,0,4:T(8,128)S(1)} %collective-permute-done.3, f32[2,4,48,1,256]{3,2,1,0,4:T(8,128)} %copy.163, f32[2,4,48,1,256]{3,2,1,0,4:T(8,128)} %copy.165, f32[2,4,48,66,1]{3,2,1,0,4:T(8,128)S(1)} %collective-permute-done.2, ...), kind=kLoop, calls=%fused_computation.8 | loop fusion | flops 188743680 | bytes 114235520 | tf_op jit(solution)/shard_map/add | solution.py:71
  478.3 6.7 slice_bitcast_fusion
  485.0 6.8 reshape.86
  491.8 54.0 %all_to_all.36 = f32[8,1,65536]{2,1,0:T(1,128)} all-to-all(f32[8,1,65536]{2,1,0:T(1,128)S(1)} %reshape.86), channel_id=1, replica_groups=mesh['grp'=2,'gx'=8,'gy'=2] {'gx'}, dimensions={0} | all-to-all | bytes 4194304 | tf_op jit(solution)/shard_map/all_to_all | solution.py:100
  545.8 0.6 broadcast.112
  546.4 7.3 reduce.4
  553.7 4.9 reshape.87
  558.5 4.6 copy.185
  563.2 6.0 copy.186
  569.1 3.4 all_to_all.29
  572.6 4.8 convolution_bitcast_fusion
  577.5 96.8 %all-reduce.2.cloned.1.call-done = f32[2,512,512]{2,1,0:T(8,128)} async-done(((f32[2,512,512]{2,1,0:T(8,128)}), f32[2,512,512]{2,1,0:T(8,128)}) %all-reduce.2.cloned.1.call-update) | async-done | bytes 2097168 | tf_op jit(solution)/shard_map/psum | solution.py:103
  674.3 3.7 fusion.46
  678.0 0.4 fusion.47
  678.5 11.7 %custom-call.10 = f32[2,64,64]{2,1,0:T(8,128)S(1)} custom-call(f32[2,64,64]{2,1,0:T(8,128)S(1)} %fusion.26), custom_call_target="Cholesky" | custom-call | tf_op jit(solution)/shard_map/jit(cholesky)/cholesky | solution.py:79
  690.3 0.1 compare_reduce_fusion.2
  690.4 0.1 select_bitcast_fusion.2
  690.5 10.0 %custom-call.11 = f32[2,1,64,64]{2,3,1,0:T(8,128)S(1)} custom-call(f32[2,1,64,64]{3,2,1,0:T(8,128)S(1)} %select_bitcast_fusion.2), custom_call_target="InvertDiagBlocksLowerTriangular" | custom-call | tf_op jit(solution)/shard_map/triangular_solve/custom-call.0 | solution.py:80
  700.5 0.4 convolution_bitcast_fusion.2
  701.0 3.7 fusion.48
  704.7 0.4 fusion.49
  705.2 11.7 %custom-call.12 = f32[2,64,64]{2,1,0:T(8,128)S(1)} custom-call(f32[2,64,64]{2,1,0:T(8,128)S(1)} %fusion.24), custom_call_target="Cholesky" | custom-call | tf_op jit(solution)/shard_map/jit(cholesky)/cholesky | solution.py:79
  716.9 0.1 compare_reduce_fusion.1
  717.1 0.1 select_bitcast_fusion.1
  717.1 9.8 %custom-call.13 = f32[2,1,64,64]{2,3,1,0:T(8,128)S(1)} custom-call(f32[2,1,64,64]{3,2,1,0:T(8,128)S(1)} %select_bitcast_fusion.1), custom_call_target="InvertDiagBlocksLowerTriangular" | custom-call | tf_op jit(solution)/shard_map/triangular_solve/custom-call.0 | solution.py:80
  727.0 0.4 convolution_bitcast_fusion.1
  727.4 3.7 fusion.50
  731.1 0.4 fusion.51
  731.6 11.7 %custom-call.14 = f32[2,64,64]{2,1,0:T(8,128)S(1)} custom-call(f32[2,64,64]{2,1,0:T(8,128)S(1)} %fusion.22), custom_call_target="Cholesky" | custom-call | tf_op jit(solution)/shard_map/jit(cholesky)/cholesky | solution.py:79
  743.4 0.1 compare_reduce_fusion
  743.6 9.8 %custom-call.15 = f32[2,1,64,64]{2,3,1,0:T(8,128)S(1)} custom-call(f32[2,1,64,64]{3,2,1,0:T(8,128)S(1)} %select_bitcast_fusion), custom_call_target="InvertDiagBlocksLowerTriangular" | custom-call | tf_op jit(solution)/shard_map/triangular_solve/custom-call.0 | solution.py:80
  753.4 0.4 fusion.20
  753.9 1.8 fusion.13
  755.7 1.1 copy.194
  756.8 1.4 reshape.88
  758.2 4.2 all-to-all-start.1
  762.4 39.8 %copy.197 = f32[2,4,48,64,256]{4,3,2,1,0:T(8,128)} copy(f32[2,4,48,64,256]{3,2,1,0,4:T(8,128)} %fusion.5) | data formatting | bytes 50331648
  802.2 1.3 reduce.5
  803.5 0.5 reshape.89
  804.0 0.6 copy.214
  804.6 0.2 copy.205
  804.8 1.1 reshape.85
  (45 shorter events, 0.9 us)
Async XLA Ops:
  7.2 667.2 %copy-start = (f32[2,512,64]{1,2,0:T(8,128)S(1)}, f32[2,512,64]{1,2,0:T(8,128)}, u32[]{:S(2)}) copy-start(f32[2,512,64]{1,2,0:T(8,128)} %param.16) | copy-start | bytes 786436
  7.2 667.1 %all-reduce.2.cloned.1.call-start = ((), (), s32[]{:S(2)}) async-start(), calls=%async_computation.2 | async-start | bytes 4194304 | tf_op jit(solution)/shard_map/psum | solution.py:103
  10.8 148.9 %collective-permute-start = (f32[2,4,48,1,256]{4,2,3,1,0:T(8,128)S(1)}, f32[2,4,48,1,256]{4,2,3,1,0:T(8,128)S(1)}, u32[]{:S(2)}, u32[]{:S(2)}) collective-permute-start(f32[2,4,48,1,256]{4,2,3,1,0:T(8,128)S(1)} %copy.208), channel_id=1, source_target_pairs={{2,0},{4,2},{6,4},{8,6},{10,8},{12,10},{14,12},{3,1},{5,3},{7,5},{... | collective-permute-start | bytes 1179656 | tf_op jit(solution)/shard_map/ppermute | solution.py:24
  12.1 185.9 %collective-permute-start.1 = (f32[2,4,48,1,256]{4,2,3,1,0:T(8,128)S(1)}, f32[2,4,48,1,256]{4,2,3,1,0:T(8,128)S(1)}, u32[]{:S(2)}, u32[]{:S(2)}) collective-permute-start(f32[2,4,48,1,256]{4,2,3,1,0:T(8,128)S(1)} %copy.209), channel_id=1, source_target_pairs={{0,2},{2,4},{4,6},{6,8},{8,10},{10,12},{12,14},{1,3},{3,5},{5,7},{... | collective-permute-start | bytes 1179656 | tf_op jit(solution)/shard_map/ppermute | solution.py:23
  127.9 23.1 %copy-start.5 = (f32[8,4,4]{0,2,1:T(4,128)S(1)}, f32[8,4,4]{0,2,1:T(4,128)}, u32[]{:S(2)}) copy-start(f32[8,4,4]{0,2,1:T(4,128)} %param.12) | copy-start | bytes 1540
  127.9 23.1 %copy-start.6 = (s32[2]{0:T(128)S(1)}, s32[2]{0:T(128)}, u32[]{:S(2)}) copy-start(s32[2]{0:T(128)} %param.11) | copy-start | bytes 28
  127.9 23.5 %copy-start.2 = (s32[2,16]{1,0:T(2,128)S(1)}, s32[2,16]{1,0:T(2,128)}, u32[]{:S(2)}) copy-start(s32[2,16]{1,0:T(2,128)} %param.13) | copy-start | bytes 388
  127.9 23.5 %copy-start.3 = (s32[2,16]{1,0:T(2,128)S(1)}, s32[2,16]{1,0:T(2,128)}, u32[]{:S(2)}) copy-start(s32[2,16]{1,0:T(2,128)} %param.15) | copy-start | bytes 388
  127.9 24.0 %copy-start.4 = (s32[2,16]{1,0:T(2,128)S(1)}, s32[2,16]{1,0:T(2,128)}, u32[]{:S(2)}) copy-start(s32[2,16]{1,0:T(2,128)} %param.14) | copy-start | bytes 388
  238.6 19.1 %collective-permute-start.2 = (f32[2,4,48,66,1]{3,2,1,0,4:T(8,128)}, f32[2,4,48,66,1]{3,2,1,0,4:T(8,128)S(1)}, u32[]{:S(2)}, u32[]{:S(2)}) collective-permute-start(f32[2,4,48,66,1]{3,2,1,0,4:T(8,128)} %get-tuple-element.20), channel_id=1, source_target_pairs={{1,0},{3,2},{5,4},{7,6},{9,8},{11,10},{13,12},{15,14},{17,16},{19,... | collective-permute-start | bytes 304136 | tf_op jit(solution)/shard_map/ppermute | solution.py:24
  239.9 17.8 %collective-permute-start.3 = (f32[2,4,48,66,1]{3,2,1,0,4:T(8,128)S(1)}, f32[2,4,48,66,1]{3,2,1,0,4:T(8,128)S(1)}, u32[]{:S(2)}, u32[]{:S(2)}) collective-permute-start(f32[2,4,48,66,1]{3,2,1,0,4:T(8,128)S(1)} %get-tuple-element.21), channel_id=1, source_target_pairs={{0,1},{2,3},{4,5},{6,7},{8,9},{10,11},{12,13},{14,15},{16,17},{18,... | collective-permute-start | bytes 304136 | tf_op jit(solution)/shard_map/ppermute | solution.py:23
  753.9 52.1 %copy-start.1 = (f32[2,64,512]{2,1,0:T(8,128)}, f32[2,64,512]{2,1,0:T(8,128)S(1)}, u32[]{:S(2)}) copy-start(f32[2,64,512]{2,1,0:T(8,128)S(1)} %fusion.20) | copy-start | bytes 786436
  758.2 44.0 %all-to-all-start.1 = ((f32[8,1,8192]{2,1,0:T(1,128)}), f32[8,1,8192]{2,1,0:T(1,128)S(1)}, u32[]{:S(2)}, u32[]{:S(2)}) async-start(f32[8,1,8192]{2,1,0:T(1,128)} %reshape.88), calls=%async_computation.1 | async-start | bytes 524288 | tf_op jit(solution)/shard_map/all_to_all | solution.py:107
Sparse Core Ops, SparseCore 0:
  577.6 96.7 all-reduce.1
where the time goes:
time: 823 us; the launch traced here: 813 us
  other arithmetic  319 us (39%)
  local copies, waits for them, and re-layouts  285 us (35%)
  waiting for transfers between devices  96.9 us (12%)
  blocking collectives  54 us (7%)
  matrix products  28.2 us (3%)
  starting transfers between devices  15.6 us (2%)
  between operations  14.9 us (2%)
    add x1, other arithmetic, advance(): fields + time_step * mobility * (kappa * laplace - drive)  221 us
    unnamed x27, local copies, waits for them, and re-layouts  107 us
    psum x1, waiting for transfers between devices, per_device(): gram = lax.psum(gram_part, ('gx', 'gy'))  96.8 us
    slice x3, local copies, waits for them, and re-layouts, advance(): below = jnp.concatenate([fields[:, :, :1], fields[:, :, :-1]], axis=2)  67.1 us
    all_to_all x1, blocking collectives, per_device(): lax.all_to_all(slab, 'gx', split_axis=4, concat_axis=3, tiled=True)  54 us
    ppermute x1, local copies, waits for them, and re-layouts, with_halo(): after = lax.ppermute(initial, axis, down)  38.4 us
    ppermute x1, local copies, waits for them, and re-layouts, with_halo(): before = lax.ppermute(last, axis, up)  38.3 us
    another operation x10, other arithmetic, orthonormal(): lower = jnp.linalg.cholesky(cov)  35.6 us
  transfers between devices with their start and end apart: 6, of which 1 were waited for; matrix products, arithmetic and copies ran while one was open for 29% of the time, Pallas kernels for 0%

commit v1 on v0

v1 whole, which is shorter than its diff:
```python
import functools
import jax
import jax.numpy as jnp
from jax import lax
from jax.experimental import pallas as pl
from jax.experimental.pallas import tpu as pltpu
from jax.sharding import PartitionSpec as P

ZS = 4
ITERS = 3
ZB = 8

highest = lax.Precision.HIGHEST
time_step = 0.05
bump_width = 18.0
source_gain = 0.5
f32 = jnp.float32
bf16 = jnp.bfloat16
MIB = 1 << 20


def smem():
    return pl.BlockSpec(memory_space=pltpu.SMEM)


def vmem():
    return pl.BlockSpec(memory_space=pltpu.VMEM)


def params_of(limit):
    return pltpu.CompilerParams(vmem_limit_bytes=limit * MIB)


def split3(value):
    high = value.astype(bf16)
    rest = value - high.astype(f32)
    middle = rest.astype(bf16)
    low = (rest - middle.astype(f32)).astype(bf16)
    return high, middle, low


def edges_kernel(idx_ref, first_ref, last_ref, half_ref, top_ref, bottom_ref, side_ref):
    fb, planes, rows = half_ref.shape[1:4]
    lane = lax.broadcasted_iota(jnp.int32, (rows, 128), 1)
    offset = jnp.where(idx_ref[1] == 0, 1, 0)
    for f in range(fb):
        side = jnp.zeros((rows, 128), f32)
        for z in range(planes):
            top_ref[0, f, z : z + 1, :] = first_ref[0, f, z, 0:1, :]
            bottom_ref[0, f, z : z + 1, :] = last_ref[0, f, z, 7:8, :]
            turned = pltpu.roll(half_ref[0, f, z], z + offset, 1)
            side = jnp.where(lane == z, turned, side)
        side_ref[0, f] = side


def edges(idx, fields, planes, fb):
    m, f, _, rows, cols = fields.shape
    last = rows // 8 - 1
    tail = cols // 128 - 1
    edge_row = jax.ShapeDtypeStruct((m, f, planes, cols), f32)
    return pl.pallas_call(
        edges_kernel,
        grid_spec=pltpu.PrefetchScalarGridSpec(
            num_scalar_prefetch=1,
            grid=(m, f // fb),
            in_specs=[
                pl.BlockSpec((1, fb, planes, 8, cols), lambda i, j, s: (i, j, 0, 0, 0)),
                pl.BlockSpec((1, fb, planes, 8, cols), lambda i, j, s: (i, j, 0, last, 0)),
                pl.BlockSpec(
                    (1, fb, planes, rows, 128),
                    lambda i, j, s: (i, j, 0, 0, jnp.where(s[1] == 0, tail, 0)),
                ),
            ],
            out_specs=[
                pl.BlockSpec((1, fb, planes, cols), lambda i, j, s: (i, j, 0, 0)),
                pl.BlockSpec((1, fb, planes, cols), lambda i, j, s: (i, j, 0, 0)),
                pl.BlockSpec((1, fb, rows, 128), lambda i, j, s: (i, j, 0, 0)),
            ],
        ),
        out_shape=[edge_row, edge_row, jax.ShapeDtypeStruct((m, f, rows, 128), f32)],
        compiler_params=params_of(32),
        cost_estimate=pl.CostEstimate(
            flops=m * f * planes * rows * 256,
            bytes_accessed=m * f * planes * (rows * 128 + 16 * cols) * 4,
            transcendentals=0,
        ),
    )(idx, fields, fields, fields)


def step_block(idx_ref, coef_ref, refs, zb, z0, m, store):
    now, before, after, xu, xd, yh, sx, sy, sz = refs
    nf, rows, cols = now.shape[1], now.shape[3], now.shape[4]
    tiles = cols // 128
    wide = sx.shape[-1]
    seeds = wide // 6
    x_start = idx_ref[0] * rows
    y_start = idx_ref[1] * cols
    along_x = (x_start + lax.broadcasted_iota(jnp.int32, (rows, wide), 0)).astype(f32)
    bump_x = jnp.exp(-jnp.square(along_x - sx[0]) / bump_width)
    along_y = (y_start + lax.broadcasted_iota(jnp.int32, (wide, cols), 1)).astype(f32)
    high, middle, low = split3(jnp.exp(-jnp.square(along_y - sy[0]) / bump_width))
    part = lax.broadcasted_iota(jnp.int32, (wide, cols), 0) // seeds
    right = jnp.where(
        part == 3,
        low.astype(f32),
        jnp.where((part == 1) | (part == 5), middle.astype(f32), high.astype(f32)),
    ).astype(bf16)
    group = lax.broadcasted_iota(jnp.int32, (rows, wide), 1) // seeds
    use_low = group == 4
    use_middle = (group == 2) | (group == 5)
    lane = lax.broadcasted_iota(jnp.int32, (8, 128), 1)
    row = lax.broadcasted_iota(jnp.int32, (8, cols), 0)
    is_left = lane == 0
    is_right = lane == 127
    is_top = row == 0
    is_bottom = row == 7
    at_end = idx_ref[1] == 0
    gain_left = jnp.where(at_end, 0.0, 1.0).astype(f32)
    gain_right = jnp.where(at_end, 1.0, 0.0).astype(f32)
    coefs = [[coef_ref[m, f, k] for k in range(5)] for f in range(nf)]

    def plane(z, below_of, above_of):
        along_z = (z0 + z).astype(f32) if not isinstance(z0 + z, int) else f32(z0 + z)
        bump_z = jnp.exp(-jnp.square(along_z - sz[0]) / bump_width)
        high, middle, low = split3(bump_x * bump_z)
        left = jnp.where(
            use_low, low.astype(f32), jnp.where(use_middle, middle.astype(f32), high.astype(f32))
        ).astype(bf16)
        source = jnp.dot(left, right, preferred_element_type=f32)
        shift = jnp.where(at_end, 127 - (z0 + z), 128 - (z0 + z))
        shift = jnp.where(shift == 128, 0, shift)
        for r in range(0, rows, 8):
            cells = [now[0, f, z, r : r + 8, :] for f in range(nf)]
            squared = [c * c for c in cells]
            squares = squared[0]
            for f in range(1, nf):
                squares = squares + squared[f]
            src = source[r : r + 8, :]
            for f in range(nf):
                c = cells[f]
                a, c0, c1, c2, s = coefs[f]
                if r == 0:
                    over = xu[0, f, pl.ds(z0 + z, 1), :]
                else:
                    over = now[0, f, z, r - 1 : r, :]
                if r + 8 == rows:
                    under = xd[0, f, pl.ds(z0 + z, 1), :]
                else:
                    under = now[0, f, z, r + 8 : r + 9, :]
                up = jnp.where(is_top, over, pltpu.roll(c, 1, 0))
                down = jnp.where(is_bottom, under, pltpu.roll(c, 7, 0))
                halo = pltpu.roll(yh[0, f, r : r + 8, :], shift, 1)
                parts = [c[:, 128 * t : 128 * t + 128] for t in range(tiles)]
                fwd = [pltpu.roll(p, 1, 1) for p in parts]
                bwd = [pltpu.roll(p, 127, 1) for p in parts]
                side = []
                for t in range(tiles):
                    from_left = halo * gain_left if t == 0 else fwd[t - 1]
                    from_right = halo * gain_right if t == tiles - 1 else bwd[t + 1]
                    side.append(
                        jnp.where(is_left, from_left, fwd[t])
                        + jnp.where(is_right, from_right, bwd[t])
                    )
                near = (
                    jnp.concatenate(side, axis=1)
                    + (up + down)
                    + (below_of(f, r) + above_of(f, r))
                )
                value = a * near + c * (c0 - c1 * squared[f] - c2 * squares) + s * src
                store(f, z, r, value)

    def prior(z):
        return lambda f, r: now[0, f, z - 1, r : r + 8, :]

    def later(z):
        return lambda f, r: now[0, f, z + 1, r : r + 8, :]

    plane(0, lambda f, r: before[0, f, 0, r : r + 8, :], later(0))

    def body(z, carry):
        plane(z, prior(z), later(z))
        return carry

    lax.fori_loop(1, zb - 1, body, 0)
    plane(zb - 1, prior(zb - 1), lambda f, r: after[0, f, 0, r : r + 8, :])


def bulk_kernel(idx_ref, coef_ref, *refs):
    out = refs[-1]
    m, t = pl.program_id(0), pl.program_id(1)

    def store(f, z, r, value):
        out[0, f, z, r : r + 8, :] = value

    step_block(idx_ref, coef_ref, refs[:-1], ZB, t * ZB, m, store)


def step_specs(fields, planes, zb, halo_planes, wide):
    m, f, nz, rows, cols = fields.shape

    def at(shape, index):
        return pl.BlockSpec(shape, index)

    return [
        at((1, f, zb, rows, cols), lambda i, t, s: (i, 0, t, 0, 0)),
        at((1, f, 1, rows, cols), lambda i, t, s: (i, 0, jnp.maximum(t * zb - 1, 0), 0, 0)),
        at((1, f, 1, rows, cols), lambda i, t, s: (i, 0, jnp.minimum(t * zb + zb, nz - 1), 0, 0)),
        at((1, f, halo_planes, cols), lambda i, t, s: (i, 0, 0, 0)),
        at((1, f, halo_planes, cols), lambda i, t, s: (i, 0, 0, 0)),
        at((1, f, rows, 128), lambda i, t, s: (i, 0, 0, 0)),
        at((1, 1, wide), lambda i, t, s: (i, 0, 0)),
        at((1, wide, 1), lambda i, t, s: (i, 0, 0)),
        at((1, 1, wide), lambda i, t, s: (i, 0, 0)),
    ]


def bulk(idx, coefs, fields, halos, seeds):
    m, f, nz, rows, cols = fields.shape
    wide = seeds[0].shape[-1]
    specs = step_specs(fields, nz, ZB, nz, wide)
    return pl.pallas_call(
        bulk_kernel,
        grid_spec=pltpu.PrefetchScalarGridSpec(
            num_scalar_prefetch=1,
            grid=(m, nz // ZB),
            in_specs=[smem()] + specs,
            out_specs=pl.BlockSpec((1, f, ZB, rows, cols), lambda i, t, s: (i, 0, t, 0, 0)),
        ),
        out_shape=jax.ShapeDtypeStruct(fields.shape, f32),
        compiler_params=params_of(40),
        cost_estimate=pl.CostEstimate(
            flops=fields.size * 30, bytes_accessed=fields.size * 10, transcendentals=0
        ),
    )(idx, coefs, fields, fields, fields, *halos, *seeds)


def slab_kernel(n, ppd, yb, idx_ref, coef_ref, *refs):
    ins, outs, scratch = refs[:9], refs[9 : 9 + n], refs[9 + n]
    m = pl.program_id(0)
    me = idx_ref[0]
    ysp = ins[0].shape[4] // yb

    def store(f, z, r, value):
        p = f * ZS + z
        for h in range(ysp):
            scratch[p * ysp + h, r : r + 8, :] = value[:, h * yb : h * yb + yb]

    step_block(idx_ref, coef_ref, ins, ZS, 0, m, store)
    for k in range(n):
        dest = me ^ k
        for j in range(ppd):
            outs[k][0, j] = scratch[dest * ppd + j]


def slab_pieces(n, fields):
    _, f, _, _, cols = fields.shape
    count = f * ZS
    ysp = max(1, n // count)
    return max(1, count // n), cols // ysp, count * ysp


def slab_step(idx, coefs, fields, halos, seeds, n):
    m, f, nz, rows, cols = fields.shape
    wide = seeds[0].shape[-1]
    ppd, yb, pieces = slab_pieces(n, fields)
    piece = jax.ShapeDtypeStruct((m, ppd, rows, yb), f32)
    specs = step_specs(fields, ZS, ZS, ZS, wide)
    return pl.pallas_call(
        functools.partial(slab_kernel, n, ppd, yb),
        grid_spec=pltpu.PrefetchScalarGridSpec(
            num_scalar_prefetch=1,
            grid=(m, 1),
            in_specs=[smem()] + specs,
            out_specs=[pl.BlockSpec((1, ppd, rows, yb), lambda i, t, s: (i, 0, 0, 0))] * n,
            scratch_shapes=[pltpu.VMEM((pieces, rows, yb), f32)],
        ),
        out_shape=[piece] * n,
        compiler_params=params_of(32),
        cost_estimate=pl.CostEstimate(
            flops=m * f * ZS * rows * cols * 30,
            bytes_accessed=m * f * ZS * rows * cols * 10,
            transcendentals=0,
        ),
    )(idx, coefs, fields, fields, fields, *halos, *seeds)


def gram_kernel(n, idx_ref, *refs):
    ins, (own_ref, other_ref, fibre), folded = refs[:n], refs[n : n + 3], refs[n + 3]
    me, core = idx_ref[0], idx_ref[1]
    members, ppd, rows, yb = ins[0].shape
    half = n * rows // 2
    groups = half // (8 * n)
    for k in range(n):
        start = pl.multiple_of((me ^ k) * rows, rows)
        for m in range(members):
            for j in range(ppd):
                fibre[m, pl.ds(start, rows), j * yb : j * yb + yb] = ins[k][m, j]
    r = lax.broadcasted_iota(jnp.int32, (half, half), 0)
    c = lax.broadcasted_iota(jnp.int32, (half, half), 1)
    contract = (((1,), (1,)), ((), ()))
    for m in range(members):
        upper = fibre[m, :half, :]
        lower = fibre[m, half:, :]
        dot = functools.partial(
            lax.dot_general, dimension_numbers=contract, precision=highest, preferred_element_type=f32
        )
        cross = dot(upper, lower)
        first = dot(upper, upper)
        second = dot(lower, lower)
        packed = jnp.where(r <= c, first, second)
        diagonal = jnp.sum(jnp.where(r == c, second, 0.0), axis=0, keepdims=True)
        for d in range(n):
            for g in range(groups):
                at = (d * groups + g) * 8
                lo = g * 2 * half
                folded[m, d, :, lo : lo + half] = cross[at : at + 8, :]
                folded[m, d, :, lo + half : lo + 2 * half] = packed[at : at + 8, :]
            tile = (d * (half // 128)) // n
            folded[m, d, :, groups * 2 * half :] = jnp.broadcast_to(
                diagonal[:, tile * 128 : tile * 128 + 128], (8, 128)
            )
    own_ref[...] = folded[core]
    other_ref[...] = folded[1 - core]


def gram(idx, pieces):
    n = len(pieces)
    members, ppd, rows, yb = pieces[0].shape
    half = n * rows // 2
    wide = half // (8 * n) * 2 * half + 128
    chunk = jax.ShapeDtypeStruct((n, 8, wide), f32)
    fibre = jax.ShapeDtypeStruct((members, n * rows, ppd * yb), f32)
    return pl.pallas_call(
        functools.partial(gram_kernel, n),
        in_specs=[smem()] + [vmem()] * n,
        out_specs=[vmem()] * 3,
        out_shape=[chunk, chunk, fibre],
        scratch_shapes=[pltpu.VMEM((members, n, 8, wide), f32)],
        compiler_params=params_of(40),
    )(idx, *pieces)


def spread_kernel(n, idx_ref, own_ref, got_ref, *outs):
    for k in range(n):
        at = idx_ref[0] ^ k
        outs[k][...] = own_ref[at] + got_ref[at]


def spread(idx, own, got):
    n = own.shape[0]
    return pl.pallas_call(
        functools.partial(spread_kernel, n),
        in_specs=[smem(), vmem(), vmem()],
        out_specs=[vmem()] * n,
        out_shape=[jax.ShapeDtypeStruct(own.shape[1:], f32)] * n,
        compiler_params=params_of(16),
    )(idx, own, got)


def total_kernel(*refs):
    value = refs[0][...]
    for ref in refs[1:-1]:
        value = value + ref[...]
    refs[-1][...] = value


def total(pieces):
    return pl.pallas_call(
        total_kernel,
        in_specs=[vmem()] * len(pieces),
        out_specs=vmem(),
        out_shape=jax.ShapeDtypeStruct(pieces[0].shape, f32),
        compiler_params=params_of(16),
    )(*pieces)


def inverse_factor(cov):
    size = cov.shape[0]
    r = lax.broadcasted_iota(jnp.int32, (size, size), 0)
    c = lax.broadcasted_iota(jnp.int32, (size, size), 1)
    both = jnp.concatenate([cov, (r == c).astype(f32)], axis=1)
    groups = [both[g : g + 8, :] for g in range(0, size, 8)]
    sub = lax.broadcasted_iota(jnp.int32, (8, 2 * size), 0)
    for j in range(size):
        g, i = divmod(j, 8)
        pivot_row = groups[g][i : i + 1, :]
        scale = lax.rsqrt(pivot_row[:, j : j + 1])
        scaled = pivot_row * scale
        for h in range(g, size // 8):
            column = groups[h][:, j : j + 1] * scale
            update = groups[h] - column * scaled
            if h == g:
                update = jnp.where(sub > i, update, jnp.where(sub == i, scaled, groups[h]))
            groups[h] = update
    return jnp.concatenate([v[:, size:] for v in groups], axis=0)


def iterate_kernel(n, idx_ref, start_ref, *refs):
    ins, out_ref, folded, tails = refs[:n], refs[n], refs[n + 1], refs[n + 2]
    me, core = idx_ref[0], idx_ref[1]
    half = folded.shape[0]
    groups = half // (8 * n)
    for k in range(n):
        at = me ^ k
        for g in range(groups):
            place = pl.multiple_of(at * (8 * groups), 8) + 8 * g
            folded[pl.ds(place, 8), :] = ins[k][:, g * 2 * half : (g + 1) * 2 * half]
        tails[at] = ins[k][:, groups * 2 * half :]
    tiles = half // 128
    diagonal = jnp.concatenate([tails[t * n // tiles][0:1, :] for t in range(tiles)], axis=1)
    r = lax.broadcasted_iota(jnp.int32, (half, half), 0)
    c = lax.broadcasted_iota(jnp.int32, (half, half), 1)
    cross = folded[:, :half]
    packed = folded[:, half:]
    turned = packed.T
    first = jnp.where(r <= c, packed, turned)
    second = jnp.where(r > c, packed, jnp.where(r < c, turned, diagonal))
    dot = functools.partial(jnp.dot, precision=highest, preferred_element_type=f32)
    across = functools.partial(
        lax.dot_general,
        dimension_numbers=(((1,), (1,)), ((), ())),
        precision=highest,
        preferred_element_type=f32,
    )
    basis = start_ref[core]
    for _ in range(ITERS):
        a, b = basis[:, :half], basis[:, half:]
        image = jnp.concatenate([dot(a, first) + across(b, cross), dot(a, cross) + dot(b, second)], axis=1)
        basis = dot(inverse_factor(across(image, image)), image)
    out_ref[...] = basis


def iterate(idx, start, pieces):
    n = len(pieces)
    _, rank, size = start.shape
    half = size // 2
    return pl.pallas_call(
        functools.partial(iterate_kernel, n),
        in_specs=[smem()] + [vmem()] * (n + 1),
        out_specs=vmem(),
        out_shape=jax.ShapeDtypeStruct((rank, size), f32),
        scratch_shapes=[pltpu.VMEM((half, 2 * half), f32), pltpu.VMEM((n, 8, 128), f32)],
        compiler_params=params_of(40),
    )(idx, start, *pieces)


def project_kernel(n, idx_ref, own_ref, got_ref, fibre, basis_ref, *refs):
    outs, rows = refs[:n], refs[n]
    me, core = idx_ref[0], idx_ref[1]
    members = fibre.shape[0]
    share = outs[0].shape[1]
    basis_ref[core] = own_ref[...]
    basis_ref[1 - core] = got_ref[...]
    for m in range(members):
        value = jnp.dot(basis_ref[m], fibre[m], precision=highest, preferred_element_type=f32)
        for d in range(n):
            rows[d, m] = value[d * share : (d + 1) * share, :]
    for k in range(n):
        outs[k][...] = rows[me ^ k]


def project(idx, own, got, fibre, n):
    members, _, depth = fibre.shape
    rank, size = own.shape
    piece = (members, rank // n, depth)
    return pl.pallas_call(
        functools.partial(project_kernel, n),
        in_specs=[smem()] + [vmem()] * 3,
        out_specs=[vmem()] * (n + 1),
        out_shape=[jax.ShapeDtypeStruct((members, rank, size), f32)] + [jax.ShapeDtypeStruct(piece, f32)] * n,
        scratch_shapes=[pltpu.VMEM((n,) + piece, f32)],
        compiler_params=params_of(32),
    )(idx, own, got, fibre)


def gather_kernel(n, ppd, yb, idx_ref, *refs):
    ins, out, held = refs[:n], refs[n], refs[n + 1]
    members, share, nf, planes, cols = out.shape
    ysp = cols // yb
    for k in range(n):
        held[idx_ref[0] ^ k] = ins[k][...]
    for m in range(members):
        for s in range(share):
            for p in range(nf * planes):
                f, z = divmod(p, planes)
                for h in range(ysp):
                    piece = p * ysp + h
                    d, j = divmod(piece, ppd)
                    out[m, s, f, z : z + 1, h * yb : (h + 1) * yb] = held[
                        d, m, s : s + 1, j * yb : (j + 1) * yb
                    ]


def gather(idx, pieces, shape, ppd, yb):
    n = len(pieces)
    return pl.pallas_call(
        functools.partial(gather_kernel, n, ppd, yb),
        in_specs=[smem()] + [vmem()] * n,
        out_specs=vmem(),
        out_shape=jax.ShapeDtypeStruct(shape, f32),
        scratch_shapes=[pltpu.VMEM((n,) + pieces[0].shape, f32)],
        compiler_params=params_of(16),
    )(idx, *pieces)


def member_params(member_index, member_table):
    table_rows = member_table.shape[0]
    onehot = (member_index[:, None] == jnp.arange(table_rows, dtype=jnp.int32)[None, :]).astype(f32)
    return jnp.einsum("mp,pfk->mfk", onehot, member_table, precision=highest)


def exchange(pieces):
    n = lax.axis_size("gx")
    return [pieces[0]] + [
        lax.ppermute(pieces[k], "gx", [(i, i ^ k) for i in range(n)]) for k in range(1, n)
    ]


def swap_cores(value):
    return lax.ppermute(value, "gy", [(0, 1), (1, 0)])


def halos_of(idx, fields, planes, fb):
    n = lax.axis_size("gx")
    up = [(i, i + 1) for i in range(n - 1)]
    down = [(j, i) for i, j in up]
    top, bottom, side = edges(idx, fields, planes, fb)
    return (lax.ppermute(bottom, "gx", up), lax.ppermute(top, "gx", down), swap_cores(side))


def per_device(fields, member_index, member_table, seed_x, seed_y, seed_z, start_basis):
    n = lax.axis_size("gx")
    members, nf = fields.shape[:2]
    assert lax.axis_size("gy") == 2 and members == 2
    idx = jnp.stack([lax.axis_index("gx"), lax.axis_index("gy")]).astype(jnp.int32)
    params = member_params(member_index, member_table)
    kappa, mobility, gamma, strength = (params[:, :, k] for k in range(4))
    pace = time_step * mobility
    near = pace * kappa
    coefs = jnp.stack(
        [near, 1.0 - 6.0 * near + pace, pace * (1.0 - gamma), pace * gamma, source_gain * strength], axis=-1
    )
    seeds = (
        jnp.tile(seed_x.astype(f32), (1, 6))[:, None, :],
        jnp.tile(seed_y.astype(f32), (1, 6))[:, :, None],
        jnp.tile(seed_z.astype(f32), (1, 6))[:, None, :],
    )
    slab_halos = halos_of(idx, fields, ZS, nf)
    halos = halos_of(idx, fields, fields.shape[2], 1)
    slab = slab_step(idx, coefs, fields, slab_halos, seeds, n)
    pieces = exchange(slab)
    fields_next = bulk(idx, coefs, fields, halos, seeds)
    own, other, fibre = gram(idx, pieces)
    parts = exchange(spread(idx, own, swap_cores(other)))
    mine = total(parts)
    grams = exchange([mine] * n)
    start = jnp.swapaxes(start_basis, 1, 2)
    basis = iterate(idx, start, grams)
    bases, *rows = project(idx, basis, swap_cores(basis), fibre, n)
    ppd, yb, _ = slab_pieces(n, fields)
    share = start_basis.shape[2] // n
    core = gather(idx, exchange(rows), (members, share, nf, ZS, fields.shape[4]), ppd, yb)
    return (fields_next, jnp.swapaxes(bases, 1, 2), core)


def solution(mesh):
    placed = (
        P("grp", None, None, "gx", "gy"),
        P("grp"),
        P(),
        P("grp", None),
        P("grp", None),
        P("grp", None),
        P("grp", None, None),
    )
    return jax.shard_map(
        per_device,
        mesh=mesh,
        in_specs=placed,
        out_specs=(
            P("grp", None, None, "gx", "gy"),
            P("grp", None, None),
            P("grp", "gx", None, None, "gy"),
        ),
        check_vma=False,
    )
```

time: 823 us -> 198 us (0.24); the launches traced: 813 us -> 197 us
  other arithmetic: 319 us -> 0.11 us
  local copies, waits for them, and re-layouts: 285 us -> 0.49 us
  Pallas kernels: 0 us -> 76.3 us
  blocking collectives: 54 us -> 0 us
  starting transfers between devices: 15.6 us -> 69.3 us
  waiting for transfers between devices: 96.9 us -> 49.9 us
  matrix products: 28.2 us -> 0.23 us
  between operations: 14.9 us -> 0.96 us
    add x1 -> x0, other arithmetic: 221 us -> none  [advance(): fields + time_step * mobility * (kappa * laplace - drive)]
    unnamed x27 -> x12, local copies, waits for them, and re-layouts: 107 us -> 0.03 us
    psum x1 -> x0, waiting for transfers between devices: 96.8 us -> none  [per_device(): gram = lax.psum(gram_part, ('gx', 'gy'))]
    ppermute x2 -> x0, local copies, waits for them, and re-layouts: 76.6 us -> none  [the longest x1 38.4 us: with_halo(): after = lax.ppermute(initial, axis, down)]
    pallas_call x0 -> x10, Pallas kernels: none -> 76.3 us  [the longest x1 30.9 us: bulk(): pl.pallas_call(bulk_kernel, grid_spec=pltpu.PrefetchScalarGridSpec(num_sc...]
    slice x8 -> x1, local copies, waits for them, and re-layouts: 71.7 us -> 0.1 us  [per_device(): kappa, mobility, gamma, strength = (params[:, :, k] for k in range(4))]
    another operation x17 -> x1, other arithmetic: 65.6 us -> 0.08 us  [per_device(): jnp.stack([lax.axis_index('gx'), lax.axis_index('gy')]).astype(jnp.int32)]
    ppermute x4 -> x36, starting transfers between devices: 11.4 us -> 69.3 us  [the longest x28 58.1 us: exchange(): lax.ppermute(pieces[k], 'gx', [(i, i ^ k) for i in range(n)])]
  transfers between devices with their start and end apart: 6 -> 36, of which waited for: 1 -> 12; matrix products, arithmetic and copies ran while one was open for 29% -> 0% of each run, Pallas kernels for 0% -> 33%
where the time goes in v1:
time: 198 us; the launch traced here: 197 us
  Pallas kernels  76.3 us (39%)
  starting transfers between devices  69.3 us (35%)
  waiting for transfers between devices  49.9 us (25%)
    ppermute x28, starting transfers between devices, exchange(): lax.ppermute(pieces[k], 'gx', [(i, i ^ k) for i in range(n)])  58.1 us
    ppermute x28, waiting for transfers between devices, exchange(): lax.ppermute(pieces[k], 'gx', [(i, i ^ k) for i in range(n)])  43 us
    pallas_call x1, Pallas kernels, bulk(): pl.pallas_call(bulk_kernel, grid_spec=pltpu.PrefetchScalarGridSpec(num_sc...  30.9 us
    pallas_call x1, Pallas kernels, iterate(): pl.pallas_call(functools.partial(iterate_kernel, n), in_specs=[smem()] +...  20.7 us
    pallas_call x2, Pallas kernels, edges(): pl.pallas_call(edges_kernel, grid_spec=pltpu.PrefetchScalarGridSpec(num_s...  12.7 us
    ppermute x2, starting transfers between devices, halos_of(): lax.ppermute(bottom, 'gx', up)  8.21 us
    pallas_call x1, Pallas kernels, slab_step(): pl.pallas_call(functools.partial(slab_kernel, n, ppd, yb), grid_spec=pltp...  4.28 us
  transfers between devices with their start and end apart: 36, of which 12 were waited for; matrix products, arithmetic and copies ran while one was open for 0% of the time, Pallas kernels for 33%

profile of v1, /device:TPU:0, one launch (start us, length us, event | category | flops | bytes accessed | tf_op | source)
XLA Modules:
  0.0 197.3 jit_solution(3383867096632173945)
XLA Ops:
  0.6 0.0 copy-start
  0.6 0.1 pad_add_fusion.idx_ref
  0.7 2.3 %shard_map.96 = (f32[2,4,4,256]{3,2,1,0:T(4,128)S(1)}, f32[2,4,4,256]{3,2,1,0:T(4,128)S(1)}, f32[2,4,64,128]{3,2,1,0:T(8,128)S(1)}) custom-call(s32[2]{0:T(128)S(1)} %pad_add_fusion.idx_ref, f32[2,4,48,64,256]{4,3,2,1,0:T(8,128)} %refs_2_.3, f32[2,4,48,64,256]{4,3,2,1,0:T(8,128)} %refs_2_.3, f32[2,4,48,64,256]{4,3,2,1,0:T(8,128)} %refs_2_.3), custom_call_target="tpu_custom_call" | custom-call | flops 524288 | bytes 1572864 | tf_op jit(solution)/shard_map/pallas_call | solution.py:61
  3.0 4.9 %collective-permute-start.3 = (f32[2,4,4,256]{3,2,1,0:T(4,128)S(1)}, f32[2,4,4,256]{3,2,1,0:T(4,128)S(1)}, u32[]{:S(2)}, u32[]{:S(2)}) collective-permute-start(f32[2,4,4,256]{3,2,1,0:T(4,128)S(1)} %get-tuple-element.40), channel_id=1, source_target_pairs={{0,2},{2,4},{4,6},{6,8},{8,10},{10,12},{12,14},{1,3},{3,5},{5,7},{... | collective-permute-start | bytes 98312 | tf_op jit(solution)/shard_map/ppermute | solution.py:528
  7.9 1.3 collective-permute-start.4
  9.2 0.1 collective-permute-start.5
  9.3 0.2 fusion
  9.5 0.1 fusion.5
  9.7 0.1 tile.29
  9.8 0.1 tile.25
  9.9 0.1 tile.30.refs_7_
  10.0 0.1 stack.20.coef_ref
  10.1 0.0 collective-permute-done.3.refs_3_
  10.1 3.6 %collective-permute-done.4.refs_4_ = f32[2,4,4,256]{3,2,1,0:T(4,128)S(1)} collective-permute-done((f32[2,4,4,256]{3,2,1,0:T(4,128)S(1)}, f32[2,4,4,256]{3,2,1,0:T(4,128)S(1)}, u32[]{:S(2)}, u32[]{:S(2)}) %collective-permute-start.4) | collective-permute-done | bytes 32800 | tf_op jit(solution)/shard_map/ppermute | solution.py:528
  13.7 4.3 %shard_map.97 = (f32[2,2,64,256]{3,2,1,0:T(8,128)S(1)}, f32[2,2,64,256]{3,2,1,0:T(8,128)S(1)}, f32[2,2,64,256]{3,2,1,0:T(8,128)S(1)}, f32[2,2,64,256]{3,2,1,0:T(...) custom-call(s32[2]{0:T(128)S(1)} %pad_add_fusion.idx_ref, ...), custom_call_target="tpu_custom_call" | custom-call | flops 15728640 | bytes 5242880 | tf_op jit(solution)/shard_map/pallas_call | solution.py:268
  18.0 2.5 %collective-permute-start.6 = (f32[2,2,64,256]{3,2,1,0:T(8,128)S(1)}, f32[2,2,64,256]{3,2,1,0:T(8,128)S(1)}, u32[]{:S(2)}, u32[]{:S(2)}) collective-permute-start(f32[2,2,64,256]{3,2,1,0:T(8,128)S(1)} %get-tuple-element.44), channel_id=1, source_target_pairs={{0,2},{2,0},{4,6},{6,4},{8,10},{10,8},{12,14},{14,12},{1,3},{3,1},... | collective-permute-start | bytes 786440 | tf_op jit(solution)/shard_map/ppermute | solution.py:515
  20.5 1.6 collective-permute-start.7
  22.0 0.0 collective-permute-start.8
  22.0 2.6 %collective-permute-start.9 = (f32[2,2,64,256]{3,2,1,0:T(8,128)S(1)}, f32[2,2,64,256]{3,2,1,0:T(8,128)S(1)}, u32[]{:S(2)}, u32[]{:S(2)}) collective-permute-start(f32[2,2,64,256]{3,2,1,0:T(8,128)S(1)} %get-tuple-element.47), channel_id=1, source_target_pairs={{0,8},{2,10},{4,12},{6,14},{8,0},{10,2},{12,4},{14,6},{1,9},{3,11}... | collective-permute-start | bytes 786440 | tf_op jit(solution)/shard_map/ppermute | solution.py:515
  24.6 1.7 collective-permute-start.10
  26.3 0.0 collective-permute-done.6.refs_1_
  26.3 2.8 %collective-permute-start.11 = (f32[2,2,64,256]{3,2,1,0:T(8,128)S(1)}, f32[2,2,64,256]{3,2,1,0:T(8,128)S(1)}, u32[]{:S(2)}, u32[]{:S(2)}) collective-permute-start(f32[2,2,64,256]{3,2,1,0:T(8,128)S(1)} %get-tuple-element.49), channel_id=1, source_target_pairs={{0,12},{2,14},{4,8},{6,10},{8,4},{10,6},{12,0},{14,2},{1,13},{3,15... | collective-permute-start | bytes 786440 | tf_op jit(solution)/shard_map/ppermute | solution.py:515
  29.1 9.8 %collective-permute-done.7.refs_2_ = f32[2,2,64,256]{3,2,1,0:T(8,128)S(1)} collective-permute-done((f32[2,2,64,256]{3,2,1,0:T(8,128)S(1)}, f32[2,2,64,256]{3,2,1,0:T(8,128)S(1)}, u32[]{:S(2)}, u32[]{:S(2)}) %collective-permute-start.7) | collective-permute-done | bytes 262176 | tf_op jit(solution)/shard_map/ppermute | solution.py:515
  38.9 2.0 collective-permute-start.12
  40.9 0.2 collective-permute-done.8.refs_3_
  41.1 20.5 %collective-permute-done.10.refs_5_ = f32[2,2,64,256]{3,2,1,0:T(8,128)S(1)} collective-permute-done((f32[2,2,64,256]{3,2,1,0:T(8,128)S(1)}, f32[2,2,64,256]{3,2,1,0:T(8,128)S(1)}, u32[]{:S(2)}, u32[]{:S(2)}) %collective-permute-start.10) | collective-permute-done | bytes 262176 | tf_op jit(solution)/shard_map/ppermute | solution.py:515
  61.6 3.6 %shard_map.98 = (f32[8,8,2176]{2,1,0:T(8,128)S(1)}, f32[8,8,2176]{2,1,0:T(8,128)S(1)}, f32[2,512,512]{2,1,0:T(8,128)S(1)}) custom-call(s32[2]{0:T(128)S(1)} %pad_add_fusion.idx_ref, f32[2,2,64,256]{3,2,1,0:T(8,128)S(1)} %get-tuple-element.43.refs_0_, f32[2,2,64,256]{3,2,1,0:T(8,128)S(1)} %collective-permute-done.6.refs_1_, ...), custom_call_target="tpu_custom_call" | custom-call | tf_op jit(solution)/shard_map/pallas_call | solution.py:333
  65.2 0.1 collective-permute-start.13
  65.3 1.9 collective-permute-done.13.got_ref
  67.2 0.6 shard_map.99
  67.8 0.1 collective-permute-start.14
  67.9 9.0 %collective-permute-start.15 = (f32[8,2176]{1,0:T(8,128)S(1)}, f32[8,2176]{1,0:T(8,128)S(1)}, u32[]{:S(2)}, u32[]{:S(2)}) collective-permute-start(f32[8,2176]{1,0:T(8,128)S(1)} %get-tuple-element.55), channel_id=1, source_target_pairs={{0,4},{2,6},{4,0},{6,2},{8,12},{10,14},{12,8},{14,10},{1,5},{3,7},... | collective-permute-start | bytes 208904 | tf_op jit(solution)/shard_map/ppermute | solution.py:515
  76.9 0.8 collective-permute-start.16
  77.7 3.2 %collective-permute-start.17 = (f32[8,2176]{1,0:T(8,128)S(1)}, f32[8,2176]{1,0:T(8,128)S(1)}, u32[]{:S(2)}, u32[]{:S(2)}) collective-permute-start(f32[8,2176]{1,0:T(8,128)S(1)} %get-tuple-element.57), channel_id=1, source_target_pairs={{0,8},{2,10},{4,12},{6,14},{8,0},{10,2},{12,4},{14,6},{1,9},{3,11}... | collective-permute-start | bytes 208904 | tf_op jit(solution)/shard_map/ppermute | solution.py:515
  80.9 0.8 collective-permute-start.18
  81.8 2.4 %collective-permute-start.19 = (f32[8,2176]{1,0:T(8,128)S(1)}, f32[8,2176]{1,0:T(8,128)S(1)}, u32[]{:S(2)}, u32[]{:S(2)}) collective-permute-start(f32[8,2176]{1,0:T(8,128)S(1)} %get-tuple-element.59), channel_id=1, source_target_pairs={{0,12},{2,14},{4,8},{6,10},{8,4},{10,6},{12,0},{14,2},{1,13},{3,15... | collective-permute-start | bytes 208904 | tf_op jit(solution)/shard_map/ppermute | solution.py:515
  84.1 1.5 collective-permute-start.20
  85.7 10.4 %shard_map.94 = (f32[2,4,48,256]{3,2,1,0:T(8,128)S(1)}, f32[2,4,48,256]{3,2,1,0:T(8,128)S(1)}, f32[2,4,64,128]{3,2,1,0:T(8,128)S(1)}) custom-call(s32[2]{0:T(128)S(1)} %pad_add_fusion.idx_ref, f32[2,4,48,64,256]{4,3,2,1,0:T(8,128)} %refs_2_.3, f32[2,4,48,64,256]{4,3,2,1,0:T(8,128)} %refs_2_.3, f32[2,4,48,64,256]{4,3,2,1,0:T(8,128)} %refs_2_.3), custom_call_target="tpu_custom_call" | custom-call | flops 6291456 | bytes 18874368 | tf_op jit(solution)/shard_map/pallas_call | solution.py:61
  96.1 3.3 %collective-permute-start = (f32[2,4,48,256]{3,2,1,0:T(8,128)S(1)}, f32[2,4,48,256]{3,2,1,0:T(8,128)S(1)}, u32[]{:S(2)}, u32[]{:S(2)}) collective-permute-start(f32[2,4,48,256]{3,2,1,0:T(8,128)S(1)} %get-tuple-element.37), channel_id=1, source_target_pairs={{0,2},{2,4},{4,6},{6,8},{8,10},{10,12},{12,14},{1,3},{3,5},{5,7},{... | collective-permute-start | bytes 1179656 | tf_op jit(solution)/shard_map/ppermute | solution.py:528
  99.4 1.5 collective-permute-start.1
  101.0 4.5 %collective-permute-start.27 = (f32[8,2176]{1,0:T(8,128)S(1)}, f32[8,2176]{1,0:T(8,128)S(1)}, u32[]{:S(2)}, u32[]{:S(2)}) collective-permute-start(f32[8,2176]{1,0:T(8,128)S(1)} %shard_map.100.refs_0_), channel_id=1, source_target_pairs={{0,14},{2,12},{4,10},{6,8},{8,6},{10,4},{12,2},{14,0},{1,15},{3,13... | collective-permute-start | bytes 208904 | tf_op jit(solution)/shard_map/ppermute | solution.py:515
  105.5 1.5 collective-permute-start.26
  107.0 0.3 collective-permute-start.25
  107.2 1.0 collective-permute-done.27.refs_7_
  108.2 9.3 %collective-permute-start.24 = (f32[8,2176]{1,0:T(8,128)S(1)}, f32[8,2176]{1,0:T(8,128)S(1)}, u32[]{:S(2)}, u32[]{:S(2)}) collective-permute-start(f32[8,2176]{1,0:T(8,128)S(1)} %shard_map.100.refs_0_), channel_id=1, source_target_pairs={{0,8},{2,10},{4,12},{6,14},{8,0},{10,2},{12,4},{14,6},{1,9},{3,11}... | collective-permute-start | bytes 208904 | tf_op jit(solution)/shard_map/ppermute | solution.py:515
  117.5 1.7 collective-permute-done.26.refs_6_
  119.2 3.6 %collective-permute-done.24.refs_4_ = f32[8,2176]{1,0:T(8,128)S(1)} collective-permute-done((f32[8,2176]{1,0:T(8,128)S(1)}, f32[8,2176]{1,0:T(8,128)S(1)}, u32[]{:S(2)}, u32[]{:S(2)}) %collective-permute-start.24) | collective-permute-done | bytes 69664 | tf_op jit(solution)/shard_map/ppermute | solution.py:515
  122.8 2.4 %collective-permute-done.23.refs_3_ = f32[8,2176]{1,0:T(8,128)S(1)} collective-permute-done((f32[8,2176]{1,0:T(8,128)S(1)}, f32[8,2176]{1,0:T(8,128)S(1)}, u32[]{:S(2)}, u32[]{:S(2)}) %collective-permute-start.23) | collective-permute-done | bytes 69664 | tf_op jit(solution)/shard_map/ppermute | solution.py:515
  125.2 0.6 collective-permute-start.21
  125.8 1.4 collective-permute-done.22.refs_2_
  127.1 2.4 %collective-permute-done.21.refs_1_ = f32[8,2176]{1,0:T(8,128)S(1)} collective-permute-done((f32[8,2176]{1,0:T(8,128)S(1)}, f32[8,2176]{1,0:T(8,128)S(1)}, u32[]{:S(2)}, u32[]{:S(2)}) %collective-permute-start.21) | collective-permute-done | bytes 69664 | tf_op jit(solution)/shard_map/ppermute | solution.py:515
  129.5 20.7 %shard_map.101.own_ref = f32[64,512]{1,0:T(8,128)S(1)} custom-call(s32[2]{0:T(128)S(1)} %pad_add_fusion.idx_ref, f32[2,64,512]{2,1,0:T(8,128)S(1)} %bitcast.12, f32[8,2176]{1,0:T(8,128)S(1)} %shard_map.100.refs_0_, f32[8,2176]{1,0:T(8,128)S(1)} %collective-permute-done.21.refs_1_, f32[8,2176]{1,0:T(8,128)S(1)} %collective-permute-done.22.refs_2_, ...), custom_call_target="tpu_custom_call" | custom-call | tf_op jit(solution)/shard_map/pallas_call | solution.py:437
  150.2 0.1 collective-permute-start.28
  150.3 1.3 collective-permute-done.28.got_ref
  151.6 2.1 %shard_map.102 = (f32[2,64,512]{2,1,0:T(8,128)}, f32[2,8,512]{2,1,0:T(8,128)S(1)}, f32[2,8,512]{2,1,0:T(8,128)S(1)}, f32[2,8,512]{2,1,0:T(8,128)S(1)}, f32[2,8,5...) custom-call(s32[2]{0:T(128)S(1)} %pad_add_fusion.idx_ref, ...), custom_call_target="tpu_custom_call" | custom-call | tf_op jit(solution)/shard_map/pallas_call | solution.py:466
  153.7 0.6 collective-permute-start.29
  154.3 1.4 collective-permute-start.30
  155.8 1.5 collective-permute-start.31
  157.2 1.5 collective-permute-start.32
  158.7 1.5 collective-permute-start.33
  160.2 2.3 %collective-permute-start.34 = (f32[2,8,512]{2,1,0:T(8,128)S(1)}, f32[2,8,512]{2,1,0:T(8,128)S(1)}, u32[]{:S(2)}, u32[]{:S(2)}) collective-permute-start(f32[2,8,512]{2,1,0:T(8,128)S(1)} %get-tuple-element.69), channel_id=1, source_target_pairs={{0,12},{2,14},{4,8},{6,10},{8,4},{10,6},{12,0},{14,2},{1,13},{3,15... | collective-permute-start | bytes 98312 | tf_op jit(solution)/shard_map/ppermute | solution.py:515
  162.5 2.3 %collective-permute-start.35 = (f32[2,8,512]{2,1,0:T(8,128)S(1)}, f32[2,8,512]{2,1,0:T(8,128)S(1)}, u32[]{:S(2)}, u32[]{:S(2)}) collective-permute-start(f32[2,8,512]{2,1,0:T(8,128)S(1)} %get-tuple-element.70), channel_id=1, source_target_pairs={{0,14},{2,12},{4,10},{6,8},{8,6},{10,4},{12,2},{14,0},{1,15},{3,13... | collective-permute-start | bytes 98312 | tf_op jit(solution)/shard_map/ppermute | solution.py:515
  164.9 30.9 %shard_map.95 = f32[2,4,48,64,256]{4,3,2,1,0:T(8,128)} custom-call(s32[2]{0:T(128)S(1)} %pad_add_fusion.idx_ref, f32[2,4,5]{2,1,0:T(4,128)S(1)} %stack.20.coef_ref, f32[2,4,48,64,256]{4,3,2,1,0:T(8,128)} %refs_2_.3, f32[2,4,48,64,256]{4,3,2,1,0:T(8,128)} %refs_2_.3, f32[2,4,48,64,256]{4,3,2,1,0:T(8,128)} %refs_2_.3, ...), custom_call_target="tpu_custom_call" | custom-call | flops 188743680 | bytes 62914560 | tf_op jit(solution)/shard_map/pallas_call | solution.py:221
  195.9 1.4 shard_map.103
  (45 shorter events, 0.2 us)
Async XLA Ops:
  0.6 8.6 %copy-start = (f32[8,4,4]{0,2,1:T(4,128)S(1)}, f32[8,4,4]{0,2,1:T(4,128)}, u32[]{:S(2)}) copy-start(f32[8,4,4]{0,2,1:T(4,128)} %param.9) | copy-start | bytes 1540
  0.7 8.5 %copy-start.5 = (s32[2]{0:T(128)S(1)}, s32[2]{0:T(128)}, u32[]{:S(2)}) copy-start(s32[2]{0:T(128)} %param.8) | copy-start | bytes 28
  0.7 8.9 %copy-start.2 = (s32[2,16]{1,0:T(2,128)S(1)}, s32[2,16]{1,0:T(2,128)}, u32[]{:S(2)}) copy-start(s32[2,16]{1,0:T(2,128)} %param.10) | copy-start | bytes 388
  0.7 8.9 %copy-start.3 = (s32[2,16]{1,0:T(2,128)S(1)}, s32[2,16]{1,0:T(2,128)}, u32[]{:S(2)}) copy-start(s32[2,16]{1,0:T(2,128)} %param.11) | copy-start | bytes 388
  0.7 9.0 %copy-start.4 = (s32[2,16]{1,0:T(2,128)S(1)}, s32[2,16]{1,0:T(2,128)}, u32[]{:S(2)}) copy-start(s32[2,16]{1,0:T(2,128)} %param.12) | copy-start | bytes 388
  3.0 7.1 %collective-permute-start.3 = (f32[2,4,4,256]{3,2,1,0:T(4,128)S(1)}, f32[2,4,4,256]{3,2,1,0:T(4,128)S(1)}, u32[]{:S(2)}, u32[]{:S(2)}) collective-permute-start(f32[2,4,4,256]{3,2,1,0:T(4,128)S(1)} %get-tuple-element.40), channel_id=1, source_target_pairs={{0,2},{2,4},{4,6},{6,8},{8,10},{10,12},{12,14},{1,3},{3,5},{5,7},{... | collective-permute-start | bytes 98312 | tf_op jit(solution)/shard_map/ppermute | solution.py:528
  7.9 5.8 %collective-permute-start.4 = (f32[2,4,4,256]{3,2,1,0:T(4,128)S(1)}, f32[2,4,4,256]{3,2,1,0:T(4,128)S(1)}, u32[]{:S(2)}, u32[]{:S(2)}) collective-permute-start(f32[2,4,4,256]{3,2,1,0:T(4,128)S(1)} %get-tuple-element.41), channel_id=1, source_target_pairs={{2,0},{4,2},{6,4},{8,6},{10,8},{12,10},{14,12},{3,1},{5,3},{7,5},{... | collective-permute-start | bytes 98312 | tf_op jit(solution)/shard_map/ppermute | solution.py:528
  9.2 4.5 %collective-permute-start.5 = (f32[2,4,64,128]{3,2,1,0:T(8,128)S(1)}, f32[2,4,64,128]{3,2,1,0:T(8,128)S(1)}, u32[]{:S(2)}, u32[]{:S(2)}) collective-permute-start(f32[2,4,64,128]{3,2,1,0:T(8,128)S(1)} %get-tuple-element.42), channel_id=1, source_target_pairs={{0,1},{1,0},{2,3},{3,2},{4,5},{5,4},{6,7},{7,6},{8,9},{9,8},{10,11... | collective-permute-start | bytes 786440 | tf_op jit(solution)/shard_map/ppermute | solution.py:520
  18.0 8.3 %collective-permute-start.6 = (f32[2,2,64,256]{3,2,1,0:T(8,128)S(1)}, f32[2,2,64,256]{3,2,1,0:T(8,128)S(1)}, u32[]{:S(2)}, u32[]{:S(2)}) collective-permute-start(f32[2,2,64,256]{3,2,1,0:T(8,128)S(1)} %get-tuple-element.44), channel_id=1, source_target_pairs={{0,2},{2,0},{4,6},{6,4},{8,10},{10,8},{12,14},{14,12},{1,3},{3,1},... | collective-permute-start | bytes 786440 | tf_op jit(solution)/shard_map/ppermute | solution.py:515
  20.5 18.5 %collective-permute-start.7 = (f32[2,2,64,256]{3,2,1,0:T(8,128)S(1)}, f32[2,2,64,256]{3,2,1,0:T(8,128)S(1)}, u32[]{:S(2)}, u32[]{:S(2)}) collective-permute-start(f32[2,2,64,256]{3,2,1,0:T(8,128)S(1)} %get-tuple-element.45), channel_id=1, source_target_pairs={{0,4},{2,6},{4,0},{6,2},{8,12},{10,14},{12,8},{14,10},{1,5},{3,7},... | collective-permute-start | bytes 786440 | tf_op jit(solution)/shard_map/ppermute | solution.py:515
  22.0 19.0 %collective-permute-start.8 = (f32[2,2,64,256]{3,2,1,0:T(8,128)S(1)}, f32[2,2,64,256]{3,2,1,0:T(8,128)S(1)}, u32[]{:S(2)}, u32[]{:S(2)}) collective-permute-start(f32[2,2,64,256]{3,2,1,0:T(8,128)S(1)} %get-tuple-element.46), channel_id=1, source_target_pairs={{0,6},{2,4},{4,2},{6,0},{8,14},{10,12},{12,10},{14,8},{1,7},{3,5},... | collective-permute-start | bytes 786440 | tf_op jit(solution)/shard_map/ppermute | solution.py:515
  22.0 19.0 %collective-permute-start.9 = (f32[2,2,64,256]{3,2,1,0:T(8,128)S(1)}, f32[2,2,64,256]{3,2,1,0:T(8,128)S(1)}, u32[]{:S(2)}, u32[]{:S(2)}) collective-permute-start(f32[2,2,64,256]{3,2,1,0:T(8,128)S(1)} %get-tuple-element.47), channel_id=1, source_target_pairs={{0,8},{2,10},{4,12},{6,14},{8,0},{10,2},{12,4},{14,6},{1,9},{3,11}... | collective-permute-start | bytes 786440 | tf_op jit(solution)/shard_map/ppermute | solution.py:515
  24.6 37.0 %collective-permute-start.10 = (f32[2,2,64,256]{3,2,1,0:T(8,128)S(1)}, f32[2,2,64,256]{3,2,1,0:T(8,128)S(1)}, u32[]{:S(2)}, u32[]{:S(2)}) collective-permute-start(f32[2,2,64,256]{3,2,1,0:T(8,128)S(1)} %get-tuple-element.48), channel_id=1, source_target_pairs={{0,10},{2,8},{4,14},{6,12},{8,2},{10,0},{12,6},{14,4},{1,11},{3,9}... | collective-permute-start | bytes 786440 | tf_op jit(solution)/shard_map/ppermute | solution.py:515
  26.3 35.3 %collective-permute-start.11 = (f32[2,2,64,256]{3,2,1,0:T(8,128)S(1)}, f32[2,2,64,256]{3,2,1,0:T(8,128)S(1)}, u32[]{:S(2)}, u32[]{:S(2)}) collective-permute-start(f32[2,2,64,256]{3,2,1,0:T(8,128)S(1)} %get-tuple-element.49), channel_id=1, source_target_pairs={{0,12},{2,14},{4,8},{6,10},{8,4},{10,6},{12,0},{14,2},{1,13},{3,15... | collective-permute-start | bytes 786440 | tf_op jit(solution)/shard_map/ppermute | solution.py:515
  38.9 22.7 %collective-permute-start.12 = (f32[2,2,64,256]{3,2,1,0:T(8,128)S(1)}, f32[2,2,64,256]{3,2,1,0:T(8,128)S(1)}, u32[]{:S(2)}, u32[]{:S(2)}) collective-permute-start(f32[2,2,64,256]{3,2,1,0:T(8,128)S(1)} %get-tuple-element.50), channel_id=1, source_target_pairs={{0,14},{2,12},{4,10},{6,8},{8,6},{10,4},{12,2},{14,0},{1,15},{3,13... | collective-permute-start | bytes 786440 | tf_op jit(solution)/shard_map/ppermute | solution.py:515
  65.2 2.0 %collective-permute-start.13 = (f32[8,8,2176]{2,1,0:T(8,128)S(1)}, f32[8,8,2176]{2,1,0:T(8,128)S(1)}, u32[]{:S(2)}, u32[]{:S(2)}) collective-permute-start(f32[8,8,2176]{2,1,0:T(8,128)S(1)} %get-tuple-element.52), channel_id=1, source_target_pairs={{0,1},{1,0},{2,3},{3,2},{4,5},{5,4},{6,7},{7,6},{8,9},{9,8},{10,11... | collective-permute-start | bytes 1671176 | tf_op jit(solution)/shard_map/ppermute | solution.py:520
  67.8 14.0 %collective-permute-start.14 = (f32[8,2176]{1,0:T(8,128)S(1)}, f32[8,2176]{1,0:T(8,128)S(1)}, u32[]{:S(2)}, u32[]{:S(2)}) collective-permute-start(f32[8,2176]{1,0:T(8,128)S(1)} %get-tuple-element.54), channel_id=1, source_target_pairs={{0,2},{2,0},{4,6},{6,4},{8,10},{10,8},{12,14},{14,12},{1,3},{3,1},... | collective-permute-start | bytes 208904 | tf_op jit(solution)/shard_map/ppermute | solution.py:515
  67.9 16.2 %collective-permute-start.15 = (f32[8,2176]{1,0:T(8,128)S(1)}, f32[8,2176]{1,0:T(8,128)S(1)}, u32[]{:S(2)}, u32[]{:S(2)}) collective-permute-start(f32[8,2176]{1,0:T(8,128)S(1)} %get-tuple-element.55), channel_id=1, source_target_pairs={{0,4},{2,6},{4,0},{6,2},{8,12},{10,14},{12,8},{14,10},{1,5},{3,7},... | collective-permute-start | bytes 208904 | tf_op jit(solution)/shard_map/ppermute | solution.py:515
  76.9 19.2 %collective-permute-start.16 = (f32[8,2176]{1,0:T(8,128)S(1)}, f32[8,2176]{1,0:T(8,128)S(1)}, u32[]{:S(2)}, u32[]{:S(2)}) collective-permute-start(f32[8,2176]{1,0:T(8,128)S(1)} %get-tuple-element.56), channel_id=1, source_target_pairs={{0,6},{2,4},{4,2},{6,0},{8,14},{10,12},{12,10},{14,8},{1,7},{3,5},... | collective-permute-start | bytes 208904 | tf_op jit(solution)/shard_map/ppermute | solution.py:515
  77.7 21.7 %collective-permute-start.17 = (f32[8,2176]{1,0:T(8,128)S(1)}, f32[8,2176]{1,0:T(8,128)S(1)}, u32[]{:S(2)}, u32[]{:S(2)}) collective-permute-start(f32[8,2176]{1,0:T(8,128)S(1)} %get-tuple-element.57), channel_id=1, source_target_pairs={{0,8},{2,10},{4,12},{6,14},{8,0},{10,2},{12,4},{14,6},{1,9},{3,11}... | collective-permute-start | bytes 208904 | tf_op jit(solution)/shard_map/ppermute | solution.py:515
  80.9 20.0 %collective-permute-start.18 = (f32[8,2176]{1,0:T(8,128)S(1)}, f32[8,2176]{1,0:T(8,128)S(1)}, u32[]{:S(2)}, u32[]{:S(2)}) collective-permute-start(f32[8,2176]{1,0:T(8,128)S(1)} %get-tuple-element.58), channel_id=1, source_target_pairs={{0,10},{2,8},{4,14},{6,12},{8,2},{10,0},{12,6},{14,4},{1,11},{3,9}... | collective-permute-start | bytes 208904 | tf_op jit(solution)/shard_map/ppermute | solution.py:515
  81.8 19.2 %collective-permute-start.19 = (f32[8,2176]{1,0:T(8,128)S(1)}, f32[8,2176]{1,0:T(8,128)S(1)}, u32[]{:S(2)}, u32[]{:S(2)}) collective-permute-start(f32[8,2176]{1,0:T(8,128)S(1)} %get-tuple-element.59), channel_id=1, source_target_pairs={{0,12},{2,14},{4,8},{6,10},{8,4},{10,6},{12,0},{14,2},{1,13},{3,15... | collective-permute-start | bytes 208904 | tf_op jit(solution)/shard_map/ppermute | solution.py:515
  84.1 45.4 %copy-start.1 = (f32[2,512,64]{1,2,0:T(8,128)S(1)}, f32[2,512,64]{1,2,0:T(8,128)}, u32[]{:S(2)}) copy-start(f32[2,512,64]{1,2,0:T(8,128)} %param.13) | copy-start | bytes 786436
  84.1 16.8 %collective-permute-start.20 = (f32[8,2176]{1,0:T(8,128)S(1)}, f32[8,2176]{1,0:T(8,128)S(1)}, u32[]{:S(2)}, u32[]{:S(2)}) collective-permute-start(f32[8,2176]{1,0:T(8,128)S(1)} %get-tuple-element.60), channel_id=1, source_target_pairs={{0,14},{2,12},{4,10},{6,8},{8,6},{10,4},{12,2},{14,0},{1,15},{3,13... | collective-permute-start | bytes 208904 | tf_op jit(solution)/shard_map/ppermute | solution.py:515
  96.1 61.1 %collective-permute-start = (f32[2,4,48,256]{3,2,1,0:T(8,128)S(1)}, f32[2,4,48,256]{3,2,1,0:T(8,128)S(1)}, u32[]{:S(2)}, u32[]{:S(2)}) collective-permute-start(f32[2,4,48,256]{3,2,1,0:T(8,128)S(1)} %get-tuple-element.37), channel_id=1, source_target_pairs={{0,2},{2,4},{4,6},{6,8},{8,10},{10,12},{12,14},{1,3},{3,5},{5,7},{... | collective-permute-start | bytes 1179656 | tf_op jit(solution)/shard_map/ppermute | solution.py:528
  99.4 59.3 %collective-permute-start.1 = (f32[2,4,48,256]{3,2,1,0:T(8,128)S(1)}, f32[2,4,48,256]{3,2,1,0:T(8,128)S(1)}, u32[]{:S(2)}, u32[]{:S(2)}) collective-permute-start(f32[2,4,48,256]{3,2,1,0:T(8,128)S(1)} %get-tuple-element.38), channel_id=1, source_target_pairs={{2,0},{4,2},{6,4},{8,6},{10,8},{12,10},{14,12},{3,1},{5,3},{7,5},{... | collective-permute-start | bytes 1179656 | tf_op jit(solution)/shard_map/ppermute | solution.py:528
  101.0 7.2 %collective-permute-start.27 = (f32[8,2176]{1,0:T(8,128)S(1)}, f32[8,2176]{1,0:T(8,128)S(1)}, u32[]{:S(2)}, u32[]{:S(2)}) collective-permute-start(f32[8,2176]{1,0:T(8,128)S(1)} %shard_map.100.refs_0_), channel_id=1, source_target_pairs={{0,14},{2,12},{4,10},{6,8},{8,6},{10,4},{12,2},{14,0},{1,15},{3,13... | collective-permute-start | bytes 208904 | tf_op jit(solution)/shard_map/ppermute | solution.py:515
  105.5 13.7 %collective-permute-start.26 = (f32[8,2176]{1,0:T(8,128)S(1)}, f32[8,2176]{1,0:T(8,128)S(1)}, u32[]{:S(2)}, u32[]{:S(2)}) collective-permute-start(f32[8,2176]{1,0:T(8,128)S(1)} %shard_map.100.refs_0_), channel_id=1, source_target_pairs={{0,12},{2,14},{4,8},{6,10},{8,4},{10,6},{12,0},{14,2},{1,13},{3,15... | collective-permute-start | bytes 208904 | tf_op jit(solution)/shard_map/ppermute | solution.py:515
  107.0 12.3 %collective-permute-start.25 = (f32[8,2176]{1,0:T(8,128)S(1)}, f32[8,2176]{1,0:T(8,128)S(1)}, u32[]{:S(2)}, u32[]{:S(2)}) collective-permute-start(f32[8,2176]{1,0:T(8,128)S(1)} %shard_map.100.refs_0_), channel_id=1, source_target_pairs={{0,10},{2,8},{4,14},{6,12},{8,2},{10,0},{12,6},{14,4},{1,11},{3,9}... | collective-permute-start | bytes 208904 | tf_op jit(solution)/shard_map/ppermute | solution.py:515
  108.2 14.6 %collective-permute-start.24 = (f32[8,2176]{1,0:T(8,128)S(1)}, f32[8,2176]{1,0:T(8,128)S(1)}, u32[]{:S(2)}, u32[]{:S(2)}) collective-permute-start(f32[8,2176]{1,0:T(8,128)S(1)} %shard_map.100.refs_0_), channel_id=1, source_target_pairs={{0,8},{2,10},{4,12},{6,14},{8,0},{10,2},{12,4},{14,6},{1,9},{3,11}... | collective-permute-start | bytes 208904 | tf_op jit(solution)/shard_map/ppermute | solution.py:515
  119.2 6.0 %collective-permute-start.23 = (f32[8,2176]{1,0:T(8,128)S(1)}, f32[8,2176]{1,0:T(8,128)S(1)}, u32[]{:S(2)}, u32[]{:S(2)}) collective-permute-start(f32[8,2176]{1,0:T(8,128)S(1)} %shard_map.100.refs_0_), channel_id=1, source_target_pairs={{0,6},{2,4},{4,2},{6,0},{8,14},{10,12},{12,10},{14,8},{1,7},{3,5},... | collective-permute-start | bytes 208904 | tf_op jit(solution)/shard_map/ppermute | solution.py:515
  119.2 36.5 %collective-permute-start.2 = (f32[2,4,64,128]{3,2,1,0:T(8,128)S(1)}, f32[2,4,64,128]{3,2,1,0:T(8,128)S(1)}, u32[]{:S(2)}, u32[]{:S(2)}) collective-permute-start(f32[2,4,64,128]{3,2,1,0:T(8,128)S(1)} %get-tuple-element.39), channel_id=1, source_target_pairs={{0,1},{1,0},{2,3},{3,2},{4,5},{5,4},{6,7},{7,6},{8,9},{9,8},{10,11... | collective-permute-start | bytes 786440 | tf_op jit(solution)/shard_map/ppermute | solution.py:520
  122.8 4.3 %collective-permute-start.22 = (f32[8,2176]{1,0:T(8,128)S(1)}, f32[8,2176]{1,0:T(8,128)S(1)}, u32[]{:S(2)}, u32[]{:S(2)}) collective-permute-start(f32[8,2176]{1,0:T(8,128)S(1)} %shard_map.100.refs_0_), channel_id=1, source_target_pairs={{0,4},{2,6},{4,0},{6,2},{8,12},{10,14},{12,8},{14,10},{1,5},{3,7},... | collective-permute-start | bytes 208904 | tf_op jit(solution)/shard_map/ppermute | solution.py:515
  125.2 4.3 %collective-permute-start.21 = (f32[8,2176]{1,0:T(8,128)S(1)}, f32[8,2176]{1,0:T(8,128)S(1)}, u32[]{:S(2)}, u32[]{:S(2)}) collective-permute-start(f32[8,2176]{1,0:T(8,128)S(1)} %shard_map.100.refs_0_), channel_id=1, source_target_pairs={{0,2},{2,0},{4,6},{6,4},{8,10},{10,8},{12,14},{14,12},{1,3},{3,1},... | collective-permute-start | bytes 208904 | tf_op jit(solution)/shard_map/ppermute | solution.py:515
  150.2 1.4 collective-permute-start.28
  153.7 6.5 %collective-permute-start.29 = (f32[2,8,512]{2,1,0:T(8,128)S(1)}, f32[2,8,512]{2,1,0:T(8,128)S(1)}, u32[]{:S(2)}, u32[]{:S(2)}) collective-permute-start(f32[2,8,512]{2,1,0:T(8,128)S(1)} %get-tuple-element.64), channel_id=1, source_target_pairs={{0,2},{2,0},{4,6},{6,4},{8,10},{10,8},{12,14},{14,12},{1,3},{3,1},... | collective-permute-start | bytes 98312 | tf_op jit(solution)/shard_map/ppermute | solution.py:515
  154.3 8.2 %collective-permute-start.30 = (f32[2,8,512]{2,1,0:T(8,128)S(1)}, f32[2,8,512]{2,1,0:T(8,128)S(1)}, u32[]{:S(2)}, u32[]{:S(2)}) collective-permute-start(f32[2,8,512]{2,1,0:T(8,128)S(1)} %get-tuple-element.65), channel_id=1, source_target_pairs={{0,4},{2,6},{4,0},{6,2},{8,12},{10,14},{12,8},{14,10},{1,5},{3,7},... | collective-permute-start | bytes 98312 | tf_op jit(solution)/shard_map/ppermute | solution.py:515
  155.8 40.1 %collective-permute-start.31 = (f32[2,8,512]{2,1,0:T(8,128)S(1)}, f32[2,8,512]{2,1,0:T(8,128)S(1)}, u32[]{:S(2)}, u32[]{:S(2)}) collective-permute-start(f32[2,8,512]{2,1,0:T(8,128)S(1)} %get-tuple-element.66), channel_id=1, source_target_pairs={{0,6},{2,4},{4,2},{6,0},{8,14},{10,12},{12,10},{14,8},{1,7},{3,5},... | collective-permute-start | bytes 98312 | tf_op jit(solution)/shard_map/ppermute | solution.py:515
  157.2 38.6 %collective-permute-start.32 = (f32[2,8,512]{2,1,0:T(8,128)S(1)}, f32[2,8,512]{2,1,0:T(8,128)S(1)}, u32[]{:S(2)}, u32[]{:S(2)}) collective-permute-start(f32[2,8,512]{2,1,0:T(8,128)S(1)} %get-tuple-element.67), channel_id=1, source_target_pairs={{0,8},{2,10},{4,12},{6,14},{8,0},{10,2},{12,4},{14,6},{1,9},{3,11}... | collective-permute-start | bytes 98312 | tf_op jit(solution)/shard_map/ppermute | solution.py:515
  158.7 37.1 %collective-permute-start.33 = (f32[2,8,512]{2,1,0:T(8,128)S(1)}, f32[2,8,512]{2,1,0:T(8,128)S(1)}, u32[]{:S(2)}, u32[]{:S(2)}) collective-permute-start(f32[2,8,512]{2,1,0:T(8,128)S(1)} %get-tuple-element.68), channel_id=1, source_target_pairs={{0,10},{2,8},{4,14},{6,12},{8,2},{10,0},{12,6},{14,4},{1,11},{3,9}... | collective-permute-start | bytes 98312 | tf_op jit(solution)/shard_map/ppermute | solution.py:515
  160.2 35.6 %collective-permute-start.34 = (f32[2,8,512]{2,1,0:T(8,128)S(1)}, f32[2,8,512]{2,1,0:T(8,128)S(1)}, u32[]{:S(2)}, u32[]{:S(2)}) collective-permute-start(f32[2,8,512]{2,1,0:T(8,128)S(1)} %get-tuple-element.69), channel_id=1, source_target_pairs={{0,12},{2,14},{4,8},{6,10},{8,4},{10,6},{12,0},{14,2},{1,13},{3,15... | collective-permute-start | bytes 98312 | tf_op jit(solution)/shard_map/ppermute | solution.py:515
  162.5 33.3 %collective-permute-start.35 = (f32[2,8,512]{2,1,0:T(8,128)S(1)}, f32[2,8,512]{2,1,0:T(8,128)S(1)}, u32[]{:S(2)}, u32[]{:S(2)}) collective-permute-start(f32[2,8,512]{2,1,0:T(8,128)S(1)} %get-tuple-element.70), channel_id=1, source_target_pairs={{0,14},{2,12},{4,10},{6,8},{8,6},{10,4},{12,2},{14,0},{1,15},{3,13... | collective-permute-start | bytes 98312 | tf_op jit(solution)/shard_map/ppermute | solution.py:515

commit v2 on v1

--- a/solution.py
+++ b/solution.py
@@ -39,15 +39,13 @@
     return high, middle, low
 
 
-def edges_kernel(idx_ref, first_ref, last_ref, half_ref, top_ref, bottom_ref, side_ref):
+def edges_kernel(idx_ref, half_ref, side_ref):
     fb, planes, rows = half_ref.shape[1:4]
     lane = lax.broadcasted_iota(jnp.int32, (rows, 128), 1)
     offset = jnp.where(idx_ref[1] == 0, 1, 0)
     for f in range(fb):
         side = jnp.zeros((rows, 128), f32)
         for z in range(planes):
-            top_ref[0, f, z : z + 1, :] = first_ref[0, f, z, 0:1, :]
-            bottom_ref[0, f, z : z + 1, :] = last_ref[0, f, z, 7:8, :]
             turned = pltpu.roll(half_ref[0, f, z], z + offset, 1)
             side = jnp.where(lane == z, turned, side)
         side_ref[0, f] = side
@@ -55,40 +53,32 @@
 
 def edges(idx, fields, planes, fb):
     m, f, _, rows, cols = fields.shape
-    last = rows // 8 - 1
     tail = cols // 128 - 1
-    edge_row = jax.ShapeDtypeStruct((m, f, planes, cols), f32)
     return pl.pallas_call(
         edges_kernel,
         grid_spec=pltpu.PrefetchScalarGridSpec(
             num_scalar_prefetch=1,
             grid=(m, f // fb),
             in_specs=[
-                pl.BlockSpec((1, fb, planes, 8, cols), lambda i, j, s: (i, j, 0, 0, 0)),
-                pl.BlockSpec((1, fb, planes, 8, cols), lambda i, j, s: (i, j, 0, last, 0)),
                 pl.BlockSpec(
                     (1, fb, planes, rows, 128),
                     lambda i, j, s: (i, j, 0, 0, jnp.where(s[1] == 0, tail, 0)),
                 ),
             ],
-            out_specs=[
-                pl.BlockSpec((1, fb, planes, cols), lambda i, j, s: (i, j, 0, 0)),
-                pl.BlockSpec((1, fb, planes, cols), lambda i, j, s: (i, j, 0, 0)),
-                pl.BlockSpec((1, fb, rows, 128), lambda i, j, s: (i, j, 0, 0)),
-            ],
-        ),
-        out_shape=[edge_row, edge_row, jax.ShapeDtypeStruct((m, f, rows, 128), f32)],
+            out_specs=pl.BlockSpec((1, fb, rows, 128), lambda i, j, s: (i, j, 0, 0)),
+        ),
+        out_shape=jax.ShapeDtypeStruct((m, f, rows, 128), f32),
         compiler_params=params_of(32),
         cost_estimate=pl.CostEstimate(
             flops=m * f * planes * rows * 256,
-            bytes_accessed=m * f * planes * (rows * 128 + 16 * cols) * 4,
+            bytes_accessed=m * f * planes * rows * 128 * 4,
             transcendentals=0,
         ),
-    )(idx, fields, fields, fields)
+    )(idx, fields)
 
 
 def step_block(idx_ref, coef_ref, refs, zb, z0, m, store):
-    now, before, after, xu, xd, yh, sx, sy, sz = refs
+    now, before, after, yh, sx, sy, sz = refs
     nf, rows, cols = now.shape[1], now.shape[3], now.shape[4]
     tiles = cols // 128
     wide = sx.shape[-1]
@@ -140,11 +130,11 @@
                 c = cells[f]
                 a, c0, c1, c2, s = coefs[f]
                 if r == 0:
-                    over = xu[0, f, pl.ds(z0 + z, 1), :]
+                    over = jnp.zeros((1, cols), f32)
                 else:
                     over = now[0, f, z, r - 1 : r, :]
                 if r + 8 == rows:
-                    under = xd[0, f, pl.ds(z0 + z, 1), :]
+                    under = jnp.zeros((1, cols), f32)
                 else:
                     under = now[0, f, z, r + 8 : r + 9, :]
                 up = jnp.where(is_top, over, pltpu.roll(c, 1, 0))
@@ -186,27 +176,31 @@
 
 
 def bulk_kernel(idx_ref, coef_ref, *refs):
-    out = refs[-1]
+    now = refs[0]
+    out, top, bottom = refs[-3:]
+    nf, rows = now.shape[1], now.shape[3]
     m, t = pl.program_id(0), pl.program_id(1)
+    for f in range(nf):
+        for z in range(ZB):
+            top[0, f, z : z + 1, :] = now[0, f, z, 0:1, :]
+            bottom[0, f, z : z + 1, :] = now[0, f, z, rows - 1 : rows, :]
 
     def store(f, z, r, value):
         out[0, f, z, r : r + 8, :] = value
 
-    step_block(idx_ref, coef_ref, refs[:-1], ZB, t * ZB, m, store)
-
-
-def step_specs(fields, planes, zb, halo_planes, wide):
+    step_block(idx_ref, coef_ref, refs[:-3], ZB, t * ZB, m, store)
+
+
+def step_specs(fields, zb, wide, place):
     m, f, nz, rows, cols = fields.shape
 
     def at(shape, index):
-        return pl.BlockSpec(shape, index)
+        return pl.BlockSpec(shape, lambda *g: index(*place(*g), None))
 
     return [
         at((1, f, zb, rows, cols), lambda i, t, s: (i, 0, t, 0, 0)),
         at((1, f, 1, rows, cols), lambda i, t, s: (i, 0, jnp.maximum(t * zb - 1, 0), 0, 0)),
         at((1, f, 1, rows, cols), lambda i, t, s: (i, 0, jnp.minimum(t * zb + zb, nz - 1), 0, 0)),
-        at((1, f, halo_planes, cols), lambda i, t, s: (i, 0, 0, 0)),
-        at((1, f, halo_planes, cols), lambda i, t, s: (i, 0, 0, 0)),
         at((1, f, rows, 128), lambda i, t, s: (i, 0, 0, 0)),
         at((1, 1, wide), lambda i, t, s: (i, 0, 0)),
         at((1, wide, 1), lambda i, t, s: (i, 0, 0)),
@@ -214,42 +208,60 @@
     ]
 
 
-def bulk(idx, coefs, fields, halos, seeds):
+def bulk(idx, coefs, fields, side, seeds):
     m, f, nz, rows, cols = fields.shape
     wide = seeds[0].shape[-1]
-    specs = step_specs(fields, nz, ZB, nz, wide)
+    specs = step_specs(fields, ZB, wide, lambda i, t, s: (i, t))
     return pl.pallas_call(
         bulk_kernel,
         grid_spec=pltpu.PrefetchScalarGridSpec(
             num_scalar_prefetch=1,
             grid=(m, nz // ZB),
             in_specs=[smem()] + specs,
-            out_specs=pl.BlockSpec((1, f, ZB, rows, cols), lambda i, t, s: (i, 0, t, 0, 0)),
-        ),
-        out_shape=jax.ShapeDtypeStruct(fields.shape, f32),
+            out_specs=[
+                pl.BlockSpec((1, f, ZB, rows, cols), lambda i, t, s: (i, 0, t, 0, 0)),
+                pl.BlockSpec((1, f, ZB, cols), lambda i, t, s: (i, 0, t, 0)),
+                pl.BlockSpec((1, f, ZB, cols), lambda i, t, s: (i, 0, t, 0)),
+            ],
+        ),
+        out_shape=[
+            jax.ShapeDtypeStruct(fields.shape, f32),
+            jax.ShapeDtypeStruct((m, f, nz, cols), f32),
+            jax.ShapeDtypeStruct((m, f, nz, cols), f32),
+        ],
         compiler_params=params_of(40),
         cost_estimate=pl.CostEstimate(
             flops=fields.size * 30, bytes_accessed=fields.size * 10, transcendentals=0
         ),
-    )(idx, coefs, fields, fields, fields, *halos, *seeds)
+    )(idx, coefs, fields, fields, fields, side, *seeds)
 
 
 def slab_kernel(n, ppd, yb, idx_ref, coef_ref, *refs):
-    ins, outs, scratch = refs[:9], refs[9 : 9 + n], refs[9 + n]
+    ins, out = refs[:7], refs[7]
+    now = ins[0]
+    nf, rows = now.shape[1], now.shape[3]
     m = pl.program_id(0)
-    me = idx_ref[0]
-    ysp = ins[0].shape[4] // yb
+    ysp = now.shape[4] // yb
+    members = (out.shape[1] - 8) // (ppd * rows)
 
     def store(f, z, r, value):
-        p = f * ZS + z
         for h in range(ysp):
-            scratch[p * ysp + h, r : r + 8, :] = value[:, h * yb : h * yb + yb]
+            d, j = divmod((f * ZS + z) * ysp + h, ppd)
+            at = pl.multiple_of((m * ppd + j) * rows, rows) + r
+            out[d, pl.ds(at, 8), :] = value[:, h * yb : h * yb + yb]
 
     step_block(idx_ref, coef_ref, ins, ZS, 0, m, store)
-    for k in range(n):
-        dest = me ^ k
-        for j in range(ppd):
-            outs[k][0, j] = scratch[dest * ppd + j]
+    for i in range(members):
+
+        @pl.when(m == i)
+        def _():
+            for f in range(nf):
+                for z in range(ZS):
+                    for h in range(ysp):
+                        d, j = divmod((f * ZS + z) * ysp + h, ppd)
+                        at = members * ppd * rows + 2 * (i * ppd + j)
+                        out[d, at : at + 1, :] = now[0, f, z, 0:1, h * yb : h * yb + yb]
+                        out[d, at + 1 : at + 2, :] = now[0, f, z, rows - 1 : rows, h * yb : h * yb + yb]
 
 
 def slab_pieces(n, fields):
@@ -259,42 +271,89 @@
     return max(1, count // n), cols // ysp, count * ysp
 
 
-def slab_step(idx, coefs, fields, halos, seeds, n):
+def slab_step(idx, coefs, fields, side, seeds, n):
     m, f, nz, rows, cols = fields.shape
     wide = seeds[0].shape[-1]
     ppd, yb, pieces = slab_pieces(n, fields)
-    piece = jax.ShapeDtypeStruct((m, ppd, rows, yb), f32)
-    specs = step_specs(fields, ZS, ZS, ZS, wide)
+    piece = jax.ShapeDtypeStruct((n, m * ppd * rows + 8, yb), f32)
+    specs = step_specs(fields, ZS, wide, lambda i, t, s: (i, t))
     return pl.pallas_call(
         functools.partial(slab_kernel, n, ppd, yb),
         grid_spec=pltpu.PrefetchScalarGridSpec(
             num_scalar_prefetch=1,
             grid=(m, 1),
             in_specs=[smem()] + specs,
-            out_specs=[pl.BlockSpec((1, ppd, rows, yb), lambda i, t, s: (i, 0, 0, 0))] * n,
-            scratch_shapes=[pltpu.VMEM((pieces, rows, yb), f32)],
-        ),
-        out_shape=[piece] * n,
+            out_specs=pl.BlockSpec(piece.shape, lambda i, t, s: (0, 0, 0)),
+        ),
+        out_shape=piece,
         compiler_params=params_of(32),
         cost_estimate=pl.CostEstimate(
             flops=m * f * ZS * rows * cols * 30,
             bytes_accessed=m * f * ZS * rows * cols * 10,
             transcendentals=0,
         ),
-    )(idx, coefs, fields, fields, fields, *halos, *seeds)
-
-
-def gram_kernel(n, idx_ref, *refs):
-    ins, (own_ref, other_ref, fibre), folded = refs[:n], refs[n : n + 3], refs[n + 3]
+    )(idx, coefs, fields, fields, fields, side, *seeds)
+
+
+def mend_kernel(coef_ref, value_ref, before_ref, after_ref, out_ref):
+    m, f, end = pl.program_id(0), pl.program_id(1), pl.program_id(2)
+    a = coef_ref[m, f, 0]
+    planes = out_ref.shape[2]
+    out_ref[...] = value_ref[...]
+
+    @pl.when(end == 0)
+    def _():
+        for z in range(planes):
+            out_ref[0, 0, z, 0:1, :] = value_ref[0, 0, z, 0:1, :] + a * before_ref[0, 0, z : z + 1, :]
+
+    @pl.when(end == 1)
+    def _():
+        for z in range(planes):
+            out_ref[0, 0, z, 7:8, :] = value_ref[0, 0, z, 7:8, :] + a * after_ref[0, 0, z : z + 1, :]
+
+
+def mend(coefs, value, before, after):
+    m, f, nz, rows, cols = value.shape
+    last = rows // 8 - 1
+    block = pl.BlockSpec((1, 1, nz, 8, cols), lambda i, j, e: (i, j, 0, e * last, 0))
+    halo = pl.BlockSpec((1, 1, nz, cols), lambda i, j, e: (i, j, 0, 0))
+    return pl.pallas_call(
+        mend_kernel,
+        grid=(m, f, 2),
+        in_specs=[smem(), block, halo, halo],
+        out_specs=block,
+        out_shape=jax.ShapeDtypeStruct(value.shape, f32),
+        input_output_aliases={1: 0},
+        compiler_params=params_of(16),
+        cost_estimate=pl.CostEstimate(
+            flops=m * f * nz * 4 * cols, bytes_accessed=m * f * nz * 32 * cols * 4, transcendentals=0
+        ),
+    )(coefs, value, before, after)
+
+
+def gram_kernel(n, ppd, ysp, idx_ref, coef_ref, *refs):
+    ins, own_ref, other_ref, fibre, folded = refs
     me, core = idx_ref[0], idx_ref[1]
-    members, ppd, rows, yb = ins[0].shape
+    yb = ins.shape[2]
+    members = fibre.shape[0]
+    rows = fibre.shape[1] // n
     half = n * rows // 2
     groups = half // (8 * n)
-    for k in range(n):
-        start = pl.multiple_of((me ^ k) * rows, rows)
+    edge = members * ppd * rows
+    for b in range(n):
         for m in range(members):
             for j in range(ppd):
-                fibre[m, pl.ds(start, rows), j * yb : j * yb + yb] = ins[k][m, j]
+                at = (m * ppd + j) * rows
+                fibre[m, b * rows : (b + 1) * rows, j * yb : j * yb + yb] = ins[b, at : at + rows, :]
+    for m in range(members):
+        for j in range(ppd):
+            a = coef_ref[m, (me * ppd + j) // (ysp * ZS), 0]
+            at = edge + 2 * (m * ppd + j)
+            here = slice(j * yb, j * yb + yb)
+            for b in range(n - 1):
+                low, up = (b + 1) * rows - 1, (b + 1) * rows
+                fibre[m, low : low + 1, here] += a * ins[b + 1, at : at + 1, :]
+                fibre[m, up : up + 1, here] += a * ins[b, at + 1 : at + 2, :]
     r = lax.broadcasted_iota(jnp.int32, (half, half), 0)
     c = lax.broadcasted_iota(jnp.int32, (half, half), 1)
     contract = (((1,), (1,)), ((), ()))
@@ -323,21 +382,21 @@
     other_ref[...] = folded[1 - core]
 
 
-def gram(idx, pieces):
-    n = len(pieces)
-    members, ppd, rows, yb = pieces[0].shape
+def gram(idx, coefs, pieces, members, ppd, ysp):
+    n, length, yb = pieces.shape
+    rows = (length - 8) // (members * ppd)
     half = n * rows // 2
     wide = half // (8 * n) * 2 * half + 128
     chunk = jax.ShapeDtypeStruct((n, 8, wide), f32)
     fibre = jax.ShapeDtypeStruct((members, n * rows, ppd * yb), f32)
     return pl.pallas_call(
-        functools.partial(gram_kernel, n),
-        in_specs=[smem()] + [vmem()] * n,
+        functools.partial(gram_kernel, n, ppd, ysp),
+        in_specs=[smem(), smem(), vmem()],
         out_specs=[vmem()] * 3,
         out_shape=[chunk, chunk, fibre],
         scratch_shapes=[pltpu.VMEM((members, n, 8, wide), f32)],
         compiler_params=params_of(40),
-    )(idx, *pieces)
+    )(idx, coefs, pieces)
 
 
 def spread_kernel(n, idx_ref, own_ref, got_ref, *outs):
@@ -444,63 +503,54 @@
     )(idx, start, *pieces)
 
 
-def project_kernel(n, idx_ref, own_ref, got_ref, fibre, basis_ref, *refs):
-    outs, rows = refs[:n], refs[n]
-    me, core = idx_ref[0], idx_ref[1]
-    members = fibre.shape[0]
-    share = outs[0].shape[1]
+def project_kernel(n, idx_ref, own_ref, got_ref, fibre, basis_ref, out_ref):
+    core = idx_ref[1]
+    share = out_ref.shape[2]
     basis_ref[core] = own_ref[...]
     basis_ref[1 - core] = got_ref[...]
-    for m in range(members):
+    for m in range(fibre.shape[0]):
         value = jnp.dot(basis_ref[m], fibre[m], precision=highest, preferred_element_type=f32)
         for d in range(n):
-            rows[d, m] = value[d * share : (d + 1) * share, :]
-    for k in range(n):
-        outs[k][...] = rows[me ^ k]
+            out_ref[d, m] = value[d * share : (d + 1) * share, :]
 
 
 def project(idx, own, got, fibre, n):
     members, _, depth = fibre.shape
     rank, size = own.shape
-    piece = (members, rank // n, depth)
     return pl.pallas_call(
         functools.partial(project_kernel, n),
         in_specs=[smem()] + [vmem()] * 3,
-        out_specs=[vmem()] * (n + 1),
-        out_shape=[jax.ShapeDtypeStruct((members, rank, size), f32)] + [jax.ShapeDtypeStruct(piece, f32)] * n,
-        scratch_shapes=[pltpu.VMEM((n,) + piece, f32)],
+        out_specs=[vmem()] * 2,
+        out_shape=[
+            jax.ShapeDtypeStruct((members, rank, size), f32),
+            jax.ShapeDtypeStruct((n, members, rank // n, depth), f32),
+        ],
         compiler_params=params_of(32),
     )(idx, own, got, fibre)
 
 
-def gather_kernel(n, ppd, yb, idx_ref, *refs):
-    ins, out, held = refs[:n], refs[n], refs[n + 1]
+def gather_kernel(ppd, yb, held, out):
     members, share, nf, planes, cols = out.shape
     ysp = cols // yb
-    for k in range(n):
-        held[idx_ref[0] ^ k] = ins[k][...]
     for m in range(members):
         for s in range(share):
             for p in range(nf * planes):
                 f, z = divmod(p, planes)
                 for h in range(ysp):
-                    piece = p * ysp + h
-                    d, j = divmod(piece, ppd)
+                    d, j = divmod(p * ysp + h, ppd)
                     out[m, s, f, z : z + 1, h * yb : (h + 1) * yb] = held[
                         d, m, s : s + 1, j * yb : (j + 1) * yb
                     ]
 
 
-def gather(idx, pieces, shape, ppd, yb):
-    n = len(pieces)
-    return pl.pallas_call(
-        functools.partial(gather_kernel, n, ppd, yb),
-        in_specs=[smem()] + [vmem()] * n,
+def gather(pieces, shape, ppd, yb):
+    return pl.pallas_call(
+        functools.partial(gather_kernel, ppd, yb),
+        in_specs=[vmem()],
         out_specs=vmem(),
         out_shape=jax.ShapeDtypeStruct(shape, f32),
-        scratch_shapes=[pltpu.VMEM((n,) + pieces[0].shape, f32)],
         compiler_params=params_of(16),
-    )(idx, *pieces)
+    )(pieces)
 
 
 def member_params(member_index, member_table):
@@ -518,14 +568,6 @@
 
 def swap_cores(value):
     return lax.ppermute(value, "gy", [(0, 1), (1, 0)])
-
-
-def halos_of(idx, fields, planes, fb):
-    n = lax.axis_size("gx")
-    up = [(i, i + 1) for i in range(n - 1)]
-    down = [(j, i) for i, j in up]
-    top, bottom, side = edges(idx, fields, planes, fb)
-    return (lax.ppermute(bottom, "gx", up), lax.ppermute(top, "gx", down), swap_cores(side))
 
 
 def per_device(fields, member_index, member_table, seed_x, seed_y, seed_z, start_basis):
@@ -545,21 +587,27 @@
         jnp.tile(seed_y.astype(f32), (1, 6))[:, :, None],
         jnp.tile(seed_z.astype(f32), (1, 6))[:, None, :],
     )
-    slab_halos = halos_of(idx, fields, ZS, nf)
-    halos = halos_of(idx, fields, fields.shape[2], 1)
-    slab = slab_step(idx, coefs, fields, slab_halos, seeds, n)
-    pieces = exchange(slab)
-    fields_next = bulk(idx, coefs, fields, halos, seeds)
-    own, other, fibre = gram(idx, pieces)
+    ppd, yb, _ = slab_pieces(n, fields)
+    up = [(i, i + 1) for i in range(n - 1)]
+    down = [(j, i) for i, j in up]
+    slab_side = swap_cores(edges(idx, fields, ZS, nf))
+    pieces = lax.all_to_all(slab_step(idx, coefs, fields, slab_side, seeds, n), "gx", 0, 0)
+    side = swap_cores(edges(idx, fields, fields.shape[2], 2))
+    value, top, bottom = bulk(idx, coefs, fields, side, seeds)
+    pieces, value = lax.optimization_barrier((pieces, value))
+    own, other, fibre = gram(idx, coefs, pieces, members, ppd, fields.shape[4] // yb)
     parts = exchange(spread(idx, own, swap_cores(other)))
     mine = total(parts)
     grams = exchange([mine] * n)
+    grams, top, bottom = lax.optimization_barrier((grams, top, bottom))
+    before, after = lax.ppermute(bottom, "gx", up), lax.ppermute(top, "gx", down)
     start = jnp.swapaxes(start_basis, 1, 2)
     basis = iterate(idx, start, grams)
-    bases, *rows = project(idx, basis, swap_cores(basis), fibre, n)
-    ppd, yb, _ = slab_pieces(n, fields)
+    basis, before, after = lax.optimization_barrier((basis, before, after))
+    bases, rows = project(idx, basis, swap_cores(basis), fibre, n)
+    fields_next = mend(coefs, value, before, after)
     share = start_basis.shape[2] // n
-    core = gather(idx, exchange(rows), (members, share, nf, ZS, fields.shape[4]), ppd, yb)
+    core = gather(lax.all_to_all(rows, "gx", 0, 0), (members, share, nf, ZS, fields.shape[4]), ppd, yb)
     return (fields_next, jnp.swapaxes(bases, 1, 2), core)
 
 

time: 198 us -> 157 us (0.79)
  starting transfers between devices: 69.3 us -> 42.6 us
  waiting for transfers between devices: 49.9 us -> 25.9 us
  Pallas kernels: 76.3 us -> 85.7 us
    ppermute x28 -> x14, starting transfers between devices: 58.1 us -> 23.1 us  [exchange(): lax.ppermute(pieces[k], 'gx', [(i, i ^ k) for i in range(n)])]
    ppermute x28 -> x14, waiting for transfers between devices: 43 us -> 10.8 us  [exchange(): lax.ppermute(pieces[k], 'gx', [(i, i ^ k) for i in range(n)])]
    all_to_all x0 -> x2, starting transfers between devices: none -> 14.1 us  [the longest x1 7.2 us: per_device(): lax.all_to_all(slab_step(idx, coefs, fields, slab_side, seeds, n), 'gx',...]
    pallas_call x2 -> x3, Pallas kernels: 4.95 us -> 15.9 us  [the longest x1 11.4 us: mend(): pl.pallas_call(mend_kernel, grid=(m, f, 2), in_specs=[smem(), block, halo...]
    all_to_all x0 -> x2, waiting for transfers between devices: none -> 9.96 us  [the longest x1 9.96 us: per_device(): lax.all_to_all(slab_step(idx, coefs, fields, slab_side, seeds, n), 'gx',...]
    ppermute x4 -> x2, starting transfers between devices: 11 us -> 4.69 us  [the longest x1 3.22 us: per_device(): lax.ppermute(bottom, 'gx', up)]
    ppermute x4 -> x2, waiting for transfers between devices: 3.6 us -> 0.01 us  [the longest x1 0.01 us: per_device(): lax.ppermute(bottom, 'gx', up)]
    pallas_call x2, Pallas kernels: 12.7 us -> 9.51 us  [edges(): pl.pallas_call(edges_kernel, grid_spec=pltpu.PrefetchScalarGridSpec(num_s...]
  transfers between devices with their start and end apart: 36 -> 22, of which waited for: 12 -> 9; matrix products, arithmetic and copies ran while one was open for 0% -> 0% of each run, Pallas kernels for 33% -> 45%
where the time goes in v2:
time: 157 us; the launch traced here: 156 us
  Pallas kernels  85.7 us (55%)
  starting transfers between devices  42.6 us (27%)
  waiting for transfers between devices  25.9 us (16%)
    pallas_call x1, Pallas kernels, bulk(): pl.pallas_call(bulk_kernel, grid_spec=pltpu.PrefetchScalarGridSpec(num_sc...  30.9 us
    ppermute x14, starting transfers between devices, exchange(): lax.ppermute(pieces[k], 'gx', [(i, i ^ k) for i in range(n)])  23.1 us
    pallas_call x1, Pallas kernels, iterate(): pl.pallas_call(functools.partial(iterate_kernel, n), in_specs=[smem()] +...  20.7 us
    pallas_call x1, Pallas kernels, mend(): pl.pallas_call(mend_kernel, grid=(m, f, 2), in_specs=[smem(), block, halo...  11.4 us
    ppermute x14, waiting for transfers between devices, exchange(): lax.ppermute(pieces[k], 'gx', [(i, i ^ k) for i in range(n)])  10.8 us
    all_to_all x1, waiting for transfers between devices, per_device(): lax.all_to_all(slab_step(idx, coefs, fields, slab_side, seeds, n), 'gx',...  9.96 us
    pallas_call x2, Pallas kernels, edges(): pl.pallas_call(edges_kernel, grid_spec=pltpu.PrefetchScalarGridSpec(num_s...  9.51 us
    all_to_all x1, starting transfers between devices, per_device(): lax.all_to_all(slab_step(idx, coefs, fields, slab_side, seeds, n), 'gx',...  7.2 us
  transfers between devices with their start and end apart: 22, of which 9 were waited for; matrix products, arithmetic and copies ran while one was open for 0% of the time, Pallas kernels for 45%

profile of v2, /device:TPU:0, one launch (start us, length us, event | category | flops | bytes accessed | tf_op | source)
XLA Modules:
  0.0 155.9 jit_solution(7089204433355485151)
XLA Ops:
  0.6 0.0 copy-start
  0.7 0.1 pad_add_fusion.idx_ref
  0.8 2.1 %shard_map.94 = f32[2,4,64,128]{3,2,1,0:T(8,128)S(1)} custom-call(s32[2]{0:T(128)S(1)} %pad_add_fusion.idx_ref, f32[2,4,48,64,256]{4,3,2,1,0:T(8,128)} %refs_2_.3), custom_call_target="tpu_custom_call" | custom-call | flops 524288 | bytes 1048576 | tf_op jit(solution)/shard_map/pallas_call | solution.py:57
  2.8 0.5 collective-permute-start
  3.4 0.2 fusion
  3.6 0.1 fusion.5
  3.7 0.0 copy-done.2
  3.7 0.1 tile.30.refs_5_
  3.9 0.1 tile.25
  4.0 0.1 tile.29
  4.0 0.1 stack.8.coef_ref
  4.1 0.4 collective-permute-done.refs_3_
  4.5 5.6 %shard_map.95 = f32[8,264,256]{2,1,0:T(8,128)} custom-call(s32[2]{0:T(128)S(1)} %pad_add_fusion.idx_ref, f32[2,4,5]{2,1,0:T(4,128)S(1)} %stack.8.coef_ref, f32[2,4,48,64,256]{4,3,2,1,0:T(8,128)} %refs_2_.3, f32[2,4,48,64,256]{4,3,2,1,0:T(8,128)} %refs_2_.3, f32[2,4,48,64,256]{4,3,2,1,0:T(8,128)} %refs_2_.3, ...), custom_call_target="tpu_custom_call" | custom-call | flops 15728640 | bytes 5242880 | tf_op jit(solution)/shard_map/pallas_call | solution.py:280
  10.1 7.2 %all-to-all-start = ((f32[8,264,256]{2,1,0:T(8,128)}), f32[8,264,256]{2,1,0:T(8,128)S(1)}, u32[]{:S(2)}, u32[]{:S(2)}) async-start(f32[8,264,256]{2,1,0:T(8,128)} %shard_map.95), calls=%async_computation | async-start | bytes 4325376 | tf_op jit(solution)/shard_map/all_to_all | solution.py:594
  17.3 7.5 %shard_map.96 = f32[2,4,64,128]{3,2,1,0:T(8,128)S(1)} custom-call(s32[2]{0:T(128)S(1)} %pad_add_fusion.idx_ref, f32[2,4,48,64,256]{4,3,2,1,0:T(8,128)} %refs_2_.3), custom_call_target="tpu_custom_call" | custom-call | flops 6291456 | bytes 12582912 | tf_op jit(solution)/shard_map/pallas_call | solution.py:57
  24.7 0.0 copy-start.1
  24.8 0.1 collective-permute-start.1
  24.8 1.5 collective-permute-done.1.refs_3_
  26.4 30.9 %shard_map.97 = (f32[2,4,48,64,256]{4,3,2,1,0:T(8,128)}, f32[2,4,48,256]{3,2,1,0:T(8,128)S(1)}, f32[2,4,48,256]{3,2,1,0:T(8,128)S(1)}) custom-call(s32[2]{0:T(128)S(1)} %pad_add_fusion.idx_ref, f32[2,4,5]{2,1,0:T(4,128)S(1)} %stack.8.coef_ref, f32[2,4,48,64,256]{4,3,2,1,0:T(8,128)} %refs_2_.3, f32[2,4,48,64,256]{4,3,2,1,0:T(8,128)} %refs_2_.3, ...), custom_call_target="tpu_custom_call" | custom-call | flops 188743680 | bytes 62914560 | tf_op jit(solution)/shard_map/pallas_call | solution.py:215
  57.3 10.0 %all-to-all-done.refs_0_ = f32[8,264,256]{2,1,0:T(8,128)S(1)} async-done(((f32[8,264,256]{2,1,0:T(8,128)}), f32[8,264,256]{2,1,0:T(8,128)S(1)}, u32[]{:S(2)}, u32[]{:S(2)}) %all-to-all-start) | async-done | bytes 2162720 | tf_op jit(solution)/shard_map/all_to_all | solution.py:594
  67.2 3.6 %shard_map.98 = (f32[8,8,2176]{2,1,0:T(8,128)S(1)}, f32[8,8,2176]{2,1,0:T(8,128)S(1)}, f32[2,512,512]{2,1,0:T(8,128)S(1)}) custom-call(s32[2]{0:T(128)S(1)} %pad_add_fusion.idx_ref, f32[2,4,5]{2,1,0:T(4,128)S(1)} %stack.8.coef_ref, f32[8,264,256]{2,1,0:T(8,128)S(1)} %all-to-all-done.refs_0_), custom_call_target="tpu_custom_call" | custom-call | tf_op jit(solution)/shard_map/pallas_call | solution.py:392
  70.8 0.1 collective-permute-start.2
  70.9 1.9 %collective-permute-done.2.got_ref = f32[8,8,2176]{2,1,0:T(8,128)S(1)} collective-permute-done((f32[8,8,2176]{2,1,0:T(8,128)S(1)}, f32[8,8,2176]{2,1,0:T(8,128)S(1)}, u32[]{:S(2)}, u32[]{:S(2)}) %collective-permute-start.2) | collective-permute-done | bytes 557088 | tf_op jit(solution)/shard_map/ppermute | solution.py:570
  72.8 0.6 shard_map.99
  73.4 1.5 collective-permute-start.3
  75.0 0.0 collective-permute-start.4
  75.0 2.0 %collective-permute-start.5 = (f32[8,2176]{1,0:T(8,128)S(1)}, f32[8,2176]{1,0:T(8,128)S(1)}, u32[]{:S(2)}, u32[]{:S(2)}) collective-permute-start(f32[8,2176]{1,0:T(8,128)S(1)} %get-tuple-element.42), channel_id=1, source_target_pairs={{0,6},{2,4},{4,2},{6,0},{8,14},{10,12},{12,10},{14,8},{1,7},{3,5},... | collective-permute-start | bytes 208904 | tf_op jit(solution)/shard_map/ppermute | solution.py:565
  77.0 0.8 collective-permute-start.6
  77.8 3.0 %collective-permute-start.7 = (f32[8,2176]{1,0:T(8,128)S(1)}, f32[8,2176]{1,0:T(8,128)S(1)}, u32[]{:S(2)}, u32[]{:S(2)}) collective-permute-start(f32[8,2176]{1,0:T(8,128)S(1)} %get-tuple-element.44), channel_id=1, source_target_pairs={{0,10},{2,8},{4,14},{6,12},{8,2},{10,0},{12,6},{14,4},{1,11},{3,9}... | collective-permute-start | bytes 208904 | tf_op jit(solution)/shard_map/ppermute | solution.py:565
  80.8 0.0 collective-permute-done.3.refs_1_
  80.8 1.5 collective-permute-start.8
  82.3 0.0 collective-permute-done.4.refs_2_
  82.3 2.4 %collective-permute-start.9 = (f32[8,2176]{1,0:T(8,128)S(1)}, f32[8,2176]{1,0:T(8,128)S(1)}, u32[]{:S(2)}, u32[]{:S(2)}) collective-permute-start(f32[8,2176]{1,0:T(8,128)S(1)} %get-tuple-element.46), channel_id=1, source_target_pairs={{0,14},{2,12},{4,10},{6,8},{8,6},{10,4},{12,2},{14,0},{1,15},{3,13... | collective-permute-start | bytes 208904 | tf_op jit(solution)/shard_map/ppermute | solution.py:565
  84.7 0.0 collective-permute-done.5.refs_3_
  84.7 1.4 collective-permute-done.6.refs_4_
  86.0 4.2 %collective-permute-done.7.refs_5_ = f32[8,2176]{1,0:T(8,128)S(1)} collective-permute-done((f32[8,2176]{1,0:T(8,128)S(1)}, f32[8,2176]{1,0:T(8,128)S(1)}, u32[]{:S(2)}, u32[]{:S(2)}) %collective-permute-start.7) | collective-permute-done | bytes 69664 | tf_op jit(solution)/shard_map/ppermute | solution.py:565
  90.2 0.0 collective-permute-done.8.refs_6_
  90.2 0.0 collective-permute-done.9.refs_7_
  90.2 1.1 collective-permute-start.10
  91.3 2.5 %collective-permute-start.11 = (f32[8,2176]{1,0:T(8,128)S(1)}, f32[8,2176]{1,0:T(8,128)S(1)}, u32[]{:S(2)}, u32[]{:S(2)}) collective-permute-start(f32[8,2176]{1,0:T(8,128)S(1)} %shard_map.100.refs_0_), channel_id=1, source_target_pairs={{0,4},{2,6},{4,0},{6,2},{8,12},{10,14},{12,8},{14,10},{1,5},{3,7},... | collective-permute-start | bytes 208904 | tf_op jit(solution)/shard_map/ppermute | solution.py:565
  93.9 0.6 collective-permute-start.12
  94.5 2.3 %collective-permute-start.13 = (f32[8,2176]{1,0:T(8,128)S(1)}, f32[8,2176]{1,0:T(8,128)S(1)}, u32[]{:S(2)}, u32[]{:S(2)}) collective-permute-start(f32[8,2176]{1,0:T(8,128)S(1)} %shard_map.100.refs_0_), channel_id=1, source_target_pairs={{0,8},{2,10},{4,12},{6,14},{8,0},{10,2},{12,4},{14,6},{1,9},{3,11}... | collective-permute-start | bytes 208904 | tf_op jit(solution)/shard_map/ppermute | solution.py:565
  96.8 0.9 collective-permute-start.14
  97.7 0.0 collective-permute-done.10.refs_1_
  97.7 2.0 %collective-permute-start.15 = (f32[8,2176]{1,0:T(8,128)S(1)}, f32[8,2176]{1,0:T(8,128)S(1)}, u32[]{:S(2)}, u32[]{:S(2)}) collective-permute-start(f32[8,2176]{1,0:T(8,128)S(1)} %shard_map.100.refs_0_), channel_id=1, source_target_pairs={{0,12},{2,14},{4,8},{6,10},{8,4},{10,6},{12,0},{14,2},{1,13},{3,15... | collective-permute-start | bytes 208904 | tf_op jit(solution)/shard_map/ppermute | solution.py:565
  99.7 0.0 collective-permute-done.11.refs_2_
  99.7 2.4 %collective-permute-start.16 = (f32[8,2176]{1,0:T(8,128)S(1)}, f32[8,2176]{1,0:T(8,128)S(1)}, u32[]{:S(2)}, u32[]{:S(2)}) collective-permute-start(f32[8,2176]{1,0:T(8,128)S(1)} %shard_map.100.refs_0_), channel_id=1, source_target_pairs={{0,14},{2,12},{4,10},{6,8},{8,6},{10,4},{12,2},{14,0},{1,15},{3,13... | collective-permute-start | bytes 208904 | tf_op jit(solution)/shard_map/ppermute | solution.py:565
  102.1 0.0 collective-permute-done.12.refs_3_
  102.1 2.8 %collective-permute-done.13.refs_4_ = f32[8,2176]{1,0:T(8,128)S(1)} collective-permute-done((f32[8,2176]{1,0:T(8,128)S(1)}, f32[8,2176]{1,0:T(8,128)S(1)}, u32[]{:S(2)}, u32[]{:S(2)}) %collective-permute-start.13) | collective-permute-done | bytes 69664 | tf_op jit(solution)/shard_map/ppermute | solution.py:565
  105.0 2.4 %collective-permute-done.14.refs_5_ = f32[8,2176]{1,0:T(8,128)S(1)} collective-permute-done((f32[8,2176]{1,0:T(8,128)S(1)}, f32[8,2176]{1,0:T(8,128)S(1)}, u32[]{:S(2)}, u32[]{:S(2)}) %collective-permute-start.14) | collective-permute-done | bytes 69664 | tf_op jit(solution)/shard_map/ppermute | solution.py:565
  107.4 0.0 collective-permute-done.15.refs_6_
  107.4 0.0 collective-permute-done.16.refs_7_
  107.4 3.2 %collective-permute-start.17 = (f32[2,4,48,256]{3,2,1,0:T(8,128)S(1)}, f32[2,4,48,256]{3,2,1,0:T(8,128)S(1)}, u32[]{:S(2)}, u32[]{:S(2)}) collective-permute-start(f32[2,4,48,256]{3,2,1,0:T(8,128)S(1)} %get-tuple-element.57), channel_id=1, source_target_pairs={{0,2},{2,4},{4,6},{6,8},{8,10},{10,12},{12,14},{1,3},{3,5},{5,7},{... | collective-permute-start | bytes 1179656 | tf_op jit(solution)/shard_map/ppermute | solution.py:603
  110.6 1.5 collective-permute-start.18
  112.1 20.7 %shard_map.101.own_ref = f32[64,512]{1,0:T(8,128)S(1)} custom-call(s32[2]{0:T(128)S(1)} %pad_add_fusion.idx_ref, f32[2,64,512]{2,1,0:T(8,128)S(1)} %bitcast.12, f32[8,2176]{1,0:T(8,128)S(1)} %shard_map.100.refs_0_, f32[8,2176]{1,0:T(8,128)S(1)} %collective-permute-done.10.refs_1_, f32[8,2176]{1,0:T(8,128)S(1)} %collective-permute-done.11.refs_2_, ...), custom_call_target="tpu_custom_call" | custom-call | tf_op jit(solution)/shard_map/pallas_call | solution.py:496
  132.8 0.0 collective-permute-done.17.before_ref
  132.8 0.0 collective-permute-done.18.after_ref
  132.8 0.1 collective-permute-start.19
  132.9 1.3 collective-permute-done.19.got_ref
  134.2 2.6 %shard_map.103 = (f32[2,64,512]{2,1,0:T(8,128)}, f32[8,2,8,512]{3,2,1,0:T(8,128)}) custom-call(s32[2]{0:T(128)S(1)} %pad_add_fusion.idx_ref, f32[64,512]{1,0:T(8,128)S(1)} %shard_map.101.own_ref, f32[64,512]{1,0:T(8,128)S(1)} %collective-permute-done.19.got_ref, f32[2,512,512]{2,1,0:T(8,128)S(1)} %get-tuple-element.62.fibre), custom_call_target="tpu_custom_call" | custom-call | tf_op jit(solution)/shard_map/pallas_call | solution.py:520
  136.8 6.9 %all-to-all-start.1 = ((f32[8,2,8,512]{3,2,1,0:T(8,128)}), f32[8,2,8,512]{3,2,1,0:T(8,128)S(1)}, u32[]{:S(2)}, u32[]{:S(2)}) async-start(f32[8,2,8,512]{3,2,1,0:T(8,128)} %get-tuple-element.64), calls=%async_computation.1 | async-start | bytes 524288 | tf_op jit(solution)/shard_map/all_to_all | solution.py:610
  143.6 11.4 %shard_map.102 = f32[2,4,48,64,256]{4,3,2,1,0:T(8,128)} custom-call(f32[2,4,5]{2,1,0:T(4,128)S(1)} %stack.8.coef_ref, f32[2,4,48,64,256]{4,3,2,1,0:T(8,128)} %get-tuple-element.35.value_ref, f32[2,4,48,256]{3,2,1,0:T(8,128)S(1)} %collective-permute-done.17.before_ref, ...), custom_call_target="tpu_custom_call", output_to_operand_aliasing={{}: (1, {})} | custom-call | flops 393216 | bytes 12582912 | tf_op jit(solution)/shard_map/pallas_call | solution.py:320
  155.1 0.0 all-to-all-done.1.held
  155.1 0.8 shard_map.104
  (18 shorter events, 0.1 us)
Async XLA Ops:
  0.6 2.7 %copy-start = (f32[8,4,4]{0,2,1:T(4,128)S(1)}, f32[8,4,4]{0,2,1:T(4,128)}, u32[]{:S(2)}) copy-start(f32[8,4,4]{0,2,1:T(4,128)} %param.9) | copy-start | bytes 1540
  0.6 2.7 %copy-start.5 = (s32[2]{0:T(128)S(1)}, s32[2]{0:T(128)}, u32[]{:S(2)}) copy-start(s32[2]{0:T(128)} %param.8) | copy-start | bytes 28
  0.7 3.0 %copy-start.2 = (s32[2,16]{1,0:T(2,128)S(1)}, s32[2,16]{1,0:T(2,128)}, u32[]{:S(2)}) copy-start(s32[2,16]{1,0:T(2,128)} %param.11) | copy-start | bytes 388
  0.7 3.2 %copy-start.3 = (s32[2,16]{1,0:T(2,128)S(1)}, s32[2,16]{1,0:T(2,128)}, u32[]{:S(2)}) copy-start(s32[2,16]{1,0:T(2,128)} %param.10) | copy-start | bytes 388
  0.7 3.3 %copy-start.4 = (s32[2,16]{1,0:T(2,128)S(1)}, s32[2,16]{1,0:T(2,128)}, u32[]{:S(2)}) copy-start(s32[2,16]{1,0:T(2,128)} %param.12) | copy-start | bytes 388
  2.8 1.7 %collective-permute-start = (f32[2,4,64,128]{3,2,1,0:T(8,128)S(1)}, f32[2,4,64,128]{3,2,1,0:T(8,128)S(1)}, u32[]{:S(2)}, u32[]{:S(2)}) collective-permute-start(f32[2,4,64,128]{3,2,1,0:T(8,128)S(1)} %shard_map.94), channel_id=1, source_target_pairs={{0,1},{1,0},{2,3},{3,2},{4,5},{5,4},{6,7},{7,6},{8,9},{9,8},{10,11... | collective-permute-start | bytes 786440 | tf_op jit(solution)/shard_map/ppermute | solution.py:570
  10.1 57.1 %all-to-all-start = ((f32[8,264,256]{2,1,0:T(8,128)}), f32[8,264,256]{2,1,0:T(8,128)S(1)}, u32[]{:S(2)}, u32[]{:S(2)}) async-start(f32[8,264,256]{2,1,0:T(8,128)} %shard_map.95), calls=%async_computation | async-start | bytes 4325376 | tf_op jit(solution)/shard_map/all_to_all | solution.py:594
  24.7 87.4 %copy-start.1 = (f32[2,512,64]{1,2,0:T(8,128)S(1)}, f32[2,512,64]{1,2,0:T(8,128)}, u32[]{:S(2)}) copy-start(f32[2,512,64]{1,2,0:T(8,128)} %param.13) | copy-start | bytes 786436
  24.8 1.6 %collective-permute-start.1 = (f32[2,4,64,128]{3,2,1,0:T(8,128)S(1)}, f32[2,4,64,128]{3,2,1,0:T(8,128)S(1)}, u32[]{:S(2)}, u32[]{:S(2)}) collective-permute-start(f32[2,4,64,128]{3,2,1,0:T(8,128)S(1)} %shard_map.96), channel_id=1, source_target_pairs={{0,1},{1,0},{2,3},{3,2},{4,5},{5,4},{6,7},{7,6},{8,9},{9,8},{10,11... | collective-permute-start | bytes 786440 | tf_op jit(solution)/shard_map/ppermute | solution.py:570
  70.8 2.0 %collective-permute-start.2 = (f32[8,8,2176]{2,1,0:T(8,128)S(1)}, f32[8,8,2176]{2,1,0:T(8,128)S(1)}, u32[]{:S(2)}, u32[]{:S(2)}) collective-permute-start(f32[8,8,2176]{2,1,0:T(8,128)S(1)} %get-tuple-element.38), channel_id=1, source_target_pairs={{0,1},{1,0},{2,3},{3,2},{4,5},{5,4},{6,7},{7,6},{8,9},{9,8},{10,11... | collective-permute-start | bytes 1671176 | tf_op jit(solution)/shard_map/ppermute | solution.py:570
  73.4 7.4 %collective-permute-start.3 = (f32[8,2176]{1,0:T(8,128)S(1)}, f32[8,2176]{1,0:T(8,128)S(1)}, u32[]{:S(2)}, u32[]{:S(2)}) collective-permute-start(f32[8,2176]{1,0:T(8,128)S(1)} %get-tuple-element.40), channel_id=1, source_target_pairs={{0,2},{2,0},{4,6},{6,4},{8,10},{10,8},{12,14},{14,12},{1,3},{3,1},... | collective-permute-start | bytes 208904 | tf_op jit(solution)/shard_map/ppermute | solution.py:565
  75.0 7.3 %collective-permute-start.4 = (f32[8,2176]{1,0:T(8,128)S(1)}, f32[8,2176]{1,0:T(8,128)S(1)}, u32[]{:S(2)}, u32[]{:S(2)}) collective-permute-start(f32[8,2176]{1,0:T(8,128)S(1)} %get-tuple-element.41), channel_id=1, source_target_pairs={{0,4},{2,6},{4,0},{6,2},{8,12},{10,14},{12,8},{14,10},{1,5},{3,7},... | collective-permute-start | bytes 208904 | tf_op jit(solution)/shard_map/ppermute | solution.py:565
  75.0 9.7 %collective-permute-start.5 = (f32[8,2176]{1,0:T(8,128)S(1)}, f32[8,2176]{1,0:T(8,128)S(1)}, u32[]{:S(2)}, u32[]{:S(2)}) collective-permute-start(f32[8,2176]{1,0:T(8,128)S(1)} %get-tuple-element.42), channel_id=1, source_target_pairs={{0,6},{2,4},{4,2},{6,0},{8,14},{10,12},{12,10},{14,8},{1,7},{3,5},... | collective-permute-start | bytes 208904 | tf_op jit(solution)/shard_map/ppermute | solution.py:565
  77.0 9.0 %collective-permute-start.6 = (f32[8,2176]{1,0:T(8,128)S(1)}, f32[8,2176]{1,0:T(8,128)S(1)}, u32[]{:S(2)}, u32[]{:S(2)}) collective-permute-start(f32[8,2176]{1,0:T(8,128)S(1)} %get-tuple-element.43), channel_id=1, source_target_pairs={{0,8},{2,10},{4,12},{6,14},{8,0},{10,2},{12,4},{14,6},{1,9},{3,11}... | collective-permute-start | bytes 208904 | tf_op jit(solution)/shard_map/ppermute | solution.py:565
  77.8 12.4 %collective-permute-start.7 = (f32[8,2176]{1,0:T(8,128)S(1)}, f32[8,2176]{1,0:T(8,128)S(1)}, u32[]{:S(2)}, u32[]{:S(2)}) collective-permute-start(f32[8,2176]{1,0:T(8,128)S(1)} %get-tuple-element.44), channel_id=1, source_target_pairs={{0,10},{2,8},{4,14},{6,12},{8,2},{10,0},{12,6},{14,4},{1,11},{3,9}... | collective-permute-start | bytes 208904 | tf_op jit(solution)/shard_map/ppermute | solution.py:565
  80.8 9.3 %collective-permute-start.8 = (f32[8,2176]{1,0:T(8,128)S(1)}, f32[8,2176]{1,0:T(8,128)S(1)}, u32[]{:S(2)}, u32[]{:S(2)}) collective-permute-start(f32[8,2176]{1,0:T(8,128)S(1)} %get-tuple-element.45), channel_id=1, source_target_pairs={{0,12},{2,14},{4,8},{6,10},{8,4},{10,6},{12,0},{14,2},{1,13},{3,15... | collective-permute-start | bytes 208904 | tf_op jit(solution)/shard_map/ppermute | solution.py:565
  82.3 7.9 %collective-permute-start.9 = (f32[8,2176]{1,0:T(8,128)S(1)}, f32[8,2176]{1,0:T(8,128)S(1)}, u32[]{:S(2)}, u32[]{:S(2)}) collective-permute-start(f32[8,2176]{1,0:T(8,128)S(1)} %get-tuple-element.46), channel_id=1, source_target_pairs={{0,14},{2,12},{4,10},{6,8},{8,6},{10,4},{12,2},{14,0},{1,15},{3,13... | collective-permute-start | bytes 208904 | tf_op jit(solution)/shard_map/ppermute | solution.py:565
  90.2 7.5 %collective-permute-start.10 = (f32[8,2176]{1,0:T(8,128)S(1)}, f32[8,2176]{1,0:T(8,128)S(1)}, u32[]{:S(2)}, u32[]{:S(2)}) collective-permute-start(f32[8,2176]{1,0:T(8,128)S(1)} %shard_map.100.refs_0_), channel_id=1, source_target_pairs={{0,2},{2,0},{4,6},{6,4},{8,10},{10,8},{12,14},{14,12},{1,3},{3,1},... | collective-permute-start | bytes 208904 | tf_op jit(solution)/shard_map/ppermute | solution.py:565
  91.3 8.4 %collective-permute-start.11 = (f32[8,2176]{1,0:T(8,128)S(1)}, f32[8,2176]{1,0:T(8,128)S(1)}, u32[]{:S(2)}, u32[]{:S(2)}) collective-permute-start(f32[8,2176]{1,0:T(8,128)S(1)} %shard_map.100.refs_0_), channel_id=1, source_target_pairs={{0,4},{2,6},{4,0},{6,2},{8,12},{10,14},{12,8},{14,10},{1,5},{3,7},... | collective-permute-start | bytes 208904 | tf_op jit(solution)/shard_map/ppermute | solution.py:565
  93.9 8.3 %collective-permute-start.12 = (f32[8,2176]{1,0:T(8,128)S(1)}, f32[8,2176]{1,0:T(8,128)S(1)}, u32[]{:S(2)}, u32[]{:S(2)}) collective-permute-start(f32[8,2176]{1,0:T(8,128)S(1)} %shard_map.100.refs_0_), channel_id=1, source_target_pairs={{0,6},{2,4},{4,2},{6,0},{8,14},{10,12},{12,10},{14,8},{1,7},{3,5},... | collective-permute-start | bytes 208904 | tf_op jit(solution)/shard_map/ppermute | solution.py:565
  94.5 10.5 %collective-permute-start.13 = (f32[8,2176]{1,0:T(8,128)S(1)}, f32[8,2176]{1,0:T(8,128)S(1)}, u32[]{:S(2)}, u32[]{:S(2)}) collective-permute-start(f32[8,2176]{1,0:T(8,128)S(1)} %shard_map.100.refs_0_), channel_id=1, source_target_pairs={{0,8},{2,10},{4,12},{6,14},{8,0},{10,2},{12,4},{14,6},{1,9},{3,11}... | collective-permute-start | bytes 208904 | tf_op jit(solution)/shard_map/ppermute | solution.py:565
  96.8 10.6 %collective-permute-start.14 = (f32[8,2176]{1,0:T(8,128)S(1)}, f32[8,2176]{1,0:T(8,128)S(1)}, u32[]{:S(2)}, u32[]{:S(2)}) collective-permute-start(f32[8,2176]{1,0:T(8,128)S(1)} %shard_map.100.refs_0_), channel_id=1, source_target_pairs={{0,10},{2,8},{4,14},{6,12},{8,2},{10,0},{12,6},{14,4},{1,11},{3,9}... | collective-permute-start | bytes 208904 | tf_op jit(solution)/shard_map/ppermute | solution.py:565
  97.7 9.7 %collective-permute-start.15 = (f32[8,2176]{1,0:T(8,128)S(1)}, f32[8,2176]{1,0:T(8,128)S(1)}, u32[]{:S(2)}, u32[]{:S(2)}) collective-permute-start(f32[8,2176]{1,0:T(8,128)S(1)} %shard_map.100.refs_0_), channel_id=1, source_target_pairs={{0,12},{2,14},{4,8},{6,10},{8,4},{10,6},{12,0},{14,2},{1,13},{3,15... | collective-permute-start | bytes 208904 | tf_op jit(solution)/shard_map/ppermute | solution.py:565
  99.7 7.7 %collective-permute-start.16 = (f32[8,2176]{1,0:T(8,128)S(1)}, f32[8,2176]{1,0:T(8,128)S(1)}, u32[]{:S(2)}, u32[]{:S(2)}) collective-permute-start(f32[8,2176]{1,0:T(8,128)S(1)} %shard_map.100.refs_0_), channel_id=1, source_target_pairs={{0,14},{2,12},{4,10},{6,8},{8,6},{10,4},{12,2},{14,0},{1,15},{3,13... | collective-permute-start | bytes 208904 | tf_op jit(solution)/shard_map/ppermute | solution.py:565
  107.4 25.4 %collective-permute-start.17 = (f32[2,4,48,256]{3,2,1,0:T(8,128)S(1)}, f32[2,4,48,256]{3,2,1,0:T(8,128)S(1)}, u32[]{:S(2)}, u32[]{:S(2)}) collective-permute-start(f32[2,4,48,256]{3,2,1,0:T(8,128)S(1)} %get-tuple-element.57), channel_id=1, source_target_pairs={{0,2},{2,4},{4,6},{6,8},{8,10},{10,12},{12,14},{1,3},{3,5},{5,7},{... | collective-permute-start | bytes 1179656 | tf_op jit(solution)/shard_map/ppermute | solution.py:603
  110.6 22.2 %collective-permute-start.18 = (f32[2,4,48,256]{3,2,1,0:T(8,128)S(1)}, f32[2,4,48,256]{3,2,1,0:T(8,128)S(1)}, u32[]{:S(2)}, u32[]{:S(2)}) collective-permute-start(f32[2,4,48,256]{3,2,1,0:T(8,128)S(1)} %get-tuple-element.58), channel_id=1, source_target_pairs={{2,0},{4,2},{6,4},{8,6},{10,8},{12,10},{14,12},{3,1},{5,3},{7,5},{... | collective-permute-start | bytes 1179656 | tf_op jit(solution)/shard_map/ppermute | solution.py:603
  132.8 1.4 collective-permute-start.19
  136.8 18.3 %all-to-all-start.1 = ((f32[8,2,8,512]{3,2,1,0:T(8,128)}), f32[8,2,8,512]{3,2,1,0:T(8,128)S(1)}, u32[]{:S(2)}, u32[]{:S(2)}) async-start(f32[8,2,8,512]{3,2,1,0:T(8,128)} %get-tuple-element.64), calls=%async_computation.1 | async-start | bytes 524288 | tf_op jit(solution)/shard_map/all_to_all | solution.py:610

commit v3 on v2

--- a/solution.py
+++ b/solution.py
@@ -39,33 +39,58 @@
     return high, middle, low
 
 
+def stacked(parts):
+    return jnp.concatenate(parts, axis=0)
+
+
+def apply3(left, right):
+    rows = left[0].shape[0]
+    first = jnp.dot(stacked(left), right[0], preferred_element_type=f32)
+    second = jnp.dot(stacked(left[:2]), right[1], preferred_element_type=f32)
+    third = jnp.dot(left[0], right[2], preferred_element_type=f32)
+    small = first[2 * rows :] + second[rows:] + third
+    return first[:rows] + (first[rows : 2 * rows] + second[:rows] + small)
+
+
+def square3(parts):
+    rows = parts[0].shape[0]
+    whole = stacked(parts)
+    every = lax.dot_general(whole, whole, (((1,), (1,)), ((), ())), preferred_element_type=f32)
+
+    def piece(i, j):
+        return every[i * rows : (i + 1) * rows, j * rows : (j + 1) * rows]
+
+    return piece(0, 0) + (piece(0, 1) + piece(1, 0) + (piece(0, 2) + piece(2, 0) + piece(1, 1)))
+
+
 def edges_kernel(idx_ref, half_ref, side_ref):
-    fb, planes, rows = half_ref.shape[1:4]
+    mb, fb, planes, rows = half_ref.shape[:4]
     lane = lax.broadcasted_iota(jnp.int32, (rows, 128), 1)
     offset = jnp.where(idx_ref[1] == 0, 1, 0)
-    for f in range(fb):
-        side = jnp.zeros((rows, 128), f32)
-        for z in range(planes):
-            turned = pltpu.roll(half_ref[0, f, z], z + offset, 1)
-            side = jnp.where(lane == z, turned, side)
-        side_ref[0, f] = side
-
-
-def edges(idx, fields, planes, fb):
+    for m in range(mb):
+        for f in range(fb):
+            side = jnp.zeros((rows, 128), f32)
+            for z in range(planes):
+                turned = pltpu.roll(half_ref[m, f, z], z + offset, 1)
+                side = jnp.where(lane == z, turned, side)
+            side_ref[m, f] = side
+
+
+def edges(idx, fields, planes, mb, fb):
     m, f, _, rows, cols = fields.shape
     tail = cols // 128 - 1
     return pl.pallas_call(
         edges_kernel,
         grid_spec=pltpu.PrefetchScalarGridSpec(
             num_scalar_prefetch=1,
-            grid=(m, f // fb),
+            grid=(m // mb, f // fb),
             in_specs=[
                 pl.BlockSpec(
-                    (1, fb, planes, rows, 128),
+                    (mb, fb, planes, rows, 128),
                     lambda i, j, s: (i, j, 0, 0, jnp.where(s[1] == 0, tail, 0)),
                 ),
             ],
-            out_specs=pl.BlockSpec((1, fb, rows, 128), lambda i, j, s: (i, j, 0, 0)),
+            out_specs=pl.BlockSpec((mb, fb, rows, 128), lambda i, j, s: (i, j, 0, 0)),
         ),
         out_shape=jax.ShapeDtypeStruct((m, f, rows, 128), f32),
         compiler_params=params_of(32),
@@ -296,35 +321,38 @@
 
 
 def mend_kernel(coef_ref, value_ref, before_ref, after_ref, out_ref):
-    m, f, end = pl.program_id(0), pl.program_id(1), pl.program_id(2)
-    a = coef_ref[m, f, 0]
-    planes = out_ref.shape[2]
+    m, end = pl.program_id(0), pl.program_id(1)
+    nf, planes = out_ref.shape[1:3]
     out_ref[...] = value_ref[...]
 
     @pl.when(end == 0)
     def _():
-        for z in range(planes):
-            out_ref[0, 0, z, 0:1, :] = value_ref[0, 0, z, 0:1, :] + a * before_ref[0, 0, z : z + 1, :]
+        for f in range(nf):
+            a = coef_ref[m, f, 0]
+            for z in range(planes):
+                out_ref[0, f, z, 0:1, :] = value_ref[0, f, z, 0:1, :] + a * before_ref[0, f, z : z + 1, :]
 
     @pl.when(end == 1)
     def _():
-        for z in range(planes):
-            out_ref[0, 0, z, 7:8, :] = value_ref[0, 0, z, 7:8, :] + a * after_ref[0, 0, z : z + 1, :]
+        for f in range(nf):
+            a = coef_ref[m, f, 0]
+            for z in range(planes):
+                out_ref[0, f, z, 7:8, :] = value_ref[0, f, z, 7:8, :] + a * after_ref[0, f, z : z + 1, :]
 
 
 def mend(coefs, value, before, after):
     m, f, nz, rows, cols = value.shape
     last = rows // 8 - 1
-    block = pl.BlockSpec((1, 1, nz, 8, cols), lambda i, j, e: (i, j, 0, e * last, 0))
-    halo = pl.BlockSpec((1, 1, nz, cols), lambda i, j, e: (i, j, 0, 0))
+    block = pl.BlockSpec((1, f, nz, 8, cols), lambda i, e: (i, 0, 0, e * last, 0))
+    halo = pl.BlockSpec((1, f, nz, cols), lambda i, e: (i, 0, 0, 0))
     return pl.pallas_call(
         mend_kernel,
-        grid=(m, f, 2),
+        grid=(m, 2),
         in_specs=[smem(), block, halo, halo],
         out_specs=block,
         out_shape=jax.ShapeDtypeStruct(value.shape, f32),
         input_output_aliases={1: 0},
-        compiler_params=params_of(16),
+        compiler_params=params_of(32),
         cost_estimate=pl.CostEstimate(
             flops=m * f * nz * 4 * cols, bytes_accessed=m * f * nz * 32 * cols * 4, transcendentals=0
         ),
@@ -435,22 +463,50 @@
 
 def inverse_factor(cov):
     size = cov.shape[0]
+    shape = (8, 2 * size)
     r = lax.broadcasted_iota(jnp.int32, (size, size), 0)
     c = lax.broadcasted_iota(jnp.int32, (size, size), 1)
     both = jnp.concatenate([cov, (r == c).astype(f32)], axis=1)
     groups = [both[g : g + 8, :] for g in range(0, size, 8)]
-    sub = lax.broadcasted_iota(jnp.int32, (8, 2 * size), 0)
-    for j in range(size):
-        g, i = divmod(j, 8)
-        pivot_row = groups[g][i : i + 1, :]
-        scale = lax.rsqrt(pivot_row[:, j : j + 1])
-        scaled = pivot_row * scale
-        for h in range(g, size // 8):
-            column = groups[h][:, j : j + 1] * scale
-            update = groups[h] - column * scaled
-            if h == g:
-                update = jnp.where(sub > i, update, jnp.where(sub == i, scaled, groups[h]))
-            groups[h] = update
+    sub = lax.broadcasted_iota(jnp.int32, shape, 0)
+
+    def column(value, at):
+        return jnp.broadcast_to(value[:, at : at + 1], shape)
+
+    def row(value, at):
+        return jnp.broadcast_to(value[at : at + 1, :], shape)
+
+    for g in range(size // 8):
+        block = groups[g]
+        columns = [column(block, 8 * g + q) for q in range(8)]
+        entry = [[row(columns[q], i) for q in range(i + 1)] for i in range(8)]
+        scale = []
+        for q in range(8):
+            scale.append(lax.rsqrt(entry[q][q]))
+            for i in range(q + 1, 8):
+                entry[i][q] = entry[i][q] * scale[q]
+            for i in range(q + 1, 8):
+                for p in range(q + 1, i + 1):
+                    entry[i][p] = entry[i][p] - entry[i][q] * entry[p][q]
+
+        def solved(raw):
+            done = []
+            for i in range(8):
+                value = raw[i]
+                for q in range(i):
+                    value = value - entry[i][q] * done[q]
+                done.append(value * scale[i])
+            return done
+
+        rows = solved([row(block, i) for i in range(8)])
+        for h in range(g + 1, size // 8):
+            below = solved([column(groups[h], 8 * g + q) for q in range(8)])
+            for q in range(8):
+                groups[h] = groups[h] - below[q] * rows[q]
+        final = rows[0]
+        for i in range(1, 8):
+            final = jnp.where(sub == i, rows[i], final)
+        groups[g] = final
     return jnp.concatenate([v[:, size:] for v in groups], axis=0)
 
 
@@ -474,18 +530,15 @@
     turned = packed.T
     first = jnp.where(r <= c, packed, turned)
     second = jnp.where(r > c, packed, jnp.where(r < c, turned, diagonal))
-    dot = functools.partial(jnp.dot, precision=highest, preferred_element_type=f32)
-    across = functools.partial(
-        lax.dot_general,
-        dimension_numbers=(((1,), (1,)), ((), ())),
-        precision=highest,
-        preferred_element_type=f32,
+    matrix = split3(
+        jnp.concatenate(
+            [jnp.concatenate([first, cross], axis=1), jnp.concatenate([cross.T, second], axis=1)], axis=0
+        )
     )
     basis = start_ref[core]
     for _ in range(ITERS):
-        a, b = basis[:, :half], basis[:, half:]
-        image = jnp.concatenate([dot(a, first) + across(b, cross), dot(a, cross) + dot(b, second)], axis=1)
-        basis = dot(inverse_factor(across(image, image)), image)
+        image = split3(apply3(split3(basis), matrix))
+        basis = apply3(split3(inverse_factor(square3(image))), image)
     out_ref[...] = basis
 
 
@@ -509,7 +562,7 @@
     basis_ref[core] = own_ref[...]
     basis_ref[1 - core] = got_ref[...]
     for m in range(fibre.shape[0]):
-        value = jnp.dot(basis_ref[m], fibre[m], precision=highest, preferred_element_type=f32)
+        value = apply3(split3(basis_ref[m]), split3(fibre[m]))
         for d in range(n):
             out_ref[d, m] = value[d * share : (d + 1) * share, :]
 
@@ -590,9 +643,9 @@
     ppd, yb, _ = slab_pieces(n, fields)
     up = [(i, i + 1) for i in range(n - 1)]
     down = [(j, i) for i, j in up]
-    slab_side = swap_cores(edges(idx, fields, ZS, nf))
+    slab_side = swap_cores(edges(idx, fields, ZS, members, nf))
     pieces = lax.all_to_all(slab_step(idx, coefs, fields, slab_side, seeds, n), "gx", 0, 0)
-    side = swap_cores(edges(idx, fields, fields.shape[2], 2))
+    side = swap_cores(edges(idx, fields, fields.shape[2], 1, 2))
     value, top, bottom = bulk(idx, coefs, fields, side, seeds)
     pieces, value = lax.optimization_barrier((pieces, value))
     own, other, fibre = gram(idx, coefs, pieces, members, ppd, fields.shape[4] // yb)
@@ -603,8 +656,8 @@
     before, after = lax.ppermute(bottom, "gx", up), lax.ppermute(top, "gx", down)
     start = jnp.swapaxes(start_basis, 1, 2)
     basis = iterate(idx, start, grams)
-    basis, before, after = lax.optimization_barrier((basis, before, after))
     bases, rows = project(idx, basis, swap_cores(basis), fibre, n)
+    rows, before, after = lax.optimization_barrier((rows, before, after))
     fields_next = mend(coefs, value, before, after)
     share = start_basis.shape[2] // n
     core = gather(lax.all_to_all(rows, "gx", 0, 0), (members, share, nf, ZS, fields.shape[4]), ppd, yb)

time: 157 us -> 142 us (0.904)
  Pallas kernels: 85.7 us -> 69.3 us
    pallas_call x1, Pallas kernels: 20.7 us -> 9.87 us  [iterate(): pl.pallas_call(functools.partial(iterate_kernel, n), in_specs=[smem()] +...]
    pallas_call x1, Pallas kernels: 11.4 us -> 6.24 us  [mend(): pl.pallas_call(mend_kernel, grid=(m, 2), in_specs=[smem(), block, halo, h...]
    all_to_all x1, waiting for transfers between devices: 0.01 us -> 2.99 us  [per_device(): lax.all_to_all(rows, 'gx', 0, 0)]
    ppermute x14, waiting for transfers between devices: 10.8 us -> 8.77 us  [exchange(): lax.ppermute(pieces[k], 'gx', [(i, i ^ k) for i in range(n)])]
  transfers between devices with their start and end apart: 22 -> 22, of which waited for: 9 -> 11; matrix products, arithmetic and copies ran while one was open for 0% -> 1% of each run, Pallas kernels for 45% -> 40%
where the time goes in v3:
time: 142 us; the launch traced here: 141 us
  Pallas kernels  69.3 us (49%)
  starting transfers between devices  42.9 us (30%)
  waiting for transfers between devices  26.9 us (19%)
    pallas_call x1, Pallas kernels, bulk(): pl.pallas_call(bulk_kernel, grid_spec=pltpu.PrefetchScalarGridSpec(num_sc...  30.9 us
    ppermute x14, starting transfers between devices, exchange(): lax.ppermute(pieces[k], 'gx', [(i, i ^ k) for i in range(n)])  24.5 us
    all_to_all x1, waiting for transfers between devices, per_device(): lax.all_to_all(slab_step(idx, coefs, fields, slab_side, seeds, n), 'gx',...  9.97 us
    pallas_call x1, Pallas kernels, iterate(): pl.pallas_call(functools.partial(iterate_kernel, n), in_specs=[smem()] +...  9.87 us
    pallas_call x2, Pallas kernels, edges(): pl.pallas_call(edges_kernel, grid_spec=pltpu.PrefetchScalarGridSpec(num_s...  9.59 us
    ppermute x14, waiting for transfers between devices, exchange(): lax.ppermute(pieces[k], 'gx', [(i, i ^ k) for i in range(n)])  8.77 us
    all_to_all x1, starting transfers between devices, per_device(): lax.all_to_all(slab_step(idx, coefs, fields, slab_side, seeds, n), 'gx',...  7.2 us
    pallas_call x1, Pallas kernels, mend(): pl.pallas_call(mend_kernel, grid=(m, 2), in_specs=[smem(), block, halo, h...  6.24 us
  transfers between devices with their start and end apart: 22, of which 11 were waited for; matrix products, arithmetic and copies ran while one was open for 1% of the time, Pallas kernels for 40%

profile of v3, /device:TPU:0, one launch (start us, length us, event | category | flops | bytes accessed | tf_op | source)
XLA Modules:
  0.0 140.8 jit_solution(14512921478609219415)
XLA Ops:
  0.6 0.0 copy-start
  0.7 0.1 pad_add_fusion.idx_ref
  0.8 2.1 %shard_map.94 = f32[2,4,64,128]{3,2,1,0:T(8,128)S(1)} custom-call(s32[2]{0:T(128)S(1)} %pad_add_fusion.idx_ref, f32[2,4,48,64,256]{4,3,2,1,0:T(8,128)} %refs_2_.3), custom_call_target="tpu_custom_call" | custom-call | flops 524288 | bytes 1048576 | tf_op jit(solution)/shard_map/pallas_call | solution.py:82
  2.9 0.5 collective-permute-start
  3.4 0.2 fusion
  3.7 0.1 fusion.5
  3.8 0.0 copy-done.2
  3.8 0.1 tile.29
  3.9 0.1 tile.25
  4.0 0.1 tile.30.refs_5_
  4.1 0.1 stack.8.coef_ref
  4.2 0.4 collective-permute-done.refs_3_
  4.6 5.6 %shard_map.95 = f32[8,264,256]{2,1,0:T(8,128)} custom-call(s32[2]{0:T(128)S(1)} %pad_add_fusion.idx_ref, f32[2,4,5]{2,1,0:T(4,128)S(1)} %stack.8.coef_ref, f32[2,4,48,64,256]{4,3,2,1,0:T(8,128)} %refs_2_.3, f32[2,4,48,64,256]{4,3,2,1,0:T(8,128)} %refs_2_.3, f32[2,4,48,64,256]{4,3,2,1,0:T(8,128)} %refs_2_.3, ...), custom_call_target="tpu_custom_call" | custom-call | flops 15728640 | bytes 5242880 | tf_op jit(solution)/shard_map/pallas_call | solution.py:305
  10.2 7.2 %all-to-all-start = ((f32[8,264,256]{2,1,0:T(8,128)}), f32[8,264,256]{2,1,0:T(8,128)S(1)}, u32[]{:S(2)}, u32[]{:S(2)}) async-start(f32[8,264,256]{2,1,0:T(8,128)} %shard_map.95), calls=%async_computation | async-start | bytes 4325376 | tf_op jit(solution)/shard_map/all_to_all | solution.py:647
  17.4 7.5 %shard_map.96 = f32[2,4,64,128]{3,2,1,0:T(8,128)S(1)} custom-call(s32[2]{0:T(128)S(1)} %pad_add_fusion.idx_ref, f32[2,4,48,64,256]{4,3,2,1,0:T(8,128)} %refs_2_.3), custom_call_target="tpu_custom_call" | custom-call | flops 6291456 | bytes 12582912 | tf_op jit(solution)/shard_map/pallas_call | solution.py:82
  24.8 0.0 copy-start.1
  24.8 0.1 collective-permute-start.1
  24.9 1.5 %collective-permute-done.1.refs_3_ = f32[2,4,64,128]{3,2,1,0:T(8,128)S(1)} collective-permute-done((f32[2,4,64,128]{3,2,1,0:T(8,128)S(1)}, f32[2,4,64,128]{3,2,1,0:T(8,128)S(1)}, u32[]{:S(2)}, u32[]{:S(2)}) %collective-permute-start.1) | collective-permute-done | bytes 262176 | tf_op jit(solution)/shard_map/ppermute | solution.py:623
  26.4 30.9 %shard_map.97 = (f32[2,4,48,64,256]{4,3,2,1,0:T(8,128)}, f32[2,4,48,256]{3,2,1,0:T(8,128)S(1)}, f32[2,4,48,256]{3,2,1,0:T(8,128)S(1)}) custom-call(s32[2]{0:T(128)S(1)} %pad_add_fusion.idx_ref, f32[2,4,5]{2,1,0:T(4,128)S(1)} %stack.8.coef_ref, f32[2,4,48,64,256]{4,3,2,1,0:T(8,128)} %refs_2_.3, f32[2,4,48,64,256]{4,3,2,1,0:T(8,128)} %refs_2_.3, ...), custom_call_target="tpu_custom_call" | custom-call | flops 188743680 | bytes 62914560 | tf_op jit(solution)/shard_map/pallas_call | solution.py:240
  57.3 10.0 %all-to-all-done.refs_0_ = f32[8,264,256]{2,1,0:T(8,128)S(1)} async-done(((f32[8,264,256]{2,1,0:T(8,128)}), f32[8,264,256]{2,1,0:T(8,128)S(1)}, u32[]{:S(2)}, u32[]{:S(2)}) %all-to-all-start) | async-done | bytes 2162720 | tf_op jit(solution)/shard_map/all_to_all | solution.py:647
  67.3 3.6 %shard_map.98 = (f32[8,8,2176]{2,1,0:T(8,128)S(1)}, f32[8,8,2176]{2,1,0:T(8,128)S(1)}, f32[2,512,512]{2,1,0:T(8,128)S(1)}) custom-call(s32[2]{0:T(128)S(1)} %pad_add_fusion.idx_ref, f32[2,4,5]{2,1,0:T(4,128)S(1)} %stack.8.coef_ref, f32[8,264,256]{2,1,0:T(8,128)S(1)} %all-to-all-done.refs_0_), custom_call_target="tpu_custom_call" | custom-call | tf_op jit(solution)/shard_map/pallas_call | solution.py:420
  70.9 0.1 collective-permute-start.2
  71.0 1.9 %collective-permute-done.2.got_ref = f32[8,8,2176]{2,1,0:T(8,128)S(1)} collective-permute-done((f32[8,8,2176]{2,1,0:T(8,128)S(1)}, f32[8,8,2176]{2,1,0:T(8,128)S(1)}, u32[]{:S(2)}, u32[]{:S(2)}) %collective-permute-start.2) | collective-permute-done | bytes 557088 | tf_op jit(solution)/shard_map/ppermute | solution.py:623
  72.9 0.6 shard_map.99
  73.5 1.5 %collective-permute-start.3 = (f32[8,2176]{1,0:T(8,128)S(1)}, f32[8,2176]{1,0:T(8,128)S(1)}, u32[]{:S(2)}, u32[]{:S(2)}) collective-permute-start(f32[8,2176]{1,0:T(8,128)S(1)} %get-tuple-element.40), channel_id=1, source_target_pairs={{0,2},{2,0},{4,6},{6,4},{8,10},{10,8},{12,14},{14,12},{1,3},{3,1},... | collective-permute-start | bytes 208904 | tf_op jit(solution)/shard_map/ppermute | solution.py:618
  75.1 0.0 collective-permute-start.4
  75.1 2.0 %collective-permute-start.5 = (f32[8,2176]{1,0:T(8,128)S(1)}, f32[8,2176]{1,0:T(8,128)S(1)}, u32[]{:S(2)}, u32[]{:S(2)}) collective-permute-start(f32[8,2176]{1,0:T(8,128)S(1)} %get-tuple-element.42), channel_id=1, source_target_pairs={{0,6},{2,4},{4,2},{6,0},{8,14},{10,12},{12,10},{14,8},{1,7},{3,5},... | collective-permute-start | bytes 208904 | tf_op jit(solution)/shard_map/ppermute | solution.py:618
  77.1 0.8 collective-permute-start.6
  77.9 3.0 %collective-permute-start.7 = (f32[8,2176]{1,0:T(8,128)S(1)}, f32[8,2176]{1,0:T(8,128)S(1)}, u32[]{:S(2)}, u32[]{:S(2)}) collective-permute-start(f32[8,2176]{1,0:T(8,128)S(1)} %get-tuple-element.44), channel_id=1, source_target_pairs={{0,10},{2,8},{4,14},{6,12},{8,2},{10,0},{12,6},{14,4},{1,11},{3,9}... | collective-permute-start | bytes 208904 | tf_op jit(solution)/shard_map/ppermute | solution.py:618
  80.9 0.0 collective-permute-done.3.refs_1_
  80.9 1.5 %collective-permute-start.8 = (f32[8,2176]{1,0:T(8,128)S(1)}, f32[8,2176]{1,0:T(8,128)S(1)}, u32[]{:S(2)}, u32[]{:S(2)}) collective-permute-start(f32[8,2176]{1,0:T(8,128)S(1)} %get-tuple-element.45), channel_id=1, source_target_pairs={{0,12},{2,14},{4,8},{6,10},{8,4},{10,6},{12,0},{14,2},{1,13},{3,15... | collective-permute-start | bytes 208904 | tf_op jit(solution)/shard_map/ppermute | solution.py:618
  82.4 0.0 collective-permute-done.4.refs_2_
  82.4 2.4 %collective-permute-start.9 = (f32[8,2176]{1,0:T(8,128)S(1)}, f32[8,2176]{1,0:T(8,128)S(1)}, u32[]{:S(2)}, u32[]{:S(2)}) collective-permute-start(f32[8,2176]{1,0:T(8,128)S(1)} %get-tuple-element.46), channel_id=1, source_target_pairs={{0,14},{2,12},{4,10},{6,8},{8,6},{10,4},{12,2},{14,0},{1,15},{3,13... | collective-permute-start | bytes 208904 | tf_op jit(solution)/shard_map/ppermute | solution.py:618
  84.7 0.0 collective-permute-done.5.refs_3_
  84.7 1.4 collective-permute-done.6.refs_4_
  86.1 4.2 %collective-permute-done.7.refs_5_ = f32[8,2176]{1,0:T(8,128)S(1)} collective-permute-done((f32[8,2176]{1,0:T(8,128)S(1)}, f32[8,2176]{1,0:T(8,128)S(1)}, u32[]{:S(2)}, u32[]{:S(2)}) %collective-permute-start.7) | collective-permute-done | bytes 69664 | tf_op jit(solution)/shard_map/ppermute | solution.py:618
  90.3 0.0 collective-permute-done.8.refs_6_
  90.3 0.0 collective-permute-done.9.refs_7_
  90.3 2.5 %collective-permute-start.16 = (f32[8,2176]{1,0:T(8,128)S(1)}, f32[8,2176]{1,0:T(8,128)S(1)}, u32[]{:S(2)}, u32[]{:S(2)}) collective-permute-start(f32[8,2176]{1,0:T(8,128)S(1)} %shard_map.100.refs_0_), channel_id=1, source_target_pairs={{0,14},{2,12},{4,10},{6,8},{8,6},{10,4},{12,2},{14,0},{1,15},{3,13... | collective-permute-start | bytes 208904 | tf_op jit(solution)/shard_map/ppermute | solution.py:618
  92.8 1.9 %collective-permute-start.15 = (f32[8,2176]{1,0:T(8,128)S(1)}, f32[8,2176]{1,0:T(8,128)S(1)}, u32[]{:S(2)}, u32[]{:S(2)}) collective-permute-start(f32[8,2176]{1,0:T(8,128)S(1)} %shard_map.100.refs_0_), channel_id=1, source_target_pairs={{0,12},{2,14},{4,8},{6,10},{8,4},{10,6},{12,0},{14,2},{1,13},{3,15... | collective-permute-start | bytes 208904 | tf_op jit(solution)/shard_map/ppermute | solution.py:618
  94.7 1.6 %collective-permute-start.14 = (f32[8,2176]{1,0:T(8,128)S(1)}, f32[8,2176]{1,0:T(8,128)S(1)}, u32[]{:S(2)}, u32[]{:S(2)}) collective-permute-start(f32[8,2176]{1,0:T(8,128)S(1)} %shard_map.100.refs_0_), channel_id=1, source_target_pairs={{0,10},{2,8},{4,14},{6,12},{8,2},{10,0},{12,6},{14,4},{1,11},{3,9}... | collective-permute-start | bytes 208904 | tf_op jit(solution)/shard_map/ppermute | solution.py:618
  96.3 1.7 %collective-permute-start.13 = (f32[8,2176]{1,0:T(8,128)S(1)}, f32[8,2176]{1,0:T(8,128)S(1)}, u32[]{:S(2)}, u32[]{:S(2)}) collective-permute-start(f32[8,2176]{1,0:T(8,128)S(1)} %shard_map.100.refs_0_), channel_id=1, source_target_pairs={{0,8},{2,10},{4,12},{6,14},{8,0},{10,2},{12,4},{14,6},{1,9},{3,11}... | collective-permute-start | bytes 208904 | tf_op jit(solution)/shard_map/ppermute | solution.py:618
  98.0 1.2 collective-permute-start.12
  99.2 0.0 collective-permute-done.16.refs_7_
  99.2 3.3 %collective-permute-start.11 = (f32[8,2176]{1,0:T(8,128)S(1)}, f32[8,2176]{1,0:T(8,128)S(1)}, u32[]{:S(2)}, u32[]{:S(2)}) collective-permute-start(f32[8,2176]{1,0:T(8,128)S(1)} %shard_map.100.refs_0_), channel_id=1, source_target_pairs={{0,4},{2,6},{4,0},{6,2},{8,12},{10,14},{12,8},{14,10},{1,5},{3,7},... | collective-permute-start | bytes 208904 | tf_op jit(solution)/shard_map/ppermute | solution.py:618
  102.6 0.0 collective-permute-done.15.refs_6_
  102.6 1.1 collective-permute-start.10
  103.6 1.8 %collective-permute-done.14.refs_5_ = f32[8,2176]{1,0:T(8,128)S(1)} collective-permute-done((f32[8,2176]{1,0:T(8,128)S(1)}, f32[8,2176]{1,0:T(8,128)S(1)}, u32[]{:S(2)}, u32[]{:S(2)}) %collective-permute-start.14) | collective-permute-done | bytes 69664 | tf_op jit(solution)/shard_map/ppermute | solution.py:618
  105.5 0.0 collective-permute-done.13.refs_4_
  105.5 0.0 collective-permute-done.12.refs_3_
  105.5 0.7 collective-permute-done.11.refs_2_
  106.2 0.7 collective-permute-done.10.refs_1_
  106.9 3.0 %collective-permute-start.18 = (f32[2,4,48,256]{3,2,1,0:T(8,128)S(1)}, f32[2,4,48,256]{3,2,1,0:T(8,128)S(1)}, u32[]{:S(2)}, u32[]{:S(2)}) collective-permute-start(f32[2,4,48,256]{3,2,1,0:T(8,128)S(1)} %get-tuple-element.59), channel_id=1, source_target_pairs={{0,2},{2,4},{4,6},{6,8},{8,10},{10,12},{12,14},{1,3},{3,5},{5,7},{... | collective-permute-start | bytes 1179656 | tf_op jit(solution)/shard_map/ppermute | solution.py:656
  109.9 1.5 %collective-permute-start.19 = (f32[2,4,48,256]{3,2,1,0:T(8,128)S(1)}, f32[2,4,48,256]{3,2,1,0:T(8,128)S(1)}, u32[]{:S(2)}, u32[]{:S(2)}) collective-permute-start(f32[2,4,48,256]{3,2,1,0:T(8,128)S(1)} %get-tuple-element.60), channel_id=1, source_target_pairs={{2,0},{4,2},{6,4},{8,6},{10,8},{12,10},{14,12},{3,1},{5,3},{7,5},{... | collective-permute-start | bytes 1179656 | tf_op jit(solution)/shard_map/ppermute | solution.py:656
  111.4 9.9 %shard_map.101.own_ref = f32[64,512]{1,0:T(8,128)S(1)} custom-call(s32[2]{0:T(128)S(1)} %pad_add_fusion.idx_ref, f32[2,64,512]{2,1,0:T(8,128)S(1)} %bitcast.12, f32[8,2176]{1,0:T(8,128)S(1)} %shard_map.100.refs_0_, f32[8,2176]{1,0:T(8,128)S(1)} %collective-permute-done.10.refs_1_, f32[8,2176]{1,0:T(8,128)S(1)} %collective-permute-done.11.refs_2_, ...), custom_call_target="tpu_custom_call" | custom-call | tf_op jit(solution)/shard_map/pallas_call | solution.py:549
  121.2 0.1 collective-permute-start.17
  121.3 1.3 collective-permute-done.17.got_ref
  122.7 2.0 %shard_map.102 = (f32[2,64,512]{2,1,0:T(8,128)}, f32[8,2,8,512]{3,2,1,0:T(8,128)}) custom-call(s32[2]{0:T(128)S(1)} %pad_add_fusion.idx_ref, f32[64,512]{1,0:T(8,128)S(1)} %shard_map.101.own_ref, f32[64,512]{1,0:T(8,128)S(1)} %collective-permute-done.17.got_ref, f32[2,512,512]{2,1,0:T(8,128)S(1)} %get-tuple-element.57.fibre), custom_call_target="tpu_custom_call" | custom-call | tf_op jit(solution)/shard_map/pallas_call | solution.py:573
  124.7 0.0 collective-permute-done.18.before_ref
  124.7 0.0 collective-permute-done.19.after_ref
  124.7 6.0 %all-to-all-start.1 = ((f32[8,2,8,512]{3,2,1,0:T(8,128)}), f32[8,2,8,512]{3,2,1,0:T(8,128)S(1)}, u32[]{:S(2)}, u32[]{:S(2)}) async-start(f32[8,2,8,512]{3,2,1,0:T(8,128)} %get-tuple-element.64), calls=%async_computation.1 | async-start | bytes 524288 | tf_op jit(solution)/shard_map/all_to_all | solution.py:663
  130.7 6.2 %shard_map.103 = f32[2,4,48,64,256]{4,3,2,1,0:T(8,128)} custom-call(f32[2,4,5]{2,1,0:T(4,128)S(1)} %stack.8.coef_ref, f32[2,4,48,64,256]{4,3,2,1,0:T(8,128)} %get-tuple-element.35.value_ref, f32[2,4,48,256]{3,2,1,0:T(8,128)S(1)} %collective-permute-done.18.before_ref, ...), custom_call_target="tpu_custom_call", output_to_operand_aliasing={{}: (1, {})} | custom-call | flops 393216 | bytes 12582912 | tf_op jit(solution)/shard_map/pallas_call | solution.py:348
  137.0 3.0 %all-to-all-done.1.held = f32[8,2,8,512]{3,2,1,0:T(8,128)S(1)} async-done(((f32[8,2,8,512]{3,2,1,0:T(8,128)}), f32[8,2,8,512]{3,2,1,0:T(8,128)S(1)}, u32[]{:S(2)}, u32[]{:S(2)}) %all-to-all-start.1) | async-done | bytes 262176 | tf_op jit(solution)/shard_map/all_to_all | solution.py:663
  140.0 0.8 shard_map.104
  (18 shorter events, 0.1 us)
Async XLA Ops:
  0.6 2.8 %copy-start = (f32[8,4,4]{0,2,1:T(4,128)S(1)}, f32[8,4,4]{0,2,1:T(4,128)}, u32[]{:S(2)}) copy-start(f32[8,4,4]{0,2,1:T(4,128)} %param.9) | copy-start | bytes 1540
  0.6 2.8 %copy-start.5 = (s32[2]{0:T(128)S(1)}, s32[2]{0:T(128)}, u32[]{:S(2)}) copy-start(s32[2]{0:T(128)} %param.8) | copy-start | bytes 28
  0.7 3.1 %copy-start.2 = (s32[2,16]{1,0:T(2,128)S(1)}, s32[2,16]{1,0:T(2,128)}, u32[]{:S(2)}) copy-start(s32[2,16]{1,0:T(2,128)} %param.10) | copy-start | bytes 388
  0.7 3.1 %copy-start.3 = (s32[2,16]{1,0:T(2,128)S(1)}, s32[2,16]{1,0:T(2,128)}, u32[]{:S(2)}) copy-start(s32[2,16]{1,0:T(2,128)} %param.11) | copy-start | bytes 388
  0.7 3.1 %copy-start.4 = (s32[2,16]{1,0:T(2,128)S(1)}, s32[2,16]{1,0:T(2,128)}, u32[]{:S(2)}) copy-start(s32[2,16]{1,0:T(2,128)} %param.12) | copy-start | bytes 388
  2.9 1.7 %collective-permute-start = (f32[2,4,64,128]{3,2,1,0:T(8,128)S(1)}, f32[2,4,64,128]{3,2,1,0:T(8,128)S(1)}, u32[]{:S(2)}, u32[]{:S(2)}) collective-permute-start(f32[2,4,64,128]{3,2,1,0:T(8,128)S(1)} %shard_map.94), channel_id=1, source_target_pairs={{0,1},{1,0},{2,3},{3,2},{4,5},{5,4},{6,7},{7,6},{8,9},{9,8},{10,11... | collective-permute-start | bytes 786440 | tf_op jit(solution)/shard_map/ppermute | solution.py:623
  10.2 57.1 %all-to-all-start = ((f32[8,264,256]{2,1,0:T(8,128)}), f32[8,264,256]{2,1,0:T(8,128)S(1)}, u32[]{:S(2)}, u32[]{:S(2)}) async-start(f32[8,264,256]{2,1,0:T(8,128)} %shard_map.95), calls=%async_computation | async-start | bytes 4325376 | tf_op jit(solution)/shard_map/all_to_all | solution.py:647
  24.8 86.5 %copy-start.1 = (f32[2,512,64]{1,2,0:T(8,128)S(1)}, f32[2,512,64]{1,2,0:T(8,128)}, u32[]{:S(2)}) copy-start(f32[2,512,64]{1,2,0:T(8,128)} %param.13) | copy-start | bytes 786436
  24.8 1.6 %collective-permute-start.1 = (f32[2,4,64,128]{3,2,1,0:T(8,128)S(1)}, f32[2,4,64,128]{3,2,1,0:T(8,128)S(1)}, u32[]{:S(2)}, u32[]{:S(2)}) collective-permute-start(f32[2,4,64,128]{3,2,1,0:T(8,128)S(1)} %shard_map.96), channel_id=1, source_target_pairs={{0,1},{1,0},{2,3},{3,2},{4,5},{5,4},{6,7},{7,6},{8,9},{9,8},{10,11... | collective-permute-start | bytes 786440 | tf_op jit(solution)/shard_map/ppermute | solution.py:623
  70.9 2.0 %collective-permute-start.2 = (f32[8,8,2176]{2,1,0:T(8,128)S(1)}, f32[8,8,2176]{2,1,0:T(8,128)S(1)}, u32[]{:S(2)}, u32[]{:S(2)}) collective-permute-start(f32[8,8,2176]{2,1,0:T(8,128)S(1)} %get-tuple-element.38), channel_id=1, source_target_pairs={{0,1},{1,0},{2,3},{3,2},{4,5},{5,4},{6,7},{7,6},{8,9},{9,8},{10,11... | collective-permute-start | bytes 1671176 | tf_op jit(solution)/shard_map/ppermute | solution.py:623
  73.5 7.4 %collective-permute-start.3 = (f32[8,2176]{1,0:T(8,128)S(1)}, f32[8,2176]{1,0:T(8,128)S(1)}, u32[]{:S(2)}, u32[]{:S(2)}) collective-permute-start(f32[8,2176]{1,0:T(8,128)S(1)} %get-tuple-element.40), channel_id=1, source_target_pairs={{0,2},{2,0},{4,6},{6,4},{8,10},{10,8},{12,14},{14,12},{1,3},{3,1},... | collective-permute-start | bytes 208904 | tf_op jit(solution)/shard_map/ppermute | solution.py:618
  75.1 7.3 %collective-permute-start.4 = (f32[8,2176]{1,0:T(8,128)S(1)}, f32[8,2176]{1,0:T(8,128)S(1)}, u32[]{:S(2)}, u32[]{:S(2)}) collective-permute-start(f32[8,2176]{1,0:T(8,128)S(1)} %get-tuple-element.41), channel_id=1, source_target_pairs={{0,4},{2,6},{4,0},{6,2},{8,12},{10,14},{12,8},{14,10},{1,5},{3,7},... | collective-permute-start | bytes 208904 | tf_op jit(solution)/shard_map/ppermute | solution.py:618
  75.1 9.7 %collective-permute-start.5 = (f32[8,2176]{1,0:T(8,128)S(1)}, f32[8,2176]{1,0:T(8,128)S(1)}, u32[]{:S(2)}, u32[]{:S(2)}) collective-permute-start(f32[8,2176]{1,0:T(8,128)S(1)} %get-tuple-element.42), channel_id=1, source_target_pairs={{0,6},{2,4},{4,2},{6,0},{8,14},{10,12},{12,10},{14,8},{1,7},{3,5},... | collective-permute-start | bytes 208904 | tf_op jit(solution)/shard_map/ppermute | solution.py:618
  77.1 9.0 %collective-permute-start.6 = (f32[8,2176]{1,0:T(8,128)S(1)}, f32[8,2176]{1,0:T(8,128)S(1)}, u32[]{:S(2)}, u32[]{:S(2)}) collective-permute-start(f32[8,2176]{1,0:T(8,128)S(1)} %get-tuple-element.43), channel_id=1, source_target_pairs={{0,8},{2,10},{4,12},{6,14},{8,0},{10,2},{12,4},{14,6},{1,9},{3,11}... | collective-permute-start | bytes 208904 | tf_op jit(solution)/shard_map/ppermute | solution.py:618
  77.9 12.4 %collective-permute-start.7 = (f32[8,2176]{1,0:T(8,128)S(1)}, f32[8,2176]{1,0:T(8,128)S(1)}, u32[]{:S(2)}, u32[]{:S(2)}) collective-permute-start(f32[8,2176]{1,0:T(8,128)S(1)} %get-tuple-element.44), channel_id=1, source_target_pairs={{0,10},{2,8},{4,14},{6,12},{8,2},{10,0},{12,6},{14,4},{1,11},{3,9}... | collective-permute-start | bytes 208904 | tf_op jit(solution)/shard_map/ppermute | solution.py:618
  80.9 9.3 %collective-permute-start.8 = (f32[8,2176]{1,0:T(8,128)S(1)}, f32[8,2176]{1,0:T(8,128)S(1)}, u32[]{:S(2)}, u32[]{:S(2)}) collective-permute-start(f32[8,2176]{1,0:T(8,128)S(1)} %get-tuple-element.45), channel_id=1, source_target_pairs={{0,12},{2,14},{4,8},{6,10},{8,4},{10,6},{12,0},{14,2},{1,13},{3,15... | collective-permute-start | bytes 208904 | tf_op jit(solution)/shard_map/ppermute | solution.py:618
  82.4 7.9 %collective-permute-start.9 = (f32[8,2176]{1,0:T(8,128)S(1)}, f32[8,2176]{1,0:T(8,128)S(1)}, u32[]{:S(2)}, u32[]{:S(2)}) collective-permute-start(f32[8,2176]{1,0:T(8,128)S(1)} %get-tuple-element.46), channel_id=1, source_target_pairs={{0,14},{2,12},{4,10},{6,8},{8,6},{10,4},{12,2},{14,0},{1,15},{3,13... | collective-permute-start | bytes 208904 | tf_op jit(solution)/shard_map/ppermute | solution.py:618
  90.3 8.9 %collective-permute-start.16 = (f32[8,2176]{1,0:T(8,128)S(1)}, f32[8,2176]{1,0:T(8,128)S(1)}, u32[]{:S(2)}, u32[]{:S(2)}) collective-permute-start(f32[8,2176]{1,0:T(8,128)S(1)} %shard_map.100.refs_0_), channel_id=1, source_target_pairs={{0,14},{2,12},{4,10},{6,8},{8,6},{10,4},{12,2},{14,0},{1,15},{3,13... | collective-permute-start | bytes 208904 | tf_op jit(solution)/shard_map/ppermute | solution.py:618
  92.8 9.8 %collective-permute-start.15 = (f32[8,2176]{1,0:T(8,128)S(1)}, f32[8,2176]{1,0:T(8,128)S(1)}, u32[]{:S(2)}, u32[]{:S(2)}) collective-permute-start(f32[8,2176]{1,0:T(8,128)S(1)} %shard_map.100.refs_0_), channel_id=1, source_target_pairs={{0,12},{2,14},{4,8},{6,10},{8,4},{10,6},{12,0},{14,2},{1,13},{3,15... | collective-permute-start | bytes 208904 | tf_op jit(solution)/shard_map/ppermute | solution.py:618
  94.7 10.8 %collective-permute-start.14 = (f32[8,2176]{1,0:T(8,128)S(1)}, f32[8,2176]{1,0:T(8,128)S(1)}, u32[]{:S(2)}, u32[]{:S(2)}) collective-permute-start(f32[8,2176]{1,0:T(8,128)S(1)} %shard_map.100.refs_0_), channel_id=1, source_target_pairs={{0,10},{2,8},{4,14},{6,12},{8,2},{10,0},{12,6},{14,4},{1,11},{3,9}... | collective-permute-start | bytes 208904 | tf_op jit(solution)/shard_map/ppermute | solution.py:618
  96.3 9.2 %collective-permute-start.13 = (f32[8,2176]{1,0:T(8,128)S(1)}, f32[8,2176]{1,0:T(8,128)S(1)}, u32[]{:S(2)}, u32[]{:S(2)}) collective-permute-start(f32[8,2176]{1,0:T(8,128)S(1)} %shard_map.100.refs_0_), channel_id=1, source_target_pairs={{0,8},{2,10},{4,12},{6,14},{8,0},{10,2},{12,4},{14,6},{1,9},{3,11}... | collective-permute-start | bytes 208904 | tf_op jit(solution)/shard_map/ppermute | solution.py:618
  98.0 7.5 %collective-permute-start.12 = (f32[8,2176]{1,0:T(8,128)S(1)}, f32[8,2176]{1,0:T(8,128)S(1)}, u32[]{:S(2)}, u32[]{:S(2)}) collective-permute-start(f32[8,2176]{1,0:T(8,128)S(1)} %shard_map.100.refs_0_), channel_id=1, source_target_pairs={{0,6},{2,4},{4,2},{6,0},{8,14},{10,12},{12,10},{14,8},{1,7},{3,5},... | collective-permute-start | bytes 208904 | tf_op jit(solution)/shard_map/ppermute | solution.py:618
  99.2 6.9 %collective-permute-start.11 = (f32[8,2176]{1,0:T(8,128)S(1)}, f32[8,2176]{1,0:T(8,128)S(1)}, u32[]{:S(2)}, u32[]{:S(2)}) collective-permute-start(f32[8,2176]{1,0:T(8,128)S(1)} %shard_map.100.refs_0_), channel_id=1, source_target_pairs={{0,4},{2,6},{4,0},{6,2},{8,12},{10,14},{12,8},{14,10},{1,5},{3,7},... | collective-permute-start | bytes 208904 | tf_op jit(solution)/shard_map/ppermute | solution.py:618
  102.6 4.3 %collective-permute-start.10 = (f32[8,2176]{1,0:T(8,128)S(1)}, f32[8,2176]{1,0:T(8,128)S(1)}, u32[]{:S(2)}, u32[]{:S(2)}) collective-permute-start(f32[8,2176]{1,0:T(8,128)S(1)} %shard_map.100.refs_0_), channel_id=1, source_target_pairs={{0,2},{2,0},{4,6},{6,4},{8,10},{10,8},{12,14},{14,12},{1,3},{3,1},... | collective-permute-start | bytes 208904 | tf_op jit(solution)/shard_map/ppermute | solution.py:618
  106.9 17.8 %collective-permute-start.18 = (f32[2,4,48,256]{3,2,1,0:T(8,128)S(1)}, f32[2,4,48,256]{3,2,1,0:T(8,128)S(1)}, u32[]{:S(2)}, u32[]{:S(2)}) collective-permute-start(f32[2,4,48,256]{3,2,1,0:T(8,128)S(1)} %get-tuple-element.59), channel_id=1, source_target_pairs={{0,2},{2,4},{4,6},{6,8},{8,10},{10,12},{12,14},{1,3},{3,5},{5,7},{... | collective-permute-start | bytes 1179656 | tf_op jit(solution)/shard_map/ppermute | solution.py:656
  109.9 14.8 %collective-permute-start.19 = (f32[2,4,48,256]{3,2,1,0:T(8,128)S(1)}, f32[2,4,48,256]{3,2,1,0:T(8,128)S(1)}, u32[]{:S(2)}, u32[]{:S(2)}) collective-permute-start(f32[2,4,48,256]{3,2,1,0:T(8,128)S(1)} %get-tuple-element.60), channel_id=1, source_target_pairs={{2,0},{4,2},{6,4},{8,6},{10,8},{12,10},{14,12},{3,1},{5,3},{7,5},{... | collective-permute-start | bytes 1179656 | tf_op jit(solution)/shard_map/ppermute | solution.py:656
  121.2 1.4 %collective-permute-start.17 = (f32[64,512]{1,0:T(8,128)S(1)}, f32[64,512]{1,0:T(8,128)S(1)}, u32[]{:S(2)}, u32[]{:S(2)}) collective-permute-start(f32[64,512]{1,0:T(8,128)S(1)} %shard_map.101.own_ref), channel_id=1, source_target_pairs={{0,1},{1,0},{2,3},{3,2},{4,5},{5,4},{6,7},{7,6},{8,9},{9,8},{10,11... | collective-permute-start | bytes 393224 | tf_op jit(solution)/shard_map/ppermute | solution.py:623
  124.7 15.3 %all-to-all-start.1 = ((f32[8,2,8,512]{3,2,1,0:T(8,128)}), f32[8,2,8,512]{3,2,1,0:T(8,128)S(1)}, u32[]{:S(2)}, u32[]{:S(2)}) async-start(f32[8,2,8,512]{3,2,1,0:T(8,128)} %get-tuple-element.64), calls=%async_computation.1 | async-start | bytes 524288 | tf_op jit(solution)/shard_map/all_to_all | solution.py:663

commit v4 on v3

--- a/solution.py
+++ b/solution.py
@@ -196,7 +196,7 @@
         plane(z, prior(z), later(z))
         return carry
 
-    lax.fori_loop(1, zb - 1, body, 0)
+    lax.fori_loop(1, zb - 1, body, 0, unroll=zb <= ZS)
     plane(zb - 1, prior(zb - 1), lambda f, r: after[0, f, 0, r : r + 8, :])
 
 

time: 142 us -> 141 us (level)
  no operation moved by 1% of the time
where the time goes in v4:
time: 141 us
  Pallas kernels  69 us (49%)
  starting transfers between devices  42.9 us (30%)
  waiting for transfers between devices  26.9 us (19%)
    pallas_call x1, Pallas kernels, bulk(): pl.pallas_call(bulk_kernel, grid_spec=pltpu.PrefetchScalarGridSpec(num_sc...  30.9 us
    ppermute x14, starting transfers between devices, exchange(): lax.ppermute(pieces[k], 'gx', [(i, i ^ k) for i in range(n)])  24.5 us
    all_to_all x1, waiting for transfers between devices, per_device(): lax.all_to_all(slab_step(idx, coefs, fields, slab_side, seeds, n), 'gx',...  9.97 us
    pallas_call x1, Pallas kernels, iterate(): pl.pallas_call(functools.partial(iterate_kernel, n), in_specs=[smem()] +...  9.88 us
    pallas_call x2, Pallas kernels, edges(): pl.pallas_call(edges_kernel, grid_spec=pltpu.PrefetchScalarGridSpec(num_s...  9.59 us
    ppermute x14, waiting for transfers between devices, exchange(): lax.ppermute(pieces[k], 'gx', [(i, i ^ k) for i in range(n)])  8.77 us
    all_to_all x1, starting transfers between devices, per_device(): lax.all_to_all(slab_step(idx, coefs, fields, slab_side, seeds, n), 'gx',...  7.2 us
    pallas_call x1, Pallas kernels, mend(): pl.pallas_call(mend_kernel, grid=(m, 2), in_specs=[smem(), block, halo, h...  6.24 us
  transfers between devices with their start and end apart: 22, of which 11 were waited for; matrix products, arithmetic and copies ran while one was open for 1% of the time, Pallas kernels for 40%

profile of v4, /device:TPU:0, one launch (start us, length us, event | category | flops | bytes accessed | tf_op | source)
XLA Modules:
  0.0 140.5 jit_solution(14137650090164868745)
XLA Ops:
  0.6 0.0 copy-start
  0.7 0.1 pad_add_fusion.idx_ref
  0.8 2.1 %shard_map.94 = f32[2,4,64,128]{3,2,1,0:T(8,128)S(1)} custom-call(s32[2]{0:T(128)S(1)} %pad_add_fusion.idx_ref, f32[2,4,48,64,256]{4,3,2,1,0:T(8,128)} %refs_2_.3), custom_call_target="tpu_custom_call" | custom-call | flops 524288 | bytes 1048576 | tf_op jit(solution)/shard_map/pallas_call | solution.py:82
  2.9 0.5 collective-permute-start
  3.4 0.2 fusion
  3.7 0.1 fusion.5
  3.8 0.0 copy-done.2
  3.8 0.1 tile.29
  3.9 0.1 tile.25
  4.0 0.1 tile.30.refs_5_
  4.1 0.1 stack.8.coef_ref
  4.2 0.4 collective-permute-done.refs_3_
  4.6 5.3 %shard_map.95 = f32[8,264,256]{2,1,0:T(8,128)} custom-call(s32[2]{0:T(128)S(1)} %pad_add_fusion.idx_ref, f32[2,4,5]{2,1,0:T(4,128)S(1)} %stack.8.coef_ref, f32[2,4,48,64,256]{4,3,2,1,0:T(8,128)} %refs_2_.3, f32[2,4,48,64,256]{4,3,2,1,0:T(8,128)} %refs_2_.3, f32[2,4,48,64,256]{4,3,2,1,0:T(8,128)} %refs_2_.3, ...), custom_call_target="tpu_custom_call" | custom-call | flops 15728640 | bytes 5242880 | tf_op jit(solution)/shard_map/pallas_call | solution.py:305
  9.9 7.2 %all-to-all-start = ((f32[8,264,256]{2,1,0:T(8,128)}), f32[8,264,256]{2,1,0:T(8,128)S(1)}, u32[]{:S(2)}, u32[]{:S(2)}) async-start(f32[8,264,256]{2,1,0:T(8,128)} %shard_map.95), calls=%async_computation | async-start | bytes 4325376 | tf_op jit(solution)/shard_map/all_to_all | solution.py:647
  17.1 7.5 %shard_map.96 = f32[2,4,64,128]{3,2,1,0:T(8,128)S(1)} custom-call(s32[2]{0:T(128)S(1)} %pad_add_fusion.idx_ref, f32[2,4,48,64,256]{4,3,2,1,0:T(8,128)} %refs_2_.3), custom_call_target="tpu_custom_call" | custom-call | flops 6291456 | bytes 12582912 | tf_op jit(solution)/shard_map/pallas_call | solution.py:82
  24.5 0.0 copy-start.1
  24.5 0.1 collective-permute-start.1
  24.6 1.5 %collective-permute-done.1.refs_3_ = f32[2,4,64,128]{3,2,1,0:T(8,128)S(1)} collective-permute-done((f32[2,4,64,128]{3,2,1,0:T(8,128)S(1)}, f32[2,4,64,128]{3,2,1,0:T(8,128)S(1)}, u32[]{:S(2)}, u32[]{:S(2)}) %collective-permute-start.1) | collective-permute-done | bytes 262176 | tf_op jit(solution)/shard_map/ppermute | solution.py:623
  26.1 30.9 %shard_map.97 = (f32[2,4,48,64,256]{4,3,2,1,0:T(8,128)}, f32[2,4,48,256]{3,2,1,0:T(8,128)S(1)}, f32[2,4,48,256]{3,2,1,0:T(8,128)S(1)}) custom-call(s32[2]{0:T(128)S(1)} %pad_add_fusion.idx_ref, f32[2,4,5]{2,1,0:T(4,128)S(1)} %stack.8.coef_ref, f32[2,4,48,64,256]{4,3,2,1,0:T(8,128)} %refs_2_.3, f32[2,4,48,64,256]{4,3,2,1,0:T(8,128)} %refs_2_.3, ...), custom_call_target="tpu_custom_call" | custom-call | flops 188743680 | bytes 62914560 | tf_op jit(solution)/shard_map/pallas_call | solution.py:240
  57.0 10.0 %all-to-all-done.refs_0_ = f32[8,264,256]{2,1,0:T(8,128)S(1)} async-done(((f32[8,264,256]{2,1,0:T(8,128)}), f32[8,264,256]{2,1,0:T(8,128)S(1)}, u32[]{:S(2)}, u32[]{:S(2)}) %all-to-all-start) | async-done | bytes 2162720 | tf_op jit(solution)/shard_map/all_to_all | solution.py:647
  67.0 3.6 %shard_map.98 = (f32[8,8,2176]{2,1,0:T(8,128)S(1)}, f32[8,8,2176]{2,1,0:T(8,128)S(1)}, f32[2,512,512]{2,1,0:T(8,128)S(1)}) custom-call(s32[2]{0:T(128)S(1)} %pad_add_fusion.idx_ref, f32[2,4,5]{2,1,0:T(4,128)S(1)} %stack.8.coef_ref, f32[8,264,256]{2,1,0:T(8,128)S(1)} %all-to-all-done.refs_0_), custom_call_target="tpu_custom_call" | custom-call | tf_op jit(solution)/shard_map/pallas_call | solution.py:420
  70.6 0.1 collective-permute-start.2
  70.7 1.9 %collective-permute-done.2.got_ref = f32[8,8,2176]{2,1,0:T(8,128)S(1)} collective-permute-done((f32[8,8,2176]{2,1,0:T(8,128)S(1)}, f32[8,8,2176]{2,1,0:T(8,128)S(1)}, u32[]{:S(2)}, u32[]{:S(2)}) %collective-permute-start.2) | collective-permute-done | bytes 557088 | tf_op jit(solution)/shard_map/ppermute | solution.py:623
  72.6 0.6 shard_map.99
  73.2 1.5 %collective-permute-start.3 = (f32[8,2176]{1,0:T(8,128)S(1)}, f32[8,2176]{1,0:T(8,128)S(1)}, u32[]{:S(2)}, u32[]{:S(2)}) collective-permute-start(f32[8,2176]{1,0:T(8,128)S(1)} %get-tuple-element.40), channel_id=1, source_target_pairs={{0,2},{2,0},{4,6},{6,4},{8,10},{10,8},{12,14},{14,12},{1,3},{3,1},... | collective-permute-start | bytes 208904 | tf_op jit(solution)/shard_map/ppermute | solution.py:618
  74.7 0.0 collective-permute-start.4
  74.7 2.0 %collective-permute-start.5 = (f32[8,2176]{1,0:T(8,128)S(1)}, f32[8,2176]{1,0:T(8,128)S(1)}, u32[]{:S(2)}, u32[]{:S(2)}) collective-permute-start(f32[8,2176]{1,0:T(8,128)S(1)} %get-tuple-element.42), channel_id=1, source_target_pairs={{0,6},{2,4},{4,2},{6,0},{8,14},{10,12},{12,10},{14,8},{1,7},{3,5},... | collective-permute-start | bytes 208904 | tf_op jit(solution)/shard_map/ppermute | solution.py:618
  76.8 0.8 collective-permute-start.6
  77.6 3.0 %collective-permute-start.7 = (f32[8,2176]{1,0:T(8,128)S(1)}, f32[8,2176]{1,0:T(8,128)S(1)}, u32[]{:S(2)}, u32[]{:S(2)}) collective-permute-start(f32[8,2176]{1,0:T(8,128)S(1)} %get-tuple-element.44), channel_id=1, source_target_pairs={{0,10},{2,8},{4,14},{6,12},{8,2},{10,0},{12,6},{14,4},{1,11},{3,9}... | collective-permute-start | bytes 208904 | tf_op jit(solution)/shard_map/ppermute | solution.py:618
  80.6 0.0 collective-permute-done.3.refs_1_
  80.6 1.5 %collective-permute-start.8 = (f32[8,2176]{1,0:T(8,128)S(1)}, f32[8,2176]{1,0:T(8,128)S(1)}, u32[]{:S(2)}, u32[]{:S(2)}) collective-permute-start(f32[8,2176]{1,0:T(8,128)S(1)} %get-tuple-element.45), channel_id=1, source_target_pairs={{0,12},{2,14},{4,8},{6,10},{8,4},{10,6},{12,0},{14,2},{1,13},{3,15... | collective-permute-start | bytes 208904 | tf_op jit(solution)/shard_map/ppermute | solution.py:618
  82.1 0.0 collective-permute-done.4.refs_2_
  82.1 2.4 %collective-permute-start.9 = (f32[8,2176]{1,0:T(8,128)S(1)}, f32[8,2176]{1,0:T(8,128)S(1)}, u32[]{:S(2)}, u32[]{:S(2)}) collective-permute-start(f32[8,2176]{1,0:T(8,128)S(1)} %get-tuple-element.46), channel_id=1, source_target_pairs={{0,14},{2,12},{4,10},{6,8},{8,6},{10,4},{12,2},{14,0},{1,15},{3,13... | collective-permute-start | bytes 208904 | tf_op jit(solution)/shard_map/ppermute | solution.py:618
  84.4 0.0 collective-permute-done.5.refs_3_
  84.4 1.4 collective-permute-done.6.refs_4_
  85.8 4.1 %collective-permute-done.7.refs_5_ = f32[8,2176]{1,0:T(8,128)S(1)} collective-permute-done((f32[8,2176]{1,0:T(8,128)S(1)}, f32[8,2176]{1,0:T(8,128)S(1)}, u32[]{:S(2)}, u32[]{:S(2)}) %collective-permute-start.7) | collective-permute-done | bytes 69664 | tf_op jit(solution)/shard_map/ppermute | solution.py:618
  89.9 0.0 collective-permute-done.8.refs_6_
  89.9 0.0 collective-permute-done.9.refs_7_
  90.0 2.5 %collective-permute-start.16 = (f32[8,2176]{1,0:T(8,128)S(1)}, f32[8,2176]{1,0:T(8,128)S(1)}, u32[]{:S(2)}, u32[]{:S(2)}) collective-permute-start(f32[8,2176]{1,0:T(8,128)S(1)} %shard_map.100.refs_0_), channel_id=1, source_target_pairs={{0,14},{2,12},{4,10},{6,8},{8,6},{10,4},{12,2},{14,0},{1,15},{3,13... | collective-permute-start | bytes 208904 | tf_op jit(solution)/shard_map/ppermute | solution.py:618
  92.5 1.9 %collective-permute-start.15 = (f32[8,2176]{1,0:T(8,128)S(1)}, f32[8,2176]{1,0:T(8,128)S(1)}, u32[]{:S(2)}, u32[]{:S(2)}) collective-permute-start(f32[8,2176]{1,0:T(8,128)S(1)} %shard_map.100.refs_0_), channel_id=1, source_target_pairs={{0,12},{2,14},{4,8},{6,10},{8,4},{10,6},{12,0},{14,2},{1,13},{3,15... | collective-permute-start | bytes 208904 | tf_op jit(solution)/shard_map/ppermute | solution.py:618
  94.3 1.6 %collective-permute-start.14 = (f32[8,2176]{1,0:T(8,128)S(1)}, f32[8,2176]{1,0:T(8,128)S(1)}, u32[]{:S(2)}, u32[]{:S(2)}) collective-permute-start(f32[8,2176]{1,0:T(8,128)S(1)} %shard_map.100.refs_0_), channel_id=1, source_target_pairs={{0,10},{2,8},{4,14},{6,12},{8,2},{10,0},{12,6},{14,4},{1,11},{3,9}... | collective-permute-start | bytes 208904 | tf_op jit(solution)/shard_map/ppermute | solution.py:618
  96.0 1.7 %collective-permute-start.13 = (f32[8,2176]{1,0:T(8,128)S(1)}, f32[8,2176]{1,0:T(8,128)S(1)}, u32[]{:S(2)}, u32[]{:S(2)}) collective-permute-start(f32[8,2176]{1,0:T(8,128)S(1)} %shard_map.100.refs_0_), channel_id=1, source_target_pairs={{0,8},{2,10},{4,12},{6,14},{8,0},{10,2},{12,4},{14,6},{1,9},{3,11}... | collective-permute-start | bytes 208904 | tf_op jit(solution)/shard_map/ppermute | solution.py:618
  97.7 1.2 collective-permute-start.12
  98.9 0.0 collective-permute-done.16.refs_7_
  98.9 3.3 %collective-permute-start.11 = (f32[8,2176]{1,0:T(8,128)S(1)}, f32[8,2176]{1,0:T(8,128)S(1)}, u32[]{:S(2)}, u32[]{:S(2)}) collective-permute-start(f32[8,2176]{1,0:T(8,128)S(1)} %shard_map.100.refs_0_), channel_id=1, source_target_pairs={{0,4},{2,6},{4,0},{6,2},{8,12},{10,14},{12,8},{14,10},{1,5},{3,7},... | collective-permute-start | bytes 208904 | tf_op jit(solution)/shard_map/ppermute | solution.py:618
  102.3 0.0 collective-permute-done.15.refs_6_
  102.3 1.1 collective-permute-start.10
  103.3 1.8 %collective-permute-done.14.refs_5_ = f32[8,2176]{1,0:T(8,128)S(1)} collective-permute-done((f32[8,2176]{1,0:T(8,128)S(1)}, f32[8,2176]{1,0:T(8,128)S(1)}, u32[]{:S(2)}, u32[]{:S(2)}) %collective-permute-start.14) | collective-permute-done | bytes 69664 | tf_op jit(solution)/shard_map/ppermute | solution.py:618
  105.2 0.0 collective-permute-done.13.refs_4_
  105.2 0.0 collective-permute-done.12.refs_3_
  105.2 0.7 collective-permute-done.11.refs_2_
  105.9 0.7 collective-permute-done.10.refs_1_
  106.6 3.0 %collective-permute-start.18 = (f32[2,4,48,256]{3,2,1,0:T(8,128)S(1)}, f32[2,4,48,256]{3,2,1,0:T(8,128)S(1)}, u32[]{:S(2)}, u32[]{:S(2)}) collective-permute-start(f32[2,4,48,256]{3,2,1,0:T(8,128)S(1)} %get-tuple-element.59), channel_id=1, source_target_pairs={{0,2},{2,4},{4,6},{6,8},{8,10},{10,12},{12,14},{1,3},{3,5},{5,7},{... | collective-permute-start | bytes 1179656 | tf_op jit(solution)/shard_map/ppermute | solution.py:656
  109.6 1.5 %collective-permute-start.19 = (f32[2,4,48,256]{3,2,1,0:T(8,128)S(1)}, f32[2,4,48,256]{3,2,1,0:T(8,128)S(1)}, u32[]{:S(2)}, u32[]{:S(2)}) collective-permute-start(f32[2,4,48,256]{3,2,1,0:T(8,128)S(1)} %get-tuple-element.60), channel_id=1, source_target_pairs={{2,0},{4,2},{6,4},{8,6},{10,8},{12,10},{14,12},{3,1},{5,3},{7,5},{... | collective-permute-start | bytes 1179656 | tf_op jit(solution)/shard_map/ppermute | solution.py:656
  111.0 9.9 %shard_map.101.own_ref = f32[64,512]{1,0:T(8,128)S(1)} custom-call(s32[2]{0:T(128)S(1)} %pad_add_fusion.idx_ref, f32[2,64,512]{2,1,0:T(8,128)S(1)} %bitcast.12, f32[8,2176]{1,0:T(8,128)S(1)} %shard_map.100.refs_0_, f32[8,2176]{1,0:T(8,128)S(1)} %collective-permute-done.10.refs_1_, f32[8,2176]{1,0:T(8,128)S(1)} %collective-permute-done.11.refs_2_, ...), custom_call_target="tpu_custom_call" | custom-call | tf_op jit(solution)/shard_map/pallas_call | solution.py:549
  120.9 0.1 collective-permute-start.17
  121.0 1.3 collective-permute-done.17.got_ref
  122.4 2.0 %shard_map.102 = (f32[2,64,512]{2,1,0:T(8,128)}, f32[8,2,8,512]{3,2,1,0:T(8,128)}) custom-call(s32[2]{0:T(128)S(1)} %pad_add_fusion.idx_ref, f32[64,512]{1,0:T(8,128)S(1)} %shard_map.101.own_ref, f32[64,512]{1,0:T(8,128)S(1)} %collective-permute-done.17.got_ref, f32[2,512,512]{2,1,0:T(8,128)S(1)} %get-tuple-element.57.fibre), custom_call_target="tpu_custom_call" | custom-call | tf_op jit(solution)/shard_map/pallas_call | solution.py:573
  124.4 0.0 collective-permute-done.18.before_ref
  124.4 0.0 collective-permute-done.19.after_ref
  124.4 6.0 %all-to-all-start.1 = ((f32[8,2,8,512]{3,2,1,0:T(8,128)}), f32[8,2,8,512]{3,2,1,0:T(8,128)S(1)}, u32[]{:S(2)}, u32[]{:S(2)}) async-start(f32[8,2,8,512]{3,2,1,0:T(8,128)} %get-tuple-element.64), calls=%async_computation.1 | async-start | bytes 524288 | tf_op jit(solution)/shard_map/all_to_all | solution.py:663
  130.4 6.2 %shard_map.103 = f32[2,4,48,64,256]{4,3,2,1,0:T(8,128)} custom-call(f32[2,4,5]{2,1,0:T(4,128)S(1)} %stack.8.coef_ref, f32[2,4,48,64,256]{4,3,2,1,0:T(8,128)} %get-tuple-element.35.value_ref, f32[2,4,48,256]{3,2,1,0:T(8,128)S(1)} %collective-permute-done.18.before_ref, ...), custom_call_target="tpu_custom_call", output_to_operand_aliasing={{}: (1, {})} | custom-call | flops 393216 | bytes 12582912 | tf_op jit(solution)/shard_map/pallas_call | solution.py:348
  136.7 3.0 %all-to-all-done.1.held = f32[8,2,8,512]{3,2,1,0:T(8,128)S(1)} async-done(((f32[8,2,8,512]{3,2,1,0:T(8,128)}), f32[8,2,8,512]{3,2,1,0:T(8,128)S(1)}, u32[]{:S(2)}, u32[]{:S(2)}) %all-to-all-start.1) | async-done | bytes 262176 | tf_op jit(solution)/shard_map/all_to_all | solution.py:663
  139.7 0.8 shard_map.104
  (18 shorter events, 0.1 us)
Async XLA Ops:
  0.6 2.8 %copy-start = (f32[8,4,4]{0,2,1:T(4,128)S(1)}, f32[8,4,4]{0,2,1:T(4,128)}, u32[]{:S(2)}) copy-start(f32[8,4,4]{0,2,1:T(4,128)} %param.9) | copy-start | bytes 1540
  0.6 2.8 %copy-start.5 = (s32[2]{0:T(128)S(1)}, s32[2]{0:T(128)}, u32[]{:S(2)}) copy-start(s32[2]{0:T(128)} %param.8) | copy-start | bytes 28
  0.7 3.1 %copy-start.2 = (s32[2,16]{1,0:T(2,128)S(1)}, s32[2,16]{1,0:T(2,128)}, u32[]{:S(2)}) copy-start(s32[2,16]{1,0:T(2,128)} %param.10) | copy-start | bytes 388
  0.7 3.1 %copy-start.3 = (s32[2,16]{1,0:T(2,128)S(1)}, s32[2,16]{1,0:T(2,128)}, u32[]{:S(2)}) copy-start(s32[2,16]{1,0:T(2,128)} %param.11) | copy-start | bytes 388
  0.7 3.1 %copy-start.4 = (s32[2,16]{1,0:T(2,128)S(1)}, s32[2,16]{1,0:T(2,128)}, u32[]{:S(2)}) copy-start(s32[2,16]{1,0:T(2,128)} %param.12) | copy-start | bytes 388
  2.9 1.7 %collective-permute-start = (f32[2,4,64,128]{3,2,1,0:T(8,128)S(1)}, f32[2,4,64,128]{3,2,1,0:T(8,128)S(1)}, u32[]{:S(2)}, u32[]{:S(2)}) collective-permute-start(f32[2,4,64,128]{3,2,1,0:T(8,128)S(1)} %shard_map.94), channel_id=1, source_target_pairs={{0,1},{1,0},{2,3},{3,2},{4,5},{5,4},{6,7},{7,6},{8,9},{9,8},{10,11... | collective-permute-start | bytes 786440 | tf_op jit(solution)/shard_map/ppermute | solution.py:623
  9.9 57.1 %all-to-all-start = ((f32[8,264,256]{2,1,0:T(8,128)}), f32[8,264,256]{2,1,0:T(8,128)S(1)}, u32[]{:S(2)}, u32[]{:S(2)}) async-start(f32[8,264,256]{2,1,0:T(8,128)} %shard_map.95), calls=%async_computation | async-start | bytes 4325376 | tf_op jit(solution)/shard_map/all_to_all | solution.py:647
  24.5 86.5 %copy-start.1 = (f32[2,512,64]{1,2,0:T(8,128)S(1)}, f32[2,512,64]{1,2,0:T(8,128)}, u32[]{:S(2)}) copy-start(f32[2,512,64]{1,2,0:T(8,128)} %param.13) | copy-start | bytes 786436
  24.5 1.6 %collective-permute-start.1 = (f32[2,4,64,128]{3,2,1,0:T(8,128)S(1)}, f32[2,4,64,128]{3,2,1,0:T(8,128)S(1)}, u32[]{:S(2)}, u32[]{:S(2)}) collective-permute-start(f32[2,4,64,128]{3,2,1,0:T(8,128)S(1)} %shard_map.96), channel_id=1, source_target_pairs={{0,1},{1,0},{2,3},{3,2},{4,5},{5,4},{6,7},{7,6},{8,9},{9,8},{10,11... | collective-permute-start | bytes 786440 | tf_op jit(solution)/shard_map/ppermute | solution.py:623
  70.6 2.0 %collective-permute-start.2 = (f32[8,8,2176]{2,1,0:T(8,128)S(1)}, f32[8,8,2176]{2,1,0:T(8,128)S(1)}, u32[]{:S(2)}, u32[]{:S(2)}) collective-permute-start(f32[8,8,2176]{2,1,0:T(8,128)S(1)} %get-tuple-element.38), channel_id=1, source_target_pairs={{0,1},{1,0},{2,3},{3,2},{4,5},{5,4},{6,7},{7,6},{8,9},{9,8},{10,11... | collective-permute-start | bytes 1671176 | tf_op jit(solution)/shard_map/ppermute | solution.py:623
  73.2 7.4 %collective-permute-start.3 = (f32[8,2176]{1,0:T(8,128)S(1)}, f32[8,2176]{1,0:T(8,128)S(1)}, u32[]{:S(2)}, u32[]{:S(2)}) collective-permute-start(f32[8,2176]{1,0:T(8,128)S(1)} %get-tuple-element.40), channel_id=1, source_target_pairs={{0,2},{2,0},{4,6},{6,4},{8,10},{10,8},{12,14},{14,12},{1,3},{3,1},... | collective-permute-start | bytes 208904 | tf_op jit(solution)/shard_map/ppermute | solution.py:618
  74.7 7.3 %collective-permute-start.4 = (f32[8,2176]{1,0:T(8,128)S(1)}, f32[8,2176]{1,0:T(8,128)S(1)}, u32[]{:S(2)}, u32[]{:S(2)}) collective-permute-start(f32[8,2176]{1,0:T(8,128)S(1)} %get-tuple-element.41), channel_id=1, source_target_pairs={{0,4},{2,6},{4,0},{6,2},{8,12},{10,14},{12,8},{14,10},{1,5},{3,7},... | collective-permute-start | bytes 208904 | tf_op jit(solution)/shard_map/ppermute | solution.py:618
  74.7 9.7 %collective-permute-start.5 = (f32[8,2176]{1,0:T(8,128)S(1)}, f32[8,2176]{1,0:T(8,128)S(1)}, u32[]{:S(2)}, u32[]{:S(2)}) collective-permute-start(f32[8,2176]{1,0:T(8,128)S(1)} %get-tuple-element.42), channel_id=1, source_target_pairs={{0,6},{2,4},{4,2},{6,0},{8,14},{10,12},{12,10},{14,8},{1,7},{3,5},... | collective-permute-start | bytes 208904 | tf_op jit(solution)/shard_map/ppermute | solution.py:618
  76.8 9.0 %collective-permute-start.6 = (f32[8,2176]{1,0:T(8,128)S(1)}, f32[8,2176]{1,0:T(8,128)S(1)}, u32[]{:S(2)}, u32[]{:S(2)}) collective-permute-start(f32[8,2176]{1,0:T(8,128)S(1)} %get-tuple-element.43), channel_id=1, source_target_pairs={{0,8},{2,10},{4,12},{6,14},{8,0},{10,2},{12,4},{14,6},{1,9},{3,11}... | collective-permute-start | bytes 208904 | tf_op jit(solution)/shard_map/ppermute | solution.py:618
  77.6 12.3 %collective-permute-start.7 = (f32[8,2176]{1,0:T(8,128)S(1)}, f32[8,2176]{1,0:T(8,128)S(1)}, u32[]{:S(2)}, u32[]{:S(2)}) collective-permute-start(f32[8,2176]{1,0:T(8,128)S(1)} %get-tuple-element.44), channel_id=1, source_target_pairs={{0,10},{2,8},{4,14},{6,12},{8,2},{10,0},{12,6},{14,4},{1,11},{3,9}... | collective-permute-start | bytes 208904 | tf_op jit(solution)/shard_map/ppermute | solution.py:618
  80.6 9.3 %collective-permute-start.8 = (f32[8,2176]{1,0:T(8,128)S(1)}, f32[8,2176]{1,0:T(8,128)S(1)}, u32[]{:S(2)}, u32[]{:S(2)}) collective-permute-start(f32[8,2176]{1,0:T(8,128)S(1)} %get-tuple-element.45), channel_id=1, source_target_pairs={{0,12},{2,14},{4,8},{6,10},{8,4},{10,6},{12,0},{14,2},{1,13},{3,15... | collective-permute-start | bytes 208904 | tf_op jit(solution)/shard_map/ppermute | solution.py:618
  82.1 7.9 %collective-permute-start.9 = (f32[8,2176]{1,0:T(8,128)S(1)}, f32[8,2176]{1,0:T(8,128)S(1)}, u32[]{:S(2)}, u32[]{:S(2)}) collective-permute-start(f32[8,2176]{1,0:T(8,128)S(1)} %get-tuple-element.46), channel_id=1, source_target_pairs={{0,14},{2,12},{4,10},{6,8},{8,6},{10,4},{12,2},{14,0},{1,15},{3,13... | collective-permute-start | bytes 208904 | tf_op jit(solution)/shard_map/ppermute | solution.py:618
  90.0 8.9 %collective-permute-start.16 = (f32[8,2176]{1,0:T(8,128)S(1)}, f32[8,2176]{1,0:T(8,128)S(1)}, u32[]{:S(2)}, u32[]{:S(2)}) collective-permute-start(f32[8,2176]{1,0:T(8,128)S(1)} %shard_map.100.refs_0_), channel_id=1, source_target_pairs={{0,14},{2,12},{4,10},{6,8},{8,6},{10,4},{12,2},{14,0},{1,15},{3,13... | collective-permute-start | bytes 208904 | tf_op jit(solution)/shard_map/ppermute | solution.py:618
  92.5 9.8 %collective-permute-start.15 = (f32[8,2176]{1,0:T(8,128)S(1)}, f32[8,2176]{1,0:T(8,128)S(1)}, u32[]{:S(2)}, u32[]{:S(2)}) collective-permute-start(f32[8,2176]{1,0:T(8,128)S(1)} %shard_map.100.refs_0_), channel_id=1, source_target_pairs={{0,12},{2,14},{4,8},{6,10},{8,4},{10,6},{12,0},{14,2},{1,13},{3,15... | collective-permute-start | bytes 208904 | tf_op jit(solution)/shard_map/ppermute | solution.py:618
  94.3 10.8 %collective-permute-start.14 = (f32[8,2176]{1,0:T(8,128)S(1)}, f32[8,2176]{1,0:T(8,128)S(1)}, u32[]{:S(2)}, u32[]{:S(2)}) collective-permute-start(f32[8,2176]{1,0:T(8,128)S(1)} %shard_map.100.refs_0_), channel_id=1, source_target_pairs={{0,10},{2,8},{4,14},{6,12},{8,2},{10,0},{12,6},{14,4},{1,11},{3,9}... | collective-permute-start | bytes 208904 | tf_op jit(solution)/shard_map/ppermute | solution.py:618
  96.0 9.2 %collective-permute-start.13 = (f32[8,2176]{1,0:T(8,128)S(1)}, f32[8,2176]{1,0:T(8,128)S(1)}, u32[]{:S(2)}, u32[]{:S(2)}) collective-permute-start(f32[8,2176]{1,0:T(8,128)S(1)} %shard_map.100.refs_0_), channel_id=1, source_target_pairs={{0,8},{2,10},{4,12},{6,14},{8,0},{10,2},{12,4},{14,6},{1,9},{3,11}... | collective-permute-start | bytes 208904 | tf_op jit(solution)/shard_map/ppermute | solution.py:618
  97.7 7.5 %collective-permute-start.12 = (f32[8,2176]{1,0:T(8,128)S(1)}, f32[8,2176]{1,0:T(8,128)S(1)}, u32[]{:S(2)}, u32[]{:S(2)}) collective-permute-start(f32[8,2176]{1,0:T(8,128)S(1)} %shard_map.100.refs_0_), channel_id=1, source_target_pairs={{0,6},{2,4},{4,2},{6,0},{8,14},{10,12},{12,10},{14,8},{1,7},{3,5},... | collective-permute-start | bytes 208904 | tf_op jit(solution)/shard_map/ppermute | solution.py:618
  98.9 6.9 %collective-permute-start.11 = (f32[8,2176]{1,0:T(8,128)S(1)}, f32[8,2176]{1,0:T(8,128)S(1)}, u32[]{:S(2)}, u32[]{:S(2)}) collective-permute-start(f32[8,2176]{1,0:T(8,128)S(1)} %shard_map.100.refs_0_), channel_id=1, source_target_pairs={{0,4},{2,6},{4,0},{6,2},{8,12},{10,14},{12,8},{14,10},{1,5},{3,7},... | collective-permute-start | bytes 208904 | tf_op jit(solution)/shard_map/ppermute | solution.py:618
  102.3 4.3 %collective-permute-start.10 = (f32[8,2176]{1,0:T(8,128)S(1)}, f32[8,2176]{1,0:T(8,128)S(1)}, u32[]{:S(2)}, u32[]{:S(2)}) collective-permute-start(f32[8,2176]{1,0:T(8,128)S(1)} %shard_map.100.refs_0_), channel_id=1, source_target_pairs={{0,2},{2,0},{4,6},{6,4},{8,10},{10,8},{12,14},{14,12},{1,3},{3,1},... | collective-permute-start | bytes 208904 | tf_op jit(solution)/shard_map/ppermute | solution.py:618
  106.6 17.8 %collective-permute-start.18 = (f32[2,4,48,256]{3,2,1,0:T(8,128)S(1)}, f32[2,4,48,256]{3,2,1,0:T(8,128)S(1)}, u32[]{:S(2)}, u32[]{:S(2)}) collective-permute-start(f32[2,4,48,256]{3,2,1,0:T(8,128)S(1)} %get-tuple-element.59), channel_id=1, source_target_pairs={{0,2},{2,4},{4,6},{6,8},{8,10},{10,12},{12,14},{1,3},{3,5},{5,7},{... | collective-permute-start | bytes 1179656 | tf_op jit(solution)/shard_map/ppermute | solution.py:656
  109.6 14.8 %collective-permute-start.19 = (f32[2,4,48,256]{3,2,1,0:T(8,128)S(1)}, f32[2,4,48,256]{3,2,1,0:T(8,128)S(1)}, u32[]{:S(2)}, u32[]{:S(2)}) collective-permute-start(f32[2,4,48,256]{3,2,1,0:T(8,128)S(1)} %get-tuple-element.60), channel_id=1, source_target_pairs={{2,0},{4,2},{6,4},{8,6},{10,8},{12,10},{14,12},{3,1},{5,3},{7,5},{... | collective-permute-start | bytes 1179656 | tf_op jit(solution)/shard_map/ppermute | solution.py:656
  120.9 1.4 %collective-permute-start.17 = (f32[64,512]{1,0:T(8,128)S(1)}, f32[64,512]{1,0:T(8,128)S(1)}, u32[]{:S(2)}, u32[]{:S(2)}) collective-permute-start(f32[64,512]{1,0:T(8,128)S(1)} %shard_map.101.own_ref), channel_id=1, source_target_pairs={{0,1},{1,0},{2,3},{3,2},{4,5},{5,4},{6,7},{7,6},{8,9},{9,8},{10,11... | collective-permute-start | bytes 393224 | tf_op jit(solution)/shard_map/ppermute | solution.py:623
  124.4 15.3 %all-to-all-start.1 = ((f32[8,2,8,512]{3,2,1,0:T(8,128)}), f32[8,2,8,512]{3,2,1,0:T(8,128)S(1)}, u32[]{:S(2)}, u32[]{:S(2)}) async-start(f32[8,2,8,512]{3,2,1,0:T(8,128)} %get-tuple-element.64), calls=%async_computation.1 | async-start | bytes 524288 | tf_op jit(solution)/shard_map/all_to_all | solution.py:663
